TPU v7x, 128 devices: a whole 4x4x4 slice. The times are simulated.
128 devices in a mesh: circ: 32 (over z, x, y_hi), rad: 2 (over y_lo), half: 2 (over core).
Axes of the slice: x: 4, y: 4 (y_hi: 2, y_lo: 2; y = y_hi * 2 + y_lo), z: 4, core: 2. Of those that a mesh axis runs over, the one named last changes fastest.
Arguments:
- state: float32 [5, 96, 512, 256], P(None, 'half', 'circ', 'rad'), may hold values from -6 to 6
- offsets: int32 [3], replicated, may hold values from 1 to 511, as said below
- pml_zone: int32 [96], P('half'), may hold values from 0 to 1, as said below
Outputs:
- advanced: float32 [5, 96, 512, 256], P(None, 'half', 'circ', 'rad')
- increment: float32 [5, 96, 512, 256], P(None, 'half', 'circ', 'rad')
Inputs may be any that keep to these rules, and one draw needn't show every extreme that they name: `pml_zone`: 1 on an inlet zone of the first planes and an outlet zone of the last planes, each 4 to 13 planes thick, 0 elsewhere. No offset is a multiple of 16; in some order the three sections' offsets lie in [496, 512), in [0, 16) and in [256, 272).
All inputs are finite; a program needn't handle non-finite values.
Results may differ from a plain program's by a relative error of at most 0.00002.
Values sent between devices are 32-bit elements; how exact they have to be, the bound alone decides.
No kernel may reach another device: no remote copies, remote signals or barrier semaphores. Data moves between devices by JAX's collectives and lax.ppermute only.
A program may use at most 128 MiB of HBM per device.

v0:
```python
import functools

import jax
import jax.numpy as jnp
import numpy as np
from jax import lax
from jax.experimental import pallas as pl
from jax.experimental.pallas import tpu as pltpu
from jax.sharding import PartitionSpec as P

SECTIONS = 3
F, A, C, L = 5, 48, 16, 128
ROWS = F * A * C
FIELD = A * C
W = 5
GROUP = 6 * C
PARAMS = pltpu.CompilerParams(vmem_limit_bytes=24 << 20)

coeffs = (0.872756993962, -0.286511173973, 0.09032000128, -0.020779405824, 0.002484594688)
mach = 0.3
step_size = 0.25
damping = 0.8
section_a = (0.0, -5.0 / 9.0, -153.0 / 128.0)
section_b = (1.0 / 3.0, 15.0 / 16.0, 8.0 / 15.0)
HI = lax.Precision.HIGHEST


def band_matrix():
    band = np.zeros((L, L), np.float32)
    for k, c in enumerate(coeffs, start=1):
        band += c * (np.eye(L, k=-k) - np.eye(L, k=k)).astype(np.float32)
    return band


def rows_of(f, a):
    return pl.ds(pl.multiple_of(f * FIELD + a * C, C), C)


def total_of(terms):
    total = terms[0]
    for term in terms[1:]:
        total = total + term
    return total


def pack(q_ref, east_ref, odd_ref, rad_ref, face_ref):
    even = lax.rem(lax.axis_index("circ"), 2) == 0
    low_rad = lax.axis_index("rad") == 0
    rotor = lax.axis_index("half") == 0
    for g, f in enumerate((2, 4)):
        head = [q_ref[pl.ds(f * FIELD + c, A, stride=C), :] for c in range(W)]
        tail = [q_ref[pl.ds(f * FIELD + C - W + c, A, stride=C), :] for c in range(W)]
        for i in range(W):
            onward = total_of([-coeffs[i + W - c - 1] * tail[c] for c in range(i, W)])
            back = total_of([coeffs[c + W - i - 1] * head[c] for c in range(i + 1)])
            row = (g * W + i) * A
            east_ref[row : row + A, :] = jnp.where(even, onward, back)
            odd_ref[row : row + A, :] = jnp.where(even, back, onward)

    lane = lax.broadcasted_iota(jnp.int32, (GROUP, L), 1)
    first = jnp.where(low_rad, W, 0)
    rims = jnp.zeros((GROUP, L), jnp.float32)
    for n in range(2 * FIELD // GROUP):
        x = q_ref[3 * FIELD + n * GROUP : 3 * FIELD + (n + 1) * GROUP, :]
        rims = jnp.where((lane >= 8 * n) & (lane < 8 * n + W), pltpu.roll(x, first + 8 * n, 1), rims)
    slot = lax.rem(lane, 8)
    onward, back = [], []
    for d in range(W):
        c = coeffs[W - 1 - d]
        onward.append(jnp.where(slot + d < W, -c, 0.0) * (pltpu.roll(rims, L - d, 1) if d else rims))
        back.append(jnp.where((slot >= d) & (slot < W), c, 0.0) * (pltpu.roll(rims, d, 1) if d else rims))
    rad_ref[...] = jnp.where(low_rad, total_of(onward), total_of(back))

    for f in range(F):
        for m in range(W):
            a = jnp.where(rotor, A - 1 - m, m)
            row = (f * W + m) * C
            face_ref[row : row + C, :] = q_ref[rows_of(f, a), :]


MESSAGES = [
    jax.ShapeDtypeStruct((2 * W * A, L), jnp.float32),
    jax.ShapeDtypeStruct((2 * W * A, L), jnp.float32),
    jax.ShapeDtypeStruct((GROUP, L), jnp.float32),
    jax.ShapeDtypeStruct((F * W * C, L), jnp.float32),
]
FIELDS = jax.ShapeDtypeStruct((ROWS, L), jnp.float32)
VM = pl.BlockSpec(memory_space=pltpu.VMEM)
SM = pl.BlockSpec(memory_space=pltpu.SMEM)


def local_kernel(section, pml_ref, band_ref, q_ref, *refs):
    inc_ref = refs[0] if section else None
    out_ref, pad = refs[-2:]
    zero = jnp.zeros((W * C, L), jnp.float32)
    span = (A + 2 * W) * C
    for f in range(F):
        pad[f * span : f * span + W * C, :] = zero
        pad[f * span + W * C : f * span + W * C + FIELD, :] = q_ref[f * FIELD : (f + 1) * FIELD, :]
        pad[(f + 1) * span - W * C : (f + 1) * span, :] = zero
    cell = lax.broadcasted_iota(jnp.int32, (C, L), 0)
    up = [jnp.where(cell < C - k, c, 0.0) for k, c in enumerate(coeffs, start=1)]
    down = [jnp.where(cell >= k, c, 0.0) for k, c in enumerate(coeffs, start=1)]

    def circ(x):
        total = None
        for k in range(1, W + 1):
            term = up[k - 1] * pltpu.roll(x, C - k, 0) - down[k - 1] * pltpu.roll(x, k, 0)
            total = term if total is None else total + term
        return total

    B = 4

    def step(n, carry):
        a0 = n * B
        axial = []
        here = []
        for f in range(F):
            planes = [
                pad[pl.ds(pl.multiple_of(f * span + (a0 + d) * C, C), C), :] for d in range(B + 2 * W)
            ]
            here.append(planes[W : W + B])
            axial.append(
                [
                    sum(c * (planes[W + p + k] - planes[W + p - k]) for k, c in enumerate(coeffs, start=1))
                    for p in range(B)
                ]
            )
        radial = jnp.dot(
            jnp.concatenate(here[3] + here[4], axis=0),
            band_ref[...],
            precision=HI,
            preferred_element_type=jnp.float32,
        )
        for p in range(B):
            rad3 = radial[p * C : (p + 1) * C]
            rad4 = radial[(B + p) * C : (B + p + 1) * C]
            div = axial[1][p] + circ(here[2][p]) + rad3
            rates = [
                mach * axial[0][p] + div,
                mach * axial[1][p] + axial[4][p],
                mach * axial[2][p] + circ(here[4][p]),
                mach * axial[3][p] + rad4,
                mach * axial[4][p] + div,
            ]
            sigma = damping * pml_ref[a0 + p].astype(jnp.float32)
            for f in range(F):
                rows = rows_of(f, a0 + p)
                value = -step_size * (rates[f] + sigma * here[f][p])
                if section:
                    value = value + section_a[section] * inc_ref[rows, :]
                out_ref[rows, :] = value
        return carry

    lax.fori_loop(0, A // B, step, 0)


def finish_kernel(
    section, last, offsets_ref, q_ref, part_ref, east_ref, odd_ref, rad_ref, own_ref, next_ref, *refs
):
    b = section_b[section]
    new_ref, inc_ref, *messages, low, high, faces = refs
    even = lax.rem(lax.axis_index("circ"), 2) == 0
    low_rad = lax.axis_index("rad") == 0
    rotor = lax.axis_index("half") == 0

    inside = slice(3 * A, 3 * A + 2 * W * A)
    low[inside, :] = jnp.where(even, odd_ref[...], east_ref[...])
    high[inside, :] = jnp.where(even, east_ref[...], odd_ref[...])
    sub = lax.broadcasted_iota(jnp.int32, (8, L), 0)

    def circ(a, g):
        lower = low[pl.ds((3 + g * W) * A + a, 8, stride=A), :]
        upper = high[pl.ds(g * W * A + a, 8, stride=A), :]
        return jnp.concatenate([jnp.where(sub < W, lower, 0.0), jnp.where(sub >= 8 - W, upper, 0.0)], axis=0)

    lane = lax.broadcasted_iota(jnp.int32, (GROUP, L), 1)
    rim_lanes = (lane >= jnp.where(low_rad, L - W, 0)) & (lane < jnp.where(low_rad, L, W))
    base = jnp.where(low_rad, L - W, 0)
    groups = A * C // GROUP

    def step(n, carry):
        rims = [
            jnp.where(rim_lanes, pltpu.roll(rad_ref[...], lax.rem(base + L - 8 * (n + g * groups), L), 1), 0.0)
            for g in range(2)
        ]
        for p in range(GROUP // C):
            a = n * (GROUP // C) + p
            div = circ(a, 0) + rims[0][p * C : (p + 1) * C]
            extra = [div, None, circ(a, 1), rims[1][p * C : (p + 1) * C], div]
            for f in range(F):
                rows = rows_of(f, a)
                value = part_ref[rows, :]
                if extra[f] is not None:
                    value = value - step_size * extra[f]
                inc_ref[rows, :] = value
                new_ref[rows, :] = q_ref[rows, :] + b * value
        return carry

    lax.fori_loop(0, groups, step, 0)

    for n in range(F * W):
        own, beyond = own_ref[n * C : (n + 1) * C, :], next_ref[n * C : (n + 1) * C, :]
        faces[2 * n * C : (2 * n + 1) * C, :] = jnp.where(rotor, own, beyond)
        faces[(2 * n + 1) * C : (2 * n + 2) * C, :] = jnp.where(rotor, beyond, own)
    shift = lax.rem(offsets_ref[section], C)
    start = jnp.where(rotor, shift, C - shift)
    sign = jnp.where(rotor, 1.0, -1.0)
    ghost = [[faces[pl.ds(2 * (f * W + m) * C + start, C), :] for m in range(W)] for f in range(F)]
    for i in range(W):
        a = jnp.where(rotor, A - 1 - i, i)
        axial = [sign * total_of([coeffs[k - 1] * ghost[f][k - 1 - i] for k in range(i + 1, W + 1)]) for f in range(F)]
        extra = [
            mach * axial[0] + axial[1],
            mach * axial[1] + axial[4],
            mach * axial[2],
            mach * axial[3],
            mach * axial[4] + axial[1],
        ]
        for f in range(F):
            rows = rows_of(f, a)
            delta = -step_size * extra[f]
            inc_ref[rows, :] += delta
            new_ref[rows, :] += b * delta
    if not last:
        pack(new_ref, *messages)


def swap_faces(face, blocks):
    count = lax.axis_size("circ")
    pairs = []
    for i in range(count):
        j = (i + blocks) % count
        pairs += [(2 * i, 2 * j + 1), (2 * j + 1, 2 * i)]
    return lax.ppermute(face, ("circ", "half"), pairs)


def exchange(messages, blocks):
    east, odd, rad, face = messages
    count = lax.axis_size("circ")
    return (
        lax.ppermute(east, "circ", [(i, i ^ 1) for i in range(count)]),
        lax.ppermute(odd, "circ", [(i, (i + (1 if i % 2 else -1)) % count) for i in range(count)]),
        lax.ppermute(rad, "rad", [(0, 1), (1, 0)]),
        swap_faces(face, blocks),
        swap_faces(face, blocks + 1),
    )


def local_terms(section, q, inc, pml_zone):
    return pl.pallas_call(
        functools.partial(local_kernel, section),
        out_shape=FIELDS,
        in_specs=[SM] + [VM] * (3 if section else 2),
        out_specs=VM,
        scratch_shapes=[pltpu.VMEM((F * (A + 2 * W) * C, L), jnp.float32)],
        compiler_params=PARAMS,
        cost_estimate=pl.CostEstimate(flops=20_000_000, bytes_accessed=3 * ROWS * L * 4, transcendentals=0),
        name=f"local{section}",
    )(pml_zone, band_matrix(), q, *([inc] if section else []))


def section_branch(section, blocks, q, inc, pml_zone, messages):
    arrived = exchange(messages, blocks)
    return local_terms(section, q, inc, pml_zone), arrived


def finish(section, offsets, q, part, arrived):
    last = section == SECTIONS - 1
    return pl.pallas_call(
        functools.partial(finish_kernel, section, last),
        out_shape=[FIELDS, FIELDS] + ([] if last else MESSAGES),
        in_specs=[SM] + [VM] * 7,
        out_specs=[VM] * (2 if last else 6),
        scratch_shapes=[
            pltpu.VMEM((16 * A, L), jnp.float32),
            pltpu.VMEM((16 * A, L), jnp.float32),
            pltpu.VMEM((2 * F * W * C, L), jnp.float32),
        ],
        compiler_params=PARAMS,
        name=f"finish{section}",
    )(offsets, q, part, *arrived)


def pack_kernel(q_ref, *messages):
    pack(q_ref, *messages)


def body(state, offsets, pml_zone):
    q = state.reshape(ROWS, L)
    inc = ()
    messages = pl.pallas_call(
        pack_kernel,
        out_shape=MESSAGES,
        in_specs=[VM],
        out_specs=[VM] * 4,
        compiler_params=PARAMS,
        name="pack",
    )(q)
    place = offsets // C
    kind = jnp.where(place == 0, 1, jnp.where(place == C, 2, 0))
    for section in range(SECTIONS):
        part, arrived = lax.switch(
            kind[section],
            [functools.partial(section_branch, section, blocks) for blocks in (-1, 0, C)],
            q,
            inc,
            pml_zone,
            messages,
        )
        q, inc, *messages = finish(section, offsets, q, part, arrived)
    return q.reshape(state.shape), inc.reshape(state.shape)


def solution(mesh):
    return jax.shard_map(
        body,
        mesh=mesh,
        in_specs=(P(None, "half", "circ", "rad"), P(), P("half")),
        out_specs=(P(None, "half", "circ", "rad"), P(None, "half", "circ", "rad")),
        check_vma=False,
    )
```

profile of v0, /device:TPU:1, one launch (start us, length us, event | category | flops | bytes accessed | tf_op | source)
XLA Modules:
  0.0 84.8 jit_solution(6825358722133557558)
XLA Ops:
  4.0 2.2 %pack.1 = (f32[480,128]{1,0:T(8,128)S(1)}, f32[480,128]{1,0:T(8,128)S(1)}, f32[96,128]{1,0:T(8,128)S(1)}, f32[400,128]{1,0:T(8,128)S(1)}) custom-call(f32[3840,128]{1,0:T(8,128)} %bitcast.6), custom_call_target="tpu_custom_call" | custom-call | tf_op jit(solution)/shard_map/pack/pallas_call | solution.py:292
  6.3 20.7 %conditional.3 = (f32[3840,128]{1,0:T(8,128)S(1)}, f32[480,128]{1,0:T(8,128)}, f32[480,128]{1,0:T(8,128)}, f32[96,128]{1,0:T(8,128)}, f32[400,128]{1,0:T(8,128)}, /*index=5*/f32[400,128]{1,0:T(8,128)}) conditional(s32[]{:T(128)} %bitcast.1, (s32[48]{0:T(128)S(1)}, f32[128,128]{1,0:T(8,128)}, f32[3840,128]{1,0:T(8,128)S(1)}, ...), branch_computations={%region_0.1_spmd, %region_1.2_spmd, %region_2.3_spmd} | conditional | flops 20000000 | bytes 9699576 | solution.py:303
  6.3 3.8 %collective-permute-start.5 = (f32[480,128]{1,0:T(8,128)S(1)}, f32[480,128]{1,0:T(8,128)}, u32[]{:S(2)}, u32[]{:S(2)}) collective-permute-start(f32[480,128]{1,0:T(8,128)S(1)} %get-tuple-element.148), channel_id=1, source_target_pairs={{0,4},{4,0},{8,12},{12,8},{16,20},{20,16},{24,28},{28,24},{32,36},... | collective-permute-start | bytes 737288 | tf_op jit(solution)/shard_map/cond/branch_1_fun/ppermute | solution.py:242
  10.1 5.8 %collective-permute-start.6 = (f32[480,128]{1,0:T(8,128)S(1)}, f32[480,128]{1,0:T(8,128)}, u32[]{:S(2)}, u32[]{:S(2)}) collective-permute-start(f32[480,128]{1,0:T(8,128)S(1)} %get-tuple-element.149), channel_id=1, source_target_pairs={{0,124},{4,8},{8,4},{12,16},{16,12},{20,24},{24,20},{28,32},{32,28... | collective-permute-start | bytes 737288 | tf_op jit(solution)/shard_map/cond/branch_1_fun/ppermute | solution.py:243
  15.9 2.5 %collective-permute-start.9 = (f32[400,128]{1,0:T(8,128)S(1)}, f32[400,128]{1,0:T(8,128)}, u32[]{:S(2)}, u32[]{:S(2)}) collective-permute-start(f32[400,128]{1,0:T(8,128)S(1)} %get-tuple-element.151), channel_id=1, source_target_pairs={{0,5},{5,0},{4,9},{9,4},{8,13},{13,8},{12,17},{17,12},{16,21},{21,... | collective-permute-start | bytes 614408 | tf_op jit(solution)/shard_map/cond/branch_1_fun/ppermute | solution.py:235
  18.8 4.6 %local0.4 = f32[3840,128]{1,0:T(8,128)S(1)} custom-call(s32[48]{0:T(128)S(1)} %get-tuple-element.145.pml_ref, f32[128,128]{1,0:T(8,128)} %get-tuple-element.146.band_ref, f32[3840,128]{1,0:T(8,128)S(1)} %get-tuple-element.147.q_ref), custom_call_target="tpu_custom_call" | custom-call | flops 20000000 | bytes 5898240 | tf_op jit(solution)/shard_map/cond/branch_1_fun/local0/pallas_call | solution.py:251
  23.4 1.1 %collective-permute-done.7 = f32[96,128]{1,0:T(8,128)} collective-permute-done((f32[96,128]{1,0:T(8,128)S(1)}, f32[96,128]{1,0:T(8,128)}, u32[]{:S(2)}, u32[]{:S(2)}) %collective-permute-start.7) | collective-permute-done | bytes 49184 | tf_op jit(solution)/shard_map/cond/branch_1_fun/ppermute | solution.py:244
  24.5 2.5 %collective-permute-done.9 = f32[400,128]{1,0:T(8,128)} collective-permute-done((f32[400,128]{1,0:T(8,128)S(1)}, f32[400,128]{1,0:T(8,128)}, u32[]{:S(2)}, u32[]{:S(2)}) %collective-permute-start.9) | collective-permute-done | bytes 204832 | tf_op jit(solution)/shard_map/cond/branch_1_fun/ppermute | solution.py:235
  27.0 1.3 %copy-done.2 = f32[3840,128]{1,0:T(8,128)} copy-done((f32[3840,128]{1,0:T(8,128)}, f32[3840,128]{1,0:T(8,128)S(1)}, u32[]{:S(2)}) %copy-start.2) | copy-done | bytes 1966104
  28.3 4.2 %finish0.1 = (f32[3840,128]{1,0:T(8,128)}, f32[3840,128]{1,0:T(8,128)S(1)}, f32[480,128]{1,0:T(8,128)S(1)}, f32[480,128]{1,0:T(8,128)S(1)}, f32[96,128]{1,0:T(8,128)S(1)}, /*index=5*/f32[400,128]{1,0:T(8,128)S(1)}) custom-call(s32[3]{0:T(128)S(1)} %copy-done, f32[3840,128]{1,0:T(8,128)S(1)} %bitcast.10, f32[3840,128]{1,0:T(8,128)} %copy-done.2, ...), custom_call_target="tpu_custom_call" | custom-call | tf_op jit(solution)/shard_map/finish0/pallas_call | solution.py:270
  32.5 25.1 %conditional.4 = (f32[3840,128]{1,0:T(8,128)S(1)}, f32[480,128]{1,0:T(8,128)}, f32[480,128]{1,0:T(8,128)}, f32[96,128]{1,0:T(8,128)}, f32[400,128]{1,0:T(8,128)}, /*index=5*/f32[400,128]{1,0:T(8,128)}) conditional(s32[]{:T(128)} %bitcast.2, (s32[48]{0:T(128)S(1)}, f32[128,128]{1,0:T(8,128)S(1)}, f32[3840,128]{1,0:T(8,128)}, ...), branch_computations={%region_3.4_spmd, %region_4.5_spmd, %region_5.6_spmd} | conditional | flops 20000000 | bytes 9699576 | solution.py:303
  32.5 2.6 %collective-permute-start.25 = (f32[480,128]{1,0:T(8,128)S(1)}, f32[480,128]{1,0:T(8,128)}, u32[]{:S(2)}, u32[]{:S(2)}) collective-permute-start(f32[480,128]{1,0:T(8,128)S(1)} %get-tuple-element.179), channel_id=1, source_target_pairs={{0,4},{4,0},{8,12},{12,8},{16,20},{20,16},{24,28},{28,24},{32,36},... | collective-permute-start | bytes 737288 | tf_op jit(solution)/shard_map/cond/branch_2_fun/ppermute | solution.py:242
  35.1 5.8 %collective-permute-start.26 = (f32[480,128]{1,0:T(8,128)S(1)}, f32[480,128]{1,0:T(8,128)}, u32[]{:S(2)}, u32[]{:S(2)}) collective-permute-start(f32[480,128]{1,0:T(8,128)S(1)} %get-tuple-element.180), channel_id=1, source_target_pairs={{0,124},{4,8},{8,4},{12,16},{16,12},{20,24},{24,20},{28,32},{32,28... | collective-permute-start | bytes 737288 | tf_op jit(solution)/shard_map/cond/branch_2_fun/ppermute | solution.py:243
  43.6 5.4 %local1.5 = f32[3840,128]{1,0:T(8,128)S(1)} custom-call(s32[48]{0:T(128)S(1)} %get-tuple-element.175.pml_ref, f32[128,128]{1,0:T(8,128)S(1)} %get-tuple-element.176.band_ref, f32[3840,128]{1,0:T(8,128)} %get-tuple-element.177.q_ref, f32[3840,128]{1,0:T(8,128)S(1)} %get-tuple-element.178.refs_0_), custom_call_target="tpu_custom_call" | custom-call | flops 20000000 | bytes 5898240 | tf_op jit(solution)/shard_map/cond/branch_2_fun/local1/pallas_call | solution.py:251
  49.0 1.5 %collective-permute-done.27 = f32[96,128]{1,0:T(8,128)} collective-permute-done((f32[96,128]{1,0:T(8,128)S(1)}, f32[96,128]{1,0:T(8,128)}, u32[]{:S(2)}, u32[]{:S(2)}) %collective-permute-start.27) | collective-permute-done | bytes 49184 | tf_op jit(solution)/shard_map/cond/branch_2_fun/ppermute | solution.py:244
  51.0 6.7 %collective-permute-done.28 = f32[400,128]{1,0:T(8,128)} collective-permute-done((f32[400,128]{1,0:T(8,128)S(1)}, f32[400,128]{1,0:T(8,128)}, u32[]{:S(2)}, u32[]{:S(2)}) %collective-permute-start.28) | collective-permute-done | bytes 204832 | tf_op jit(solution)/shard_map/cond/branch_2_fun/ppermute | solution.py:235
  57.6 3.4 %finish1.1 = (f32[3840,128]{1,0:T(8,128)S(1)}, f32[3840,128]{1,0:T(8,128)S(1)}, f32[480,128]{1,0:T(8,128)S(1)}, f32[480,128]{1,0:T(8,128)S(1)}, f32[96,128]{1,0:T(8,128)S(1)}, /*index=5*/f32[400,128]{1,0:T(8,128)S(1)}) custom-call(s32[3]{0:T(128)S(1)} %copy-done, f32[3840,128]{1,0:T(8,128)} %get-tuple-element.255.q_ref, ...), custom_call_target="tpu_custom_call" | custom-call | tf_op jit(solution)/shard_map/finish1/pallas_call | solution.py:270
  61.0 19.6 %conditional.5 = (f32[3840,128]{1,0:T(8,128)S(1)}, f32[480,128]{1,0:T(8,128)}, f32[480,128]{1,0:T(8,128)}, f32[96,128]{1,0:T(8,128)}, f32[400,128]{1,0:T(8,128)}, /*index=5*/f32[400,128]{1,0:T(8,128)}) conditional(s32[]{:T(128)} %bitcast.3, (s32[48]{0:T(128)S(1)}, f32[128,128]{1,0:T(8,128)S(1)}, f32[3840,128]{1,0:T(8,128)S(1)}, ...), branch_computations={%region_6.7_spmd, %region_7.8_spmd, %region_8.9_spmd} | conditional | flops 20000000 | bytes 9699576 | solution.py:303
  61.1 3.6 %collective-permute-start.31 = (f32[480,128]{1,0:T(8,128)S(1)}, f32[480,128]{1,0:T(8,128)}, u32[]{:S(2)}, u32[]{:S(2)}) collective-permute-start(f32[480,128]{1,0:T(8,128)S(1)} %get-tuple-element.188), channel_id=1, source_target_pairs={{0,124},{4,8},{8,4},{12,16},{16,12},{20,24},{24,20},{28,32},{32,28... | collective-permute-start | bytes 737288 | tf_op jit(solution)/shard_map/cond/branch_0_fun/ppermute | solution.py:243
  65.6 1.2 %collective-permute-start.32 = (f32[96,128]{1,0:T(8,128)S(1)}, f32[96,128]{1,0:T(8,128)}, u32[]{:S(2)}, u32[]{:S(2)}) collective-permute-start(f32[96,128]{1,0:T(8,128)S(1)} %get-tuple-element.189), channel_id=1, source_target_pairs={{0,2},{2,0},{1,3},{3,1},{4,6},{6,4},{5,7},{7,5},{8,10},{10,8},{9,1... | collective-permute-start | bytes 147464 | tf_op jit(solution)/shard_map/cond/branch_0_fun/ppermute | solution.py:244
  66.8 4.4 %local2.3 = f32[3840,128]{1,0:T(8,128)S(1)} custom-call(s32[48]{0:T(128)S(1)} %get-tuple-element.183.pml_ref, f32[128,128]{1,0:T(8,128)S(1)} %get-tuple-element.184.band_ref, f32[3840,128]{1,0:T(8,128)S(1)} %get-tuple-element.185.q_ref, f32[3840,128]{1,0:T(8,128)S(1)} %get-tuple-element.186.refs_0_), custom_call_target="tpu_custom_call" | custom-call | flops 20000000 | bytes 5898240 | tf_op jit(solution)/shard_map/cond/branch_0_fun/local2/pallas_call | solution.py:251
  71.2 7.5 %collective-permute-done.32 = f32[96,128]{1,0:T(8,128)} collective-permute-done((f32[96,128]{1,0:T(8,128)S(1)}, f32[96,128]{1,0:T(8,128)}, u32[]{:S(2)}, u32[]{:S(2)}) %collective-permute-start.32) | collective-permute-done | bytes 49184 | tf_op jit(solution)/shard_map/cond/branch_0_fun/ppermute | solution.py:244
  78.7 1.9 %collective-permute-done.33 = f32[400,128]{1,0:T(8,128)} collective-permute-done((f32[400,128]{1,0:T(8,128)S(1)}, f32[400,128]{1,0:T(8,128)}, u32[]{:S(2)}, u32[]{:S(2)}) %collective-permute-start.33) | collective-permute-done | bytes 204832 | tf_op jit(solution)/shard_map/cond/branch_0_fun/ppermute | solution.py:235
  80.6 4.2 %finish2.1 = (f32[3840,128]{1,0:T(8,128)}, f32[3840,128]{1,0:T(8,128)}) custom-call(s32[3]{0:T(128)S(1)} %copy-done, f32[3840,128]{1,0:T(8,128)S(1)} %get-tuple-element.267.q_ref, f32[3840,128]{1,0:T(8,128)S(1)} %get-tuple-element.273.part_ref, f32[480,128]{1,0:T(8,128)} %get-tuple-element.274.east_ref, f32[480,128]{1,0:T(8,128)} %get-tuple-element.275.odd_ref, ...), custom_call_target="tpu_custom_call" | custom-call | tf_op jit(solution)/shard_map/finish2/pallas_call | solution.py:270
  (28 shorter events, 6.0 us)
Async XLA Ops:
  0.6 5.6 %copy-start.4 = (s32[48]{0:T(128)S(1)}, s32[48]{0:T(128)}, u32[]{:S(2)}) copy-start(s32[48]{0:T(128)} %param.23) | copy-start | bytes 580
  0.6 5.6 %copy-start.1 = (f32[5,48,16,128]{3,2,1,0:T(8,128)S(1)}, f32[5,48,16,128]{3,2,1,0:T(8,128)}, u32[]{:S(2)}) copy-start(f32[5,48,16,128]{3,2,1,0:T(8,128)} %param.21) | copy-start | bytes 5898244
  6.3 22.0 %copy-start = (s32[3]{0:T(128)S(1)}, s32[3]{0:T(128)}, u32[]{:S(2)}) copy-start(s32[3]{0:T(128)} %offsets_ref.5) | copy-start | bytes 40
  6.3 20.7 %collective-permute-start.5 = (f32[480,128]{1,0:T(8,128)S(1)}, f32[480,128]{1,0:T(8,128)}, u32[]{:S(2)}, u32[]{:S(2)}) collective-permute-start(f32[480,128]{1,0:T(8,128)S(1)} %get-tuple-element.148), channel_id=1, source_target_pairs={{0,4},{4,0},{8,12},{12,8},{16,20},{20,16},{24,28},{28,24},{32,36},... | collective-permute-start | bytes 737288 | tf_op jit(solution)/shard_map/cond/branch_1_fun/ppermute | solution.py:242
  10.1 16.9 %collective-permute-start.6 = (f32[480,128]{1,0:T(8,128)S(1)}, f32[480,128]{1,0:T(8,128)}, u32[]{:S(2)}, u32[]{:S(2)}) collective-permute-start(f32[480,128]{1,0:T(8,128)S(1)} %get-tuple-element.149), channel_id=1, source_target_pairs={{0,124},{4,8},{8,4},{12,16},{16,12},{20,24},{24,20},{28,32},{32,28... | collective-permute-start | bytes 737288 | tf_op jit(solution)/shard_map/cond/branch_1_fun/ppermute | solution.py:243
  15.9 11.1 %collective-permute-start.9 = (f32[400,128]{1,0:T(8,128)S(1)}, f32[400,128]{1,0:T(8,128)}, u32[]{:S(2)}, u32[]{:S(2)}) collective-permute-start(f32[400,128]{1,0:T(8,128)S(1)} %get-tuple-element.151), channel_id=1, source_target_pairs={{0,5},{5,0},{4,9},{9,4},{8,13},{13,8},{12,17},{17,12},{16,21},{21,... | collective-permute-start | bytes 614408 | tf_op jit(solution)/shard_map/cond/branch_1_fun/ppermute | solution.py:235
  18.4 8.6 %collective-permute-start.8 = (f32[400,128]{1,0:T(8,128)S(1)}, f32[400,128]{1,0:T(8,128)}, u32[]{:S(2)}, u32[]{:S(2)}) collective-permute-start(f32[400,128]{1,0:T(8,128)S(1)} %get-tuple-element.151), channel_id=1, source_target_pairs={{0,1},{1,0},{4,5},{5,4},{8,9},{9,8},{12,13},{13,12},{16,17},{17,16... | collective-permute-start | bytes 614408 | tf_op jit(solution)/shard_map/cond/branch_1_fun/ppermute | solution.py:235
  18.4 6.1 %collective-permute-start.7 = (f32[96,128]{1,0:T(8,128)S(1)}, f32[96,128]{1,0:T(8,128)}, u32[]{:S(2)}, u32[]{:S(2)}) collective-permute-start(f32[96,128]{1,0:T(8,128)S(1)} %get-tuple-element.150), channel_id=1, source_target_pairs={{0,2},{2,0},{1,3},{3,1},{4,6},{6,4},{5,7},{7,5},{8,10},{10,8},{9,1... | collective-permute-start | bytes 147464 | tf_op jit(solution)/shard_map/cond/branch_1_fun/ppermute | solution.py:244
  27.0 1.3 %copy-start.2 = (f32[3840,128]{1,0:T(8,128)}, f32[3840,128]{1,0:T(8,128)S(1)}, u32[]{:S(2)}) copy-start(f32[3840,128]{1,0:T(8,128)S(1)} %get-tuple-element.249.part_ref) | copy-start | bytes 5898244
  28.3 4.2 %copy-start.3 = (f32[128,128]{1,0:T(8,128)S(1)}, f32[128,128]{1,0:T(8,128)}, u32[]{:S(2)}) copy-start(f32[128,128]{1,0:T(8,128)} %constant.33.clone) | copy-start | bytes 196612
  32.5 25.1 %collective-permute-start.25 = (f32[480,128]{1,0:T(8,128)S(1)}, f32[480,128]{1,0:T(8,128)}, u32[]{:S(2)}, u32[]{:S(2)}) collective-permute-start(f32[480,128]{1,0:T(8,128)S(1)} %get-tuple-element.179), channel_id=1, source_target_pairs={{0,4},{4,0},{8,12},{12,8},{16,20},{20,16},{24,28},{28,24},{32,36},... | collective-permute-start | bytes 737288 | tf_op jit(solution)/shard_map/cond/branch_2_fun/ppermute | solution.py:242
  35.1 22.5 %collective-permute-start.26 = (f32[480,128]{1,0:T(8,128)S(1)}, f32[480,128]{1,0:T(8,128)}, u32[]{:S(2)}, u32[]{:S(2)}) collective-permute-start(f32[480,128]{1,0:T(8,128)S(1)} %get-tuple-element.180), channel_id=1, source_target_pairs={{0,124},{4,8},{8,4},{12,16},{16,12},{20,24},{24,20},{28,32},{32,28... | collective-permute-start | bytes 737288 | tf_op jit(solution)/shard_map/cond/branch_2_fun/ppermute | solution.py:243
  40.9 10.1 %collective-permute-start.29 = (f32[400,128]{1,0:T(8,128)S(1)}, f32[400,128]{1,0:T(8,128)}, u32[]{:S(2)}, u32[]{:S(2)}) collective-permute-start(f32[400,128]{1,0:T(8,128)S(1)} %get-tuple-element.182), channel_id=1, source_target_pairs={{0,69},{69,0},{4,73},{73,4},{8,77},{77,8},{12,81},{81,12},{16,85},... | collective-permute-start | bytes 614408 | tf_op jit(solution)/shard_map/cond/branch_2_fun/ppermute | solution.py:235
  41.8 15.8 %collective-permute-start.28 = (f32[400,128]{1,0:T(8,128)S(1)}, f32[400,128]{1,0:T(8,128)}, u32[]{:S(2)}, u32[]{:S(2)}) collective-permute-start(f32[400,128]{1,0:T(8,128)S(1)} %get-tuple-element.182), channel_id=1, source_target_pairs={{0,65},{65,0},{4,69},{69,4},{8,73},{73,8},{12,77},{77,12},{16,81},... | collective-permute-start | bytes 614408 | tf_op jit(solution)/shard_map/cond/branch_2_fun/ppermute | solution.py:235
  42.5 8.0 %collective-permute-start.27 = (f32[96,128]{1,0:T(8,128)S(1)}, f32[96,128]{1,0:T(8,128)}, u32[]{:S(2)}, u32[]{:S(2)}) collective-permute-start(f32[96,128]{1,0:T(8,128)S(1)} %get-tuple-element.181), channel_id=1, source_target_pairs={{0,2},{2,0},{1,3},{3,1},{4,6},{6,4},{5,7},{7,5},{8,10},{10,8},{9,1... | collective-permute-start | bytes 147464 | tf_op jit(solution)/shard_map/cond/branch_2_fun/ppermute | solution.py:244
  61.0 19.6 %collective-permute-start.30 = (f32[480,128]{1,0:T(8,128)S(1)}, f32[480,128]{1,0:T(8,128)}, u32[]{:S(2)}, u32[]{:S(2)}) collective-permute-start(f32[480,128]{1,0:T(8,128)S(1)} %get-tuple-element.187), channel_id=1, source_target_pairs={{0,4},{4,0},{8,12},{12,8},{16,20},{20,16},{24,28},{28,24},{32,36},... | collective-permute-start | bytes 737288 | tf_op jit(solution)/shard_map/cond/branch_0_fun/ppermute | solution.py:242
  61.1 19.5 %collective-permute-start.31 = (f32[480,128]{1,0:T(8,128)S(1)}, f32[480,128]{1,0:T(8,128)}, u32[]{:S(2)}, u32[]{:S(2)}) collective-permute-start(f32[480,128]{1,0:T(8,128)S(1)} %get-tuple-element.188), channel_id=1, source_target_pairs={{0,124},{4,8},{8,4},{12,16},{16,12},{20,24},{24,20},{28,32},{32,28... | collective-permute-start | bytes 737288 | tf_op jit(solution)/shard_map/cond/branch_0_fun/ppermute | solution.py:243
  64.7 14.0 %collective-permute-start.34 = (f32[400,128]{1,0:T(8,128)S(1)}, f32[400,128]{1,0:T(8,128)}, u32[]{:S(2)}, u32[]{:S(2)}) collective-permute-start(f32[400,128]{1,0:T(8,128)S(1)} %get-tuple-element.190), channel_id=1, source_target_pairs={{0,1},{1,0},{4,5},{5,4},{8,9},{9,8},{12,13},{13,12},{16,17},{17,16... | collective-permute-start | bytes 614408 | tf_op jit(solution)/shard_map/cond/branch_0_fun/ppermute | solution.py:235
  65.6 15.0 %collective-permute-start.33 = (f32[400,128]{1,0:T(8,128)S(1)}, f32[400,128]{1,0:T(8,128)}, u32[]{:S(2)}, u32[]{:S(2)}) collective-permute-start(f32[400,128]{1,0:T(8,128)S(1)} %get-tuple-element.190), channel_id=1, source_target_pairs={{0,125},{125,0},{4,1},{1,4},{8,5},{5,8},{12,9},{9,12},{16,13},{13,... | collective-permute-start | bytes 614408 | tf_op jit(solution)/shard_map/cond/branch_0_fun/ppermute | solution.py:235
  65.6 13.1 %collective-permute-start.32 = (f32[96,128]{1,0:T(8,128)S(1)}, f32[96,128]{1,0:T(8,128)}, u32[]{:S(2)}, u32[]{:S(2)}) collective-permute-start(f32[96,128]{1,0:T(8,128)S(1)} %get-tuple-element.189), channel_id=1, source_target_pairs={{0,2},{2,0},{1,3},{3,1},{4,6},{6,4},{5,7},{7,5},{8,10},{10,8},{9,1... | collective-permute-start | bytes 147464 | tf_op jit(solution)/shard_map/cond/branch_0_fun/ppermute | solution.py:244
where the time goes:
time: 83.7 us; the launch traced here: 84.8 us
  starting transfers between devices  29.4 us (35%)
  Pallas kernels  28.4 us (34%)
  waiting for transfers between devices  21.5 us (26%)
  between operations  2.64 us (3%)
  local copies, waits for them, and re-layouts  1.94 us (2%)
    ppermute x3, starting transfers between devices, exchange(): lax.ppermute(odd, 'circ', [(i, (i + (1 if i % 2 else -1)) % count) for i...  15.1 us
    pallas_call x3, Pallas kernels, local_terms(): pl.pallas_call(functools.partial(local_kernel, section), out_shape=FIELDS...  14.4 us
    pallas_call x3, Pallas kernels, finish(): pl.pallas_call(functools.partial(finish_kernel, section, last), out_shape...  11.8 us
    ppermute x6, waiting for transfers between devices, swap_faces(): return lax.ppermute(face, ('circ', 'half'), pairs)  11.5 us
    ppermute x3, waiting for transfers between devices, exchange(): lax.ppermute(rad, 'rad', [(0, 1), (1, 0)])  10.1 us
    ppermute x3, starting transfers between devices, exchange(): lax.ppermute(east, 'circ', [(i, i ^ 1) for i in range(count)])  6.5 us
    ppermute x6, starting transfers between devices, swap_faces(): return lax.ppermute(face, ('circ', 'half'), pairs)  5.1 us
    ppermute x3, starting transfers between devices, exchange(): lax.ppermute(rad, 'rad', [(0, 1), (1, 0)])  2.65 us
  transfers between devices with their start and end apart: 15, of which 7 were waited for; matrix products, arithmetic and copies ran while one was open for 0% of the time, Pallas kernels for 17%

commit v1 on v0

--- a/solution.py
+++ b/solution.py
@@ -235,15 +235,13 @@
     return lax.ppermute(face, ("circ", "half"), pairs)
 
 
-def exchange(messages, blocks):
-    east, odd, rad, face = messages
+def exchange_rims(messages):
+    east, odd, rad, _ = messages
     count = lax.axis_size("circ")
     return (
         lax.ppermute(east, "circ", [(i, i ^ 1) for i in range(count)]),
         lax.ppermute(odd, "circ", [(i, (i + (1 if i % 2 else -1)) % count) for i in range(count)]),
         lax.ppermute(rad, "rad", [(0, 1), (1, 0)]),
-        swap_faces(face, blocks),
-        swap_faces(face, blocks + 1),
     )
 
 
@@ -260,9 +258,8 @@
     )(pml_zone, band_matrix(), q, *([inc] if section else []))
 
 
-def section_branch(section, blocks, q, inc, pml_zone, messages):
-    arrived = exchange(messages, blocks)
-    return local_terms(section, q, inc, pml_zone), arrived
+def section_branch(section, blocks, q, inc, pml_zone, face):
+    return local_terms(section, q, inc, pml_zone), swap_faces(face, blocks), swap_faces(face, blocks + 1)
 
 
 def finish(section, offsets, q, part, arrived):
@@ -282,33 +279,60 @@
     )(offsets, q, part, *arrived)
 
 
-def pack_kernel(q_ref, *messages):
+def enter_kernel(offsets_ref, state_ref, *refs):
+    *messages, kind0, kind1, kind2, q_ref, sems = refs
+    copies = []
+    for n, f in enumerate((2, 4, 3)):
+        rows = pl.ds(f * FIELD, FIELD)
+        copies.append(pltpu.make_async_copy(state_ref.at[rows], q_ref.at[rows], sems.at[n]))
+    edge = jnp.where(lax.axis_index("half") == 0, (A - W) * C, 0)
+    for f in (0, 1):
+        rows = pl.ds(pl.multiple_of(f * FIELD + edge, C), W * C)
+        copies.append(pltpu.make_async_copy(state_ref.at[rows], q_ref.at[rows], sems.at[3 + f]))
+    for copy in copies:
+        copy.start()
+    for section, kind in enumerate((kind0, kind1, kind2)):
+        place = lax.div(offsets_ref[section], C)
+        kind[0] = jnp.where(place == 0, 1, jnp.where(place == C, 2, 0))
+    for copy in copies:
+        copy.wait()
     pack(q_ref, *messages)
+
+
+def first_branch(blocks, q, offsets, pml_zone, messages):
+    rims = exchange_rims(messages)
+    part, own, beyond = section_branch(0, blocks, q, (), pml_zone, messages[3])
+    return finish(0, offsets, q, part, (*rims, own, beyond))
 
 
 def body(state, offsets, pml_zone):
     q = state.reshape(ROWS, L)
-    inc = ()
-    messages = pl.pallas_call(
-        pack_kernel,
-        out_shape=MESSAGES,
-        in_specs=[VM],
-        out_specs=[VM] * 4,
+    flag = jax.ShapeDtypeStruct((1,), jnp.int32)
+    rest = pl.pallas_call(
+        enter_kernel,
+        out_shape=MESSAGES + [flag] * SECTIONS,
+        in_specs=[SM, pl.BlockSpec(memory_space=pltpu.HBM)],
+        out_specs=[VM] * 4 + [SM] * SECTIONS,
+        scratch_shapes=[pltpu.VMEM((ROWS, L), jnp.float32), pltpu.SemaphoreType.DMA((W,))],
         compiler_params=PARAMS,
-        name="pack",
-    )(q)
-    place = offsets // C
-    kind = jnp.where(place == 0, 1, jnp.where(place == C, 2, 0))
-    for section in range(SECTIONS):
-        part, arrived = lax.switch(
-            kind[section],
-            [functools.partial(section_branch, section, blocks) for blocks in (-1, 0, C)],
+        name="enter",
+    )(offsets, pltpu.with_memory_space_constraint(q, pltpu.HBM))
+    messages, kinds = rest[:4], rest[4:]
+    shifts = (-1, 0, C)
+    q, inc, *messages = lax.switch(
+        kinds[0][0], [functools.partial(first_branch, blocks) for blocks in shifts], q, offsets, pml_zone, messages
+    )
+    for section in range(1, SECTIONS):
+        rims = exchange_rims(messages)
+        part, own, beyond = lax.switch(
+            kinds[section][0],
+            [functools.partial(section_branch, section, blocks) for blocks in shifts],
             q,
             inc,
             pml_zone,
-            messages,
+            messages[3],
         )
-        q, inc, *messages = finish(section, offsets, q, part, arrived)
+        q, inc, *messages = finish(section, offsets, q, part, (*rims, own, beyond))
     return q.reshape(state.shape), inc.reshape(state.shape)
 
 

time: 83.7 us -> 80.9 us (0.967); the launches traced: 84.8 us -> 79.4 us
  waiting for transfers between devices: 21.5 us -> 17.8 us
    ppermute x9, waiting for transfers between devices: 10.1 us -> 0.41 us  [the longest x3 0.39 us: exchange_rims(): lax.ppermute(rad, 'rad', [(0, 1), (1, 0)])]
    ppermute x6, waiting for transfers between devices: 11.5 us -> 17.4 us  [swap_faces(): return lax.ppermute(face, ('circ', 'half'), pairs)]
    ppermute x9, starting transfers between devices: 24.3 us -> 19.5 us  [the longest x3 12.7 us: exchange_rims(): lax.ppermute(odd, 'circ', [(i, (i + (1 if i % 2 else -1)) % count) for i...]
    ppermute x6, starting transfers between devices: 5.1 us -> 9.89 us  [swap_faces(): return lax.ppermute(face, ('circ', 'half'), pairs)]
    pallas_call x3, Pallas kernels: 11.8 us -> 10.9 us  [finish(): pl.pallas_call(functools.partial(finish_kernel, section, last), out_shape...]
  transfers between devices with their start and end apart: 15 -> 15, of which waited for: 7 -> 5; matrix products, arithmetic and copies ran while one was open for 0% -> 0% of each run, Pallas kernels for 17% -> 18%
where the time goes in v1:
time: 80.9 us; the launch traced here: 79.4 us
  starting transfers between devices  29.3 us (36%)
  Pallas kernels  28.2 us (35%)
  waiting for transfers between devices  17.8 us (22%)
  between operations  2.68 us (3%)
  local copies, waits for them, and re-layouts  1.27 us (2%)
    ppermute x6, waiting for transfers between devices, swap_faces(): return lax.ppermute(face, ('circ', 'half'), pairs)  17.4 us
    pallas_call x3, Pallas kernels, local_terms(): pl.pallas_call(functools.partial(local_kernel, section), out_shape=FIELDS...  14.4 us
    ppermute x3, starting transfers between devices, exchange_rims(): lax.ppermute(odd, 'circ', [(i, (i + (1 if i % 2 else -1)) % count) for i...  12.7 us
    pallas_call x3, Pallas kernels, finish(): pl.pallas_call(functools.partial(finish_kernel, section, last), out_shape...  10.9 us
    ppermute x6, starting transfers between devices, swap_faces(): return lax.ppermute(face, ('circ', 'half'), pairs)  9.89 us
    ppermute x3, starting transfers between devices, exchange_rims(): lax.ppermute(east, 'circ', [(i, i ^ 1) for i in range(count)])  4.15 us
    pallas_call x1, Pallas kernels, body(): pl.pallas_call(enter_kernel, out_shape=MESSAGES + [flag] * SECTIONS, in_s...  2.9 us
    ppermute x3, starting transfers between devices, exchange_rims(): lax.ppermute(rad, 'rad', [(0, 1), (1, 0)])  2.61 us
  transfers between devices with their start and end apart: 15, of which 5 were waited for; matrix products, arithmetic and copies ran while one was open for 0% of the time, Pallas kernels for 18%

profile of v1, /device:TPU:1, one launch (start us, length us, event | category | flops | bytes accessed | tf_op | source)
XLA Modules:
  0.0 79.4 jit_solution(9540506054622641052)
XLA Ops:
  0.7 2.9 %enter.1 = (f32[480,128]{1,0:T(8,128)S(1)}, f32[480,128]{1,0:T(8,128)S(1)}, f32[96,128]{1,0:T(8,128)S(1)}, f32[400,128]{1,0:T(8,128)S(1)}, s32[1]{0:T(128)}, /*index=5*/s32[1]{0:T(128)}, s32[1]{0:T(128)}) custom-call(s32[3]{0:T(128)} %offsets_ref.5, f32[3840,128]{1,0:T(8,128)} %bitcast.6), custom_call_target="tpu_custom_call" | custom-call | tf_op jit(solution)/shard_map/enter/pallas_call | solution.py:311
  4.3 29.5 %conditional.3 = ((f32[3840,128]{1,0:T(8,128)}, f32[3840,128]{1,0:T(8,128)S(1)}, f32[480,128]{1,0:T(8,128)S(1)}, f32[480,128]{1,0:T(8,128)S(1)}, f32[96,128]{1,0:T(8,128)S(1)}, /*index=5*/f32[400,128]{1,0:T(8,128)S(1)})) conditional(s32[]{:T(128)} %bitcast.1, (s32[48]{0:T(128)S(1)}, f32[128,128]{1,0:T(8,128)}, ...), branch_computations={%region_0.0_spmd, %region_1.0_spmd, %region_2.0_spmd} | conditional | flops 20000000 | bytes 9699536 | solution.py:322
  4.3 3.8 %collective-permute-start.10 = (f32[480,128]{1,0:T(8,128)S(1)}, f32[480,128]{1,0:T(8,128)S(1)}, u32[]{:S(2)}, u32[]{:S(2)}) collective-permute-start(f32[480,128]{1,0:T(8,128)S(1)} %get-tuple-element.128), channel_id=1, source_target_pairs={{0,4},{4,0},{8,12},{12,8},{16,20},{20,16},{24,28},{28,24},{32,36},... | collective-permute-start | bytes 737288 | tf_op jit(solution)/shard_map/cond/branch_2_fun/ppermute | solution.py:242
  8.1 5.8 %collective-permute-start.11 = (f32[480,128]{1,0:T(8,128)S(1)}, f32[480,128]{1,0:T(8,128)S(1)}, u32[]{:S(2)}, u32[]{:S(2)}) collective-permute-start(f32[480,128]{1,0:T(8,128)S(1)} %get-tuple-element.129), channel_id=1, source_target_pairs={{0,124},{4,8},{8,4},{12,16},{16,12},{20,24},{24,20},{28,32},{32,28... | collective-permute-start | bytes 737288 | tf_op jit(solution)/shard_map/cond/branch_2_fun/ppermute | solution.py:243
  13.9 3.1 %collective-permute-start.14 = (f32[400,128]{1,0:T(8,128)S(1)}, f32[400,128]{1,0:T(8,128)S(1)}, u32[]{:S(2)}, u32[]{:S(2)}) collective-permute-start(f32[400,128]{1,0:T(8,128)S(1)} %get-tuple-element.131), channel_id=1, source_target_pairs={{0,69},{69,0},{4,73},{73,4},{8,77},{77,8},{12,81},{81,12},{16,85},... | collective-permute-start | bytes 614408 | tf_op jit(solution)/shard_map/cond/branch_2_fun/ppermute | solution.py:235
  17.4 4.6 %local0.5.part_ref = f32[3840,128]{1,0:T(8,128)S(1)} custom-call(s32[48]{0:T(128)S(1)} %get-tuple-element.126.pml_ref, f32[128,128]{1,0:T(8,128)} %get-tuple-element.127.band_ref, f32[3840,128]{1,0:T(8,128)S(1)} %get-tuple-element.125.q_ref), custom_call_target="tpu_custom_call" | custom-call | flops 20000000 | bytes 5898240 | tf_op jit(solution)/shard_map/cond/branch_2_fun/local0/pallas_call | solution.py:249
  22.4 2.3 %collective-permute-done.14.next_ref = f32[400,128]{1,0:T(8,128)S(1)} collective-permute-done((f32[400,128]{1,0:T(8,128)S(1)}, f32[400,128]{1,0:T(8,128)S(1)}, u32[]{:S(2)}, u32[]{:S(2)}) %collective-permute-start.14) | collective-permute-done | bytes 204832 | tf_op jit(solution)/shard_map/cond/branch_2_fun/ppermute | solution.py:235
  24.6 5.9 %collective-permute-done.13.own_ref = f32[400,128]{1,0:T(8,128)S(1)} collective-permute-done((f32[400,128]{1,0:T(8,128)S(1)}, f32[400,128]{1,0:T(8,128)S(1)}, u32[]{:S(2)}, u32[]{:S(2)}) %collective-permute-start.13) | collective-permute-done | bytes 204832 | tf_op jit(solution)/shard_map/cond/branch_2_fun/ppermute | solution.py:235
  30.6 3.2 %finish0.5 = (f32[3840,128]{1,0:T(8,128)}, f32[3840,128]{1,0:T(8,128)S(1)}, f32[480,128]{1,0:T(8,128)S(1)}, f32[480,128]{1,0:T(8,128)S(1)}, f32[96,128]{1,0:T(8,128)S(1)}, /*index=5*/f32[400,128]{1,0:T(8,128)S(1)}) custom-call(s32[3]{0:T(128)S(1)} %get-tuple-element.124.offsets_ref, f32[3840,128]{1,0:T(8,128)S(1)} %get-tuple-element.125.q_ref, ...), custom_call_target="tpu_custom_call" | custom-call | tf_op jit(solution)/shard_map/cond/branch_2_fun/finish0/pallas_call | solution.py:267
  34.0 3.4 %collective-permute-start.28 = (f32[480,128]{1,0:T(8,128)S(1)}, f32[480,128]{1,0:T(8,128)S(1)}, u32[]{:S(2)}, u32[]{:S(2)}) collective-permute-start(f32[480,128]{1,0:T(8,128)S(1)} %get-tuple-element.202), channel_id=1, source_target_pairs={{0,124},{4,8},{8,4},{12,16},{16,12},{20,24},{24,20},{28,32},{32,28... | collective-permute-start | bytes 737288 | tf_op jit(solution)/shard_map/ppermute | solution.py:243
  37.3 1.1 %collective-permute-start.29 = (f32[96,128]{1,0:T(8,128)S(1)}, f32[96,128]{1,0:T(8,128)S(1)}, u32[]{:S(2)}, u32[]{:S(2)}) collective-permute-start(f32[96,128]{1,0:T(8,128)S(1)} %get-tuple-element.203), channel_id=1, source_target_pairs={{0,2},{2,0},{1,3},{3,1},{4,6},{6,4},{5,7},{7,5},{8,10},{10,8},{9,1... | collective-permute-start | bytes 147464 | tf_op jit(solution)/shard_map/ppermute | solution.py:244
  39.1 14.6 %conditional.4 = (f32[3840,128]{1,0:T(8,128)S(1)}, f32[400,128]{1,0:T(8,128)}, f32[400,128]{1,0:T(8,128)}) conditional(s32[]{:T(128)} %bitcast.2, (s32[48]{0:T(128)S(1)}, f32[128,128]{1,0:T(8,128)}, f32[3840,128]{1,0:T(8,128)}, f32[3840,128]{1,0:T(8,128)S(1)}, f32[400,128]{1,0:T(8,128)S(1)}) %tuple.72, (s32[48]{0:T(128)S(1)}, ...), branch_computations={%region_3.0_spmd, %region_4.0_spmd, %region_5.0_spmd} | conditional | flops 20000000 | bytes 7536744 | solution.py:327
  39.1 1.5 %collective-permute-start.16 = (f32[400,128]{1,0:T(8,128)S(1)}, f32[400,128]{1,0:T(8,128)}, u32[]{:S(2)}, u32[]{:S(2)}) collective-permute-start(f32[400,128]{1,0:T(8,128)S(1)} %get-tuple-element.136), channel_id=1, source_target_pairs={{0,1},{1,0},{4,5},{5,4},{8,9},{9,8},{12,13},{13,12},{16,17},{17,16... | collective-permute-start | bytes 614408 | tf_op jit(solution)/shard_map/cond/branch_0_fun/ppermute | solution.py:235
  40.6 5.5 %local1.3 = f32[3840,128]{1,0:T(8,128)S(1)} custom-call(s32[48]{0:T(128)S(1)} %get-tuple-element.132.pml_ref, f32[128,128]{1,0:T(8,128)} %get-tuple-element.133.band_ref, f32[3840,128]{1,0:T(8,128)} %get-tuple-element.134.q_ref, f32[3840,128]{1,0:T(8,128)S(1)} %get-tuple-element.135.refs_0_), custom_call_target="tpu_custom_call" | custom-call | flops 20000000 | bytes 5898240 | tf_op jit(solution)/shard_map/cond/branch_0_fun/local1/pallas_call | solution.py:249
  46.1 7.6 %collective-permute-done.15 = f32[400,128]{1,0:T(8,128)} collective-permute-done((f32[400,128]{1,0:T(8,128)S(1)}, f32[400,128]{1,0:T(8,128)}, u32[]{:S(2)}, u32[]{:S(2)}) %collective-permute-start.15) | collective-permute-done | bytes 204832 | tf_op jit(solution)/shard_map/cond/branch_0_fun/ppermute | solution.py:235
  53.8 1.2 %copy-done.1 = f32[3840,128]{1,0:T(8,128)} copy-done((f32[3840,128]{1,0:T(8,128)}, f32[3840,128]{1,0:T(8,128)S(1)}, u32[]{:S(2)}) %copy-start.1) | copy-done | bytes 1966104
  55.0 3.8 %finish1.1 = (f32[3840,128]{1,0:T(8,128)S(1)}, f32[3840,128]{1,0:T(8,128)S(1)}, f32[480,128]{1,0:T(8,128)S(1)}, f32[480,128]{1,0:T(8,128)S(1)}, f32[96,128]{1,0:T(8,128)S(1)}, /*index=5*/f32[400,128]{1,0:T(8,128)S(1)}) custom-call(s32[3]{0:T(128)S(1)} %copy-done.4, f32[3840,128]{1,0:T(8,128)} %get-tuple-element.196.q_ref, f32[3840,128]{1,0:T(8,128)} %copy-done.1, ...), custom_call_target="tpu_custom_call" | custom-call | tf_op jit(solution)/shard_map/finish1/pallas_call | solution.py:267
  58.9 3.6 %collective-permute-start.31 = (f32[480,128]{1,0:T(8,128)S(1)}, f32[480,128]{1,0:T(8,128)S(1)}, u32[]{:S(2)}, u32[]{:S(2)}) collective-permute-start(f32[480,128]{1,0:T(8,128)S(1)} %get-tuple-element.212), channel_id=1, source_target_pairs={{0,124},{4,8},{8,4},{12,16},{16,12},{20,24},{24,20},{28,32},{32,28... | collective-permute-start | bytes 737288 | tf_op jit(solution)/shard_map/ppermute | solution.py:243
  62.5 1.1 %collective-permute-start.32 = (f32[96,128]{1,0:T(8,128)S(1)}, f32[96,128]{1,0:T(8,128)S(1)}, u32[]{:S(2)}, u32[]{:S(2)}) collective-permute-start(f32[96,128]{1,0:T(8,128)S(1)} %get-tuple-element.213), channel_id=1, source_target_pairs={{0,2},{2,0},{1,3},{3,1},{4,6},{6,4},{5,7},{7,5},{8,10},{10,8},{9,1... | collective-permute-start | bytes 147464 | tf_op jit(solution)/shard_map/ppermute | solution.py:244
  64.2 11.2 %conditional.5 = (f32[3840,128]{1,0:T(8,128)S(1)}, f32[400,128]{1,0:T(8,128)}, f32[400,128]{1,0:T(8,128)}) conditional(s32[]{:T(128)} %bitcast.3, (s32[48]{0:T(128)S(1)}, f32[128,128]{1,0:T(8,128)S(1)}, f32[3840,128]{1,0:T(8,128)S(1)}, f32[3840,128]{1,0:T(8,128)S(1)}, f32[400,128]{1,0:T(8,128)S(1)}) %tuple.75, (s32[48]{0:T(128)S(1)}, ...), branch_computations={%region_6.0_spmd, %region_7.0_spmd, %region_8.0_spmd} | conditional | flops 20000000 | bytes 7536744 | solution.py:327
  64.2 5.2 %collective-permute-start.24 = (f32[400,128]{1,0:T(8,128)S(1)}, f32[400,128]{1,0:T(8,128)}, u32[]{:S(2)}, u32[]{:S(2)}) collective-permute-start(f32[400,128]{1,0:T(8,128)S(1)} %get-tuple-element.156), channel_id=1, source_target_pairs={{0,5},{5,0},{4,9},{9,4},{8,13},{13,8},{12,17},{17,12},{16,21},{21,... | collective-permute-start | bytes 614408 | tf_op jit(solution)/shard_map/cond/branch_1_fun/ppermute | solution.py:235
  69.5 4.4 %local2.4 = f32[3840,128]{1,0:T(8,128)S(1)} custom-call(s32[48]{0:T(128)S(1)} %get-tuple-element.152.pml_ref, f32[128,128]{1,0:T(8,128)S(1)} %get-tuple-element.153.band_ref, f32[3840,128]{1,0:T(8,128)S(1)} %get-tuple-element.154.q_ref, f32[3840,128]{1,0:T(8,128)S(1)} %get-tuple-element.155.refs_0_), custom_call_target="tpu_custom_call" | custom-call | flops 20000000 | bytes 5898240 | tf_op jit(solution)/shard_map/cond/branch_1_fun/local2/pallas_call | solution.py:249
  73.9 1.6 %collective-permute-done.24 = f32[400,128]{1,0:T(8,128)} collective-permute-done((f32[400,128]{1,0:T(8,128)S(1)}, f32[400,128]{1,0:T(8,128)}, u32[]{:S(2)}, u32[]{:S(2)}) %collective-permute-start.24) | collective-permute-done | bytes 204832 | tf_op jit(solution)/shard_map/cond/branch_1_fun/ppermute | solution.py:235
  75.4 3.9 %finish2.1 = (f32[3840,128]{1,0:T(8,128)}, f32[3840,128]{1,0:T(8,128)}) custom-call(s32[3]{0:T(128)S(1)} %copy-done.4, f32[3840,128]{1,0:T(8,128)S(1)} %get-tuple-element.206.q_ref, f32[3840,128]{1,0:T(8,128)S(1)} %get-tuple-element.210.part_ref, f32[480,128]{1,0:T(8,128)S(1)} %collective-permute-done.30.east_ref, ...), custom_call_target="tpu_custom_call" | custom-call | tf_op jit(solution)/shard_map/finish2/pallas_call | solution.py:267
  (26 shorter events, 1.2 us)
Async XLA Ops:
  0.6 3.6 %copy-start.4 = (s32[3]{0:T(128)S(1)}, s32[3]{0:T(128)}, u32[]{:S(2)}) copy-start(s32[3]{0:T(128)} %offsets_ref.5) | copy-start | bytes 40
  0.6 3.6 %copy-start = (f32[5,48,16,128]{3,2,1,0:T(8,128)S(1)}, f32[5,48,16,128]{3,2,1,0:T(8,128)}, u32[]{:S(2)}) copy-start(f32[5,48,16,128]{3,2,1,0:T(8,128)} %param.21) | copy-start | bytes 5898244
  0.6 3.6 %copy-start.3 = (s32[48]{0:T(128)S(1)}, s32[48]{0:T(128)}, u32[]{:S(2)}) copy-start(s32[48]{0:T(128)} %param.23) | copy-start | bytes 580
  4.3 26.3 %collective-permute-start.10 = (f32[480,128]{1,0:T(8,128)S(1)}, f32[480,128]{1,0:T(8,128)S(1)}, u32[]{:S(2)}, u32[]{:S(2)}) collective-permute-start(f32[480,128]{1,0:T(8,128)S(1)} %get-tuple-element.128), channel_id=1, source_target_pairs={{0,4},{4,0},{8,12},{12,8},{16,20},{20,16},{24,28},{28,24},{32,36},... | collective-permute-start | bytes 737288 | tf_op jit(solution)/shard_map/cond/branch_2_fun/ppermute | solution.py:242
  8.1 22.5 %collective-permute-start.11 = (f32[480,128]{1,0:T(8,128)S(1)}, f32[480,128]{1,0:T(8,128)S(1)}, u32[]{:S(2)}, u32[]{:S(2)}) collective-permute-start(f32[480,128]{1,0:T(8,128)S(1)} %get-tuple-element.129), channel_id=1, source_target_pairs={{0,124},{4,8},{8,4},{12,16},{16,12},{20,24},{24,20},{28,32},{32,28... | collective-permute-start | bytes 737288 | tf_op jit(solution)/shard_map/cond/branch_2_fun/ppermute | solution.py:243
  13.9 10.8 %collective-permute-start.14 = (f32[400,128]{1,0:T(8,128)S(1)}, f32[400,128]{1,0:T(8,128)S(1)}, u32[]{:S(2)}, u32[]{:S(2)}) collective-permute-start(f32[400,128]{1,0:T(8,128)S(1)} %get-tuple-element.131), channel_id=1, source_target_pairs={{0,69},{69,0},{4,73},{73,4},{8,77},{77,8},{12,81},{81,12},{16,85},... | collective-permute-start | bytes 614408 | tf_op jit(solution)/shard_map/cond/branch_2_fun/ppermute | solution.py:235
  17.0 13.5 %collective-permute-start.13 = (f32[400,128]{1,0:T(8,128)S(1)}, f32[400,128]{1,0:T(8,128)S(1)}, u32[]{:S(2)}, u32[]{:S(2)}) collective-permute-start(f32[400,128]{1,0:T(8,128)S(1)} %get-tuple-element.131), channel_id=1, source_target_pairs={{0,65},{65,0},{4,69},{69,4},{8,73},{73,8},{12,77},{77,12},{16,81},... | collective-permute-start | bytes 614408 | tf_op jit(solution)/shard_map/cond/branch_2_fun/ppermute | solution.py:235
  17.0 5.3 %collective-permute-start.12 = (f32[96,128]{1,0:T(8,128)S(1)}, f32[96,128]{1,0:T(8,128)S(1)}, u32[]{:S(2)}, u32[]{:S(2)}) collective-permute-start(f32[96,128]{1,0:T(8,128)S(1)} %get-tuple-element.130), channel_id=1, source_target_pairs={{0,2},{2,0},{1,3},{3,1},{4,6},{6,4},{5,7},{7,5},{8,10},{10,8},{9,1... | collective-permute-start | bytes 147464 | tf_op jit(solution)/shard_map/cond/branch_2_fun/ppermute | solution.py:244
  33.7 20.0 %collective-permute-start.27 = (f32[480,128]{1,0:T(8,128)S(1)}, f32[480,128]{1,0:T(8,128)S(1)}, u32[]{:S(2)}, u32[]{:S(2)}) collective-permute-start(f32[480,128]{1,0:T(8,128)S(1)} %get-tuple-element.201), channel_id=1, source_target_pairs={{0,4},{4,0},{8,12},{12,8},{16,20},{20,16},{24,28},{28,24},{32,36},... | collective-permute-start | bytes 737288 | tf_op jit(solution)/shard_map/ppermute | solution.py:242
  34.0 19.8 %collective-permute-start.28 = (f32[480,128]{1,0:T(8,128)S(1)}, f32[480,128]{1,0:T(8,128)S(1)}, u32[]{:S(2)}, u32[]{:S(2)}) collective-permute-start(f32[480,128]{1,0:T(8,128)S(1)} %get-tuple-element.202), channel_id=1, source_target_pairs={{0,124},{4,8},{8,4},{12,16},{16,12},{20,24},{24,20},{28,32},{32,28... | collective-permute-start | bytes 737288 | tf_op jit(solution)/shard_map/ppermute | solution.py:243
  37.3 16.4 %collective-permute-start.29 = (f32[96,128]{1,0:T(8,128)S(1)}, f32[96,128]{1,0:T(8,128)S(1)}, u32[]{:S(2)}, u32[]{:S(2)}) collective-permute-start(f32[96,128]{1,0:T(8,128)S(1)} %get-tuple-element.203), channel_id=1, source_target_pairs={{0,2},{2,0},{1,3},{3,1},{4,6},{6,4},{5,7},{7,5},{8,10},{10,8},{9,1... | collective-permute-start | bytes 147464 | tf_op jit(solution)/shard_map/ppermute | solution.py:244
  39.1 7.0 %collective-permute-start.16 = (f32[400,128]{1,0:T(8,128)S(1)}, f32[400,128]{1,0:T(8,128)}, u32[]{:S(2)}, u32[]{:S(2)}) collective-permute-start(f32[400,128]{1,0:T(8,128)S(1)} %get-tuple-element.136), channel_id=1, source_target_pairs={{0,1},{1,0},{4,5},{5,4},{8,9},{9,8},{12,13},{13,12},{16,17},{17,16... | collective-permute-start | bytes 614408 | tf_op jit(solution)/shard_map/cond/branch_0_fun/ppermute | solution.py:235
  40.6 13.1 %collective-permute-start.15 = (f32[400,128]{1,0:T(8,128)S(1)}, f32[400,128]{1,0:T(8,128)}, u32[]{:S(2)}, u32[]{:S(2)}) collective-permute-start(f32[400,128]{1,0:T(8,128)S(1)} %get-tuple-element.136), channel_id=1, source_target_pairs={{0,125},{125,0},{4,1},{1,4},{8,5},{5,8},{12,9},{9,12},{16,13},{13,... | collective-permute-start | bytes 614408 | tf_op jit(solution)/shard_map/cond/branch_0_fun/ppermute | solution.py:235
  53.7 1.3 %copy-start.1 = (f32[3840,128]{1,0:T(8,128)}, f32[3840,128]{1,0:T(8,128)S(1)}, u32[]{:S(2)}) copy-start(f32[3840,128]{1,0:T(8,128)S(1)} %get-tuple-element.200.part_ref) | copy-start | bytes 5898244
  55.0 9.2 %copy-start.2 = (f32[128,128]{1,0:T(8,128)S(1)}, f32[128,128]{1,0:T(8,128)}, u32[]{:S(2)}) copy-start(f32[128,128]{1,0:T(8,128)} %constant.12.clone) | copy-start | bytes 196612
  58.8 16.7 %collective-permute-start.30 = (f32[480,128]{1,0:T(8,128)S(1)}, f32[480,128]{1,0:T(8,128)S(1)}, u32[]{:S(2)}, u32[]{:S(2)}) collective-permute-start(f32[480,128]{1,0:T(8,128)S(1)} %get-tuple-element.211), channel_id=1, source_target_pairs={{0,4},{4,0},{8,12},{12,8},{16,20},{20,16},{24,28},{28,24},{32,36},... | collective-permute-start | bytes 737288 | tf_op jit(solution)/shard_map/ppermute | solution.py:242
  58.9 16.6 %collective-permute-start.31 = (f32[480,128]{1,0:T(8,128)S(1)}, f32[480,128]{1,0:T(8,128)S(1)}, u32[]{:S(2)}, u32[]{:S(2)}) collective-permute-start(f32[480,128]{1,0:T(8,128)S(1)} %get-tuple-element.212), channel_id=1, source_target_pairs={{0,124},{4,8},{8,4},{12,16},{16,12},{20,24},{24,20},{28,32},{32,28... | collective-permute-start | bytes 737288 | tf_op jit(solution)/shard_map/ppermute | solution.py:243
  62.5 13.0 %collective-permute-start.32 = (f32[96,128]{1,0:T(8,128)S(1)}, f32[96,128]{1,0:T(8,128)S(1)}, u32[]{:S(2)}, u32[]{:S(2)}) collective-permute-start(f32[96,128]{1,0:T(8,128)S(1)} %get-tuple-element.213), channel_id=1, source_target_pairs={{0,2},{2,0},{1,3},{3,1},{4,6},{6,4},{5,7},{7,5},{8,10},{10,8},{9,1... | collective-permute-start | bytes 147464 | tf_op jit(solution)/shard_map/ppermute | solution.py:244
  64.2 11.2 %collective-permute-start.24 = (f32[400,128]{1,0:T(8,128)S(1)}, f32[400,128]{1,0:T(8,128)}, u32[]{:S(2)}, u32[]{:S(2)}) collective-permute-start(f32[400,128]{1,0:T(8,128)S(1)} %get-tuple-element.156), channel_id=1, source_target_pairs={{0,5},{5,0},{4,9},{9,4},{8,13},{13,8},{12,17},{17,12},{16,21},{21,... | collective-permute-start | bytes 614408 | tf_op jit(solution)/shard_map/cond/branch_1_fun/ppermute | solution.py:235
  69.5 6.0 %collective-permute-start.23 = (f32[400,128]{1,0:T(8,128)S(1)}, f32[400,128]{1,0:T(8,128)}, u32[]{:S(2)}, u32[]{:S(2)}) collective-permute-start(f32[400,128]{1,0:T(8,128)S(1)} %get-tuple-element.156), channel_id=1, source_target_pairs={{0,1},{1,0},{4,5},{5,4},{8,9},{9,8},{12,13},{13,12},{16,17},{17,16... | collective-permute-start | bytes 614408 | tf_op jit(solution)/shard_map/cond/branch_1_fun/ppermute | solution.py:235

commit v2 on v1

v2 whole, which is shorter than its diff:
```python
import functools

import jax
import jax.numpy as jnp
import numpy as np
from jax import lax
from jax.experimental import pallas as pl
from jax.experimental.pallas import tpu as pltpu
from jax.sharding import PartitionSpec as P

SECTIONS = 3
F, A, C, L = 5, 48, 16, 128
ROWS = F * A * C
FIELD = A * C
W = 5
GROUP = 6 * C
PARAMS = pltpu.CompilerParams(vmem_limit_bytes=24 << 20)

coeffs = (0.872756993962, -0.286511173973, 0.09032000128, -0.020779405824, 0.002484594688)
mach = 0.3
step_size = 0.25
damping = 0.8
section_a = (0.0, -5.0 / 9.0, -153.0 / 128.0)
section_b = (1.0 / 3.0, 15.0 / 16.0, 8.0 / 15.0)
HI = lax.Precision.HIGHEST


def band_matrix():
    band = np.zeros((L, L), np.float32)
    for k, c in enumerate(coeffs, start=1):
        band += c * (np.eye(L, k=-k) - np.eye(L, k=k)).astype(np.float32)
    return band


def rows_of(f, a):
    return pl.ds(pl.multiple_of(f * FIELD + a * C, C), C)


def total_of(terms):
    total = terms[0]
    for term in terms[1:]:
        total = total + term
    return total


def cells_of(ref, f, first):
    return [ref[pl.ds(f * FIELD + first + c, A, stride=C), :] for c in range(W)]


def contributions(cells, upward):
    added = []
    for i in range(W):
        onward = total_of([-coeffs[i + W - c - 1] * cells[c] for c in range(i, W)])
        back = total_of([coeffs[c + W - i - 1] * cells[c] for c in range(i + 1)])
        added.append(jnp.where(upward, onward, back))
    return added


def is_even():
    return lax.rem(lax.axis_index("circ"), 2) == 0


def sides():
    even = is_even()
    return (jnp.where(even, C - W, 0), even), (jnp.where(even, 0, C - W), jnp.logical_not(even))


def pack_rims(q_ref, east_ref, odd_ref):
    for out_ref, (first, upward) in zip((east_ref, odd_ref), sides()):
        for g, f in enumerate((2, 4)):
            for i, added in enumerate(contributions(cells_of(q_ref, f, first), upward)):
                out_ref[(g * W + i) * A : (g * W + i + 1) * A, :] = added


def pack_rad(q_ref, rad_ref):
    low_rad = lax.axis_index("rad") == 0
    lane = lax.broadcasted_iota(jnp.int32, (GROUP, L), 1)
    first = jnp.where(low_rad, W, 0)
    rims = jnp.zeros((GROUP, L), jnp.float32)
    for n in range(2 * FIELD // GROUP):
        x = q_ref[3 * FIELD + n * GROUP : 3 * FIELD + (n + 1) * GROUP, :]
        rims = jnp.where((lane >= 8 * n) & (lane < 8 * n + W), pltpu.roll(x, first + 8 * n, 1), rims)
    slot = lax.rem(lane, 8)
    onward, back = [], []
    for d in range(W):
        c = coeffs[W - 1 - d]
        onward.append(jnp.where(slot + d < W, -c, 0.0) * (pltpu.roll(rims, L - d, 1) if d else rims))
        back.append(jnp.where((slot >= d) & (slot < W), c, 0.0) * (pltpu.roll(rims, d, 1) if d else rims))
    rad_ref[...] = jnp.where(low_rad, total_of(onward), total_of(back))


def interface_planes():
    rotor = lax.axis_index("half") == 0
    return [jnp.where(rotor, A - 1 - m, m) for m in range(W)]


def pack_faces(q_ref, face_ref):
    for f in range(F):
        for m, a in enumerate(interface_planes()):
            row = (f * W + m) * C
            face_ref[row : row + C, :] = q_ref[rows_of(f, a), :]


RIM = jax.ShapeDtypeStruct((2 * W * A, L), jnp.float32)
RIMS = jax.ShapeDtypeStruct((4 * W * A, L), jnp.float32)
RAD = jax.ShapeDtypeStruct((GROUP, L), jnp.float32)
FACE = jax.ShapeDtypeStruct((F * W * C, L), jnp.float32)
FIELDS = jax.ShapeDtypeStruct((ROWS, L), jnp.float32)
VM = pl.BlockSpec(memory_space=pltpu.VMEM)
SM = pl.BlockSpec(memory_space=pltpu.SMEM)
ANY = pl.BlockSpec(memory_space=pl.ANY)


def local_kernel(section, pml_ref, band_ref, q_ref, *refs):
    inc_ref = refs[0] if section else None
    *outs, pad = refs[1:] if section else refs
    out_ref = outs[0]
    zero = jnp.zeros((W * C, L), jnp.float32)
    span = (A + 2 * W) * C
    for f in range(F):
        pad[f * span : f * span + W * C, :] = zero
        pad[f * span + W * C : f * span + W * C + FIELD, :] = q_ref[f * FIELD : (f + 1) * FIELD, :]
        pad[(f + 1) * span - W * C : (f + 1) * span, :] = zero
    cell = lax.broadcasted_iota(jnp.int32, (C, L), 0)
    up = [jnp.where(cell < C - k, c, 0.0) for k, c in enumerate(coeffs, start=1)]
    down = [jnp.where(cell >= k, c, 0.0) for k, c in enumerate(coeffs, start=1)]

    def circ(x):
        total = None
        for k in range(1, W + 1):
            term = up[k - 1] * pltpu.roll(x, C - k, 0) - down[k - 1] * pltpu.roll(x, k, 0)
            total = term if total is None else total + term
        return total

    B = 4

    def step(n, carry):
        a0 = n * B
        axial = []
        here = []
        for f in range(F):
            planes = [
                pad[pl.ds(pl.multiple_of(f * span + (a0 + d) * C, C), C), :] for d in range(B + 2 * W)
            ]
            here.append(planes[W : W + B])
            axial.append(
                [
                    sum(c * (planes[W + p + k] - planes[W + p - k]) for k, c in enumerate(coeffs, start=1))
                    for p in range(B)
                ]
            )
        radial = jnp.dot(
            jnp.concatenate(here[3] + here[4], axis=0),
            band_ref[...],
            precision=HI,
            preferred_element_type=jnp.float32,
        )
        for p in range(B):
            rad3 = radial[p * C : (p + 1) * C]
            rad4 = radial[(B + p) * C : (B + p + 1) * C]
            div = axial[1][p] + circ(here[2][p]) + rad3
            rates = [
                mach * axial[0][p] + div,
                mach * axial[1][p] + axial[4][p],
                mach * axial[2][p] + circ(here[4][p]),
                mach * axial[3][p] + rad4,
                mach * axial[4][p] + div,
            ]
            sigma = damping * pml_ref[a0 + p].astype(jnp.float32)
            for f in range(F):
                rows = rows_of(f, a0 + p)
                value = -step_size * (rates[f] + sigma * here[f][p])
                if section:
                    value = value + section_a[section] * inc_ref[rows, :]
                out_ref[rows, :] = value
        return carry

    lax.fori_loop(0, A // B, step, 0)
    if len(outs) > 1:
        for side, (first, _) in enumerate(sides()):
            for g, f in enumerate((2, 4)):
                for c, (now, part) in enumerate(zip(cells_of(q_ref, f, first), cells_of(out_ref, f, first))):
                    row = ((2 * side + g) * W + c) * A
                    outs[1][row : row + A, :] = now + section_b[section] * part
        for f in range(F):
            for m, a in enumerate(interface_planes()):
                row = (f * W + m) * C
                rows = rows_of(f, a)
                outs[2][row : row + C, :] = q_ref[rows, :] + section_b[section] * out_ref[rows, :]


def rim_rows(rad_ref, g, n):
    low_rad = lax.axis_index("rad") == 0
    lane = lax.broadcasted_iota(jnp.int32, (GROUP, L), 1)
    inside = (lane >= jnp.where(low_rad, L - W, 0)) & (lane < jnp.where(low_rad, L, W))
    base = jnp.where(low_rad, L - W, 0)
    turn = lax.rem(base + L - 8 * (n + g * (FIELD // GROUP)), L)
    return jnp.where(inside, pltpu.roll(rad_ref[...], turn, 1), 0.0)


def interface_terms(section, offsets_ref, own_ref, next_ref, faces, fields):
    rotor = lax.axis_index("half") == 0
    for f in fields:
        for n in range(f * W, f * W + W):
            own, beyond = own_ref[n * C : (n + 1) * C, :], next_ref[n * C : (n + 1) * C, :]
            faces[2 * n * C : (2 * n + 1) * C, :] = jnp.where(rotor, own, beyond)
            faces[(2 * n + 1) * C : (2 * n + 2) * C, :] = jnp.where(rotor, beyond, own)
    shift = lax.rem(offsets_ref[section], C)
    start = jnp.where(rotor, shift, C - shift)
    sign = jnp.where(rotor, 1.0, -1.0)
    ghost = {f: [faces[pl.ds(2 * (f * W + m) * C + start, C), :] for m in range(W)] for f in fields}
    planes = []
    for i in range(W):
        axial = {
            f: sign * total_of([coeffs[k - 1] * ghost[f][k - 1 - i] for k in range(i + 1, W + 1)]) for f in fields
        }
        extra = {f: mach * axial[f] for f in fields}
        for f, other in ((0, 1), (1, 4), (4, 1)):
            if f in fields:
                extra[f] = extra[f] + axial[other]
        planes.append((jnp.where(rotor, A - 1 - i, i), extra))
    return planes


def circ_reader(low, high, east_ref, odd_ref):
    even = is_even()

    inside = slice(3 * A, 3 * A + 2 * W * A)
    low[inside, :] = jnp.where(even, odd_ref[...], east_ref[...])
    high[inside, :] = jnp.where(even, east_ref[...], odd_ref[...])
    sub = lax.broadcasted_iota(jnp.int32, (8, L), 0)

    def circ(a, g):
        lower = low[pl.ds((3 + g * W) * A + a, 8, stride=A), :]
        upper = high[pl.ds(g * W * A + a, 8, stride=A), :]
        return jnp.concatenate([jnp.where(sub < W, lower, 0.0), jnp.where(sub >= 8 - W, upper, 0.0)], axis=0)

    return circ


def lead_kernel(
    section, offsets_ref, rim_ref, face_ref, east_ref, odd_ref, rad_ref, own_ref, next_ref, *refs
):
    to_east, to_odd, to_face, extra2, extra4, faces, low, high, rim4 = refs
    rotor = lax.axis_index("half") == 0
    circ = circ_reader(low, high, east_ref, odd_ref)
    rim4[...] = rim_rows(rad_ref, 1, jnp.where(rotor, FIELD // GROUP - 1, 0))
    scale = step_size * section_b[section]
    extra2[...] = jnp.zeros_like(extra2)
    for n in range(FIELD // GROUP):
        extra4[n * GROUP : (n + 1) * GROUP, :] = rim_rows(rad_ref, 0, n)
    for m, (a, extra) in enumerate(interface_terms(section, offsets_ref, own_ref, next_ref, faces, range(F))):
        rows = rows_of(0, a)
        rim3 = extra4[rows, :]
        beside = rim4[pl.ds(pl.multiple_of(jnp.where(rotor, GROUP // C - 1 - m, m) * C, C), C), :]
        div = circ(a, 0) + rim3
        deltas = [div + extra[0], extra[1], circ(a, 1) + extra[2], beside + extra[3], div + extra[4]]
        for f in range(F):
            row = (f * W + m) * C
            to_face[row : row + C, :] = face_ref[row : row + C, :] - scale * deltas[f]
        extra2[rows, :] += extra[2]
        extra4[rows, :] = rim3 + extra[4]
    for side, (first, upward) in enumerate(sides()):
        from_ref, out_ref = ((east_ref, to_east), (odd_ref, to_odd))[side]
        for g, beside in enumerate((extra2, extra4)):
            cells = []
            for c, other in enumerate(cells_of(beside, 0, first)):
                row = ((2 * side + g) * W + c) * A
                arrived = from_ref[((1 - g) * W + c) * A : ((1 - g) * W + c + 1) * A, :]
                cells.append(rim_ref[row : row + A, :] - scale * (arrived + other))
            for i, added in enumerate(contributions(cells, upward)):
                out_ref[(g * W + i) * A : (g * W + i + 1) * A, :] = added


def finish_kernel(
    section, last, offsets_ref, q_ref, part_ref, east_ref, odd_ref, rad_ref, own_ref, next_ref, *refs
):
    b = section_b[section]
    new_ref, inc_ref, *messages, low, high, faces = refs
    circ = circ_reader(low, high, east_ref, odd_ref)

    def step(n, carry):
        rims = [rim_rows(rad_ref, g, n) for g in range(2)]
        for p in range(GROUP // C):
            a = n * (GROUP // C) + p
            div = circ(a, 0) + rims[0][p * C : (p + 1) * C]
            extra = [div, None, circ(a, 1), rims[1][p * C : (p + 1) * C], div]
            for f in range(F):
                rows = rows_of(f, a)
                value = part_ref[rows, :]
                if extra[f] is not None:
                    value = value - step_size * extra[f]
                inc_ref[rows, :] = value
                new_ref[rows, :] = q_ref[rows, :] + b * value
        return carry

    lax.fori_loop(0, FIELD // GROUP, step, 0)

    for a, extra in interface_terms(section, offsets_ref, own_ref, next_ref, faces, range(F)):
        for f in range(F):
            rows = rows_of(f, a)
            delta = -step_size * extra[f]
            inc_ref[rows, :] += delta
            new_ref[rows, :] += b * delta
    if not last:
        pack_rad(new_ref, messages[0])


def swap_faces(face, blocks):
    count = lax.axis_size("circ")
    pairs = []
    for i in range(count):
        j = (i + blocks) % count
        pairs += [(2 * i, 2 * j + 1), (2 * j + 1, 2 * i)]
    return lax.ppermute(face, ("circ", "half"), pairs)


def send_east(east):
    return lax.ppermute(east, "circ", [(i, i ^ 1) for i in range(lax.axis_size("circ"))])


def send_odd(odd):
    count = lax.axis_size("circ")
    return lax.ppermute(odd, "circ", [(i, (i + (1 if i % 2 else -1)) % count) for i in range(count)])


def local_terms(section, q, inc, pml_zone):
    known = [] if section == SECTIONS - 1 else [RIMS, FACE]
    return pl.pallas_call(
        functools.partial(local_kernel, section),
        out_shape=[FIELDS] + known,
        in_specs=[SM] + [VM] * (3 if section else 2),
        out_specs=[VM] * (1 + len(known)),
        scratch_shapes=[pltpu.VMEM((F * (A + 2 * W) * C, L), jnp.float32)],
        compiler_params=PARAMS,
        cost_estimate=pl.CostEstimate(flops=20_000_000, bytes_accessed=3 * ROWS * L * 4, transcendentals=0),
        name=f"local{section}",
    )(pml_zone, band_matrix(), q, *([inc] if section else []))


def first_branch(blocks, q, pml_zone, face):
    own, beyond = swap_faces(face, blocks), swap_faces(face, blocks + 1)
    return local_terms(0, q, (), pml_zone), own, beyond


def section_branch(section, blocks, offsets, q, part, arrived, pml_zone, face):
    own, beyond = swap_faces(face, blocks), swap_faces(face, blocks + 1)
    q, inc, rad = finish(section - 1, offsets, q, part, arrived)
    return q, local_terms(section, q, inc, pml_zone), send_rad(rad), own, beyond


def send_rad(rad):
    return lax.ppermute(rad, "rad", [(0, 1), (1, 0)])


def lead(section, offsets, known, arrived):
    window = pltpu.VMEM((16 * A, L), jnp.float32)
    field = pltpu.VMEM((FIELD, L), jnp.float32)
    return pl.pallas_call(
        functools.partial(lead_kernel, section),
        out_shape=[RIM, RIM, FACE],
        in_specs=[SM] + [VM] * 7,
        out_specs=[VM] * 3,
        scratch_shapes=[field, field, pltpu.VMEM((2 * F * W * C, L), jnp.float32), window, window]
        + [pltpu.VMEM((GROUP, L), jnp.float32)],
        compiler_params=PARAMS,
        name=f"lead{section}",
    )(offsets, *known, *arrived)


def finish(section, offsets, q, part, arrived):
    last = section == SECTIONS - 1
    window = pltpu.VMEM((16 * A, L), jnp.float32)
    return pl.pallas_call(
        functools.partial(finish_kernel, section, last),
        out_shape=[FIELDS, FIELDS] + ([] if last else [RAD]),
        in_specs=[SM] + [VM] * 7,
        out_specs=[VM] * (2 if last else 3),
        scratch_shapes=[window, window, pltpu.VMEM((2 * F * W * C, L), jnp.float32)],
        compiler_params=PARAMS,
        cost_estimate=pl.CostEstimate(flops=8_000_000, bytes_accessed=4 * ROWS * L * 4, transcendentals=0),
        name=f"finish{section}",
    )(offsets, q, part, *arrived)


def enter_lead_kernel(offsets_ref, state_ref, east_ref, odd_ref, kind0, kind1, kind2, q_ref, sems):
    copies = []
    for n, f in enumerate((2, 4)):
        rows = pl.ds(f * FIELD, FIELD)
        copies.append(pltpu.make_async_copy(state_ref.at[rows], q_ref.at[rows], sems.at[n]))
    for copy in copies:
        copy.start()
    for section, kind in enumerate((kind0, kind1, kind2)):
        place = lax.div(offsets_ref[section], C)
        kind[0] = jnp.where(place == 0, 1, jnp.where(place == C, 2, 0))
    for copy in copies:
        copy.wait()
    pack_rims(q_ref, east_ref, odd_ref)


def enter_kernel(state_ref, sent_ref, *refs):
    *messages, q_ref, sems = refs
    copies = []
    for n, f in enumerate((3, 4)):
        rows = pl.ds(f * FIELD, FIELD)
        copies.append(pltpu.make_async_copy(state_ref.at[rows], q_ref.at[rows], sems.at[n]))
    edge = jnp.where(lax.axis_index("half") == 0, (A - W) * C, 0)
    for f in (0, 1, 2):
        rows = pl.ds(pl.multiple_of(f * FIELD + edge, C), W * C)
        copies.append(pltpu.make_async_copy(state_ref.at[rows], q_ref.at[rows], sems.at[2 + f]))
    for copy in copies:
        copy.start()
    for copy in copies:
        copy.wait()
    pack_rad(q_ref, messages[0])
    pack_faces(q_ref, messages[1])


def body(state, offsets, pml_zone):
    q = state.reshape(ROWS, L)
    held = pltpu.with_memory_space_constraint(q, pltpu.HBM)
    flag = jax.ShapeDtypeStruct((1,), jnp.int32)
    east, odd, *kinds = pl.pallas_call(
        enter_lead_kernel,
        out_shape=[RIM, RIM] + [flag] * SECTIONS,
        in_specs=[SM, pl.BlockSpec(memory_space=pltpu.HBM)],
        out_specs=[VM, VM] + [SM] * SECTIONS,
        scratch_shapes=[pltpu.VMEM((ROWS, L), jnp.float32), pltpu.SemaphoreType.DMA((2,))],
        compiler_params=PARAMS,
        name="enter_lead",
    )(offsets, held)
    rad, face = pl.pallas_call(
        enter_kernel,
        out_shape=[RAD, FACE],
        in_specs=[pl.BlockSpec(memory_space=pltpu.HBM), ANY],
        out_specs=[VM] * 2,
        scratch_shapes=[pltpu.VMEM((ROWS, L), jnp.float32), pltpu.SemaphoreType.DMA((W,))],
        compiler_params=PARAMS,
        cost_estimate=pl.CostEstimate(flops=8_000_000, bytes_accessed=4 * ROWS * L * 4, transcendentals=0),
        name="enter",
    )(held, east)
    shifts = (-1, 0, C)
    for section in range(SECTIONS):
        from_east, from_odd = send_east(east), send_odd(odd)
        if section == 0:
            from_rad = send_rad(rad)
            (part, *known), own, beyond = lax.switch(
                kinds[0][0], [functools.partial(first_branch, blocks) for blocks in shifts], q, pml_zone, face
            )
        else:
            q, (part, *known), from_rad, own, beyond = lax.switch(
                kinds[section][0],
                [functools.partial(section_branch, section, blocks) for blocks in shifts],
                offsets,
                q,
                part,
                arrived,
                pml_zone,
                face,
            )
        arrived = (from_east, from_odd, from_rad, own, beyond)
        if known:
            east, odd, face = lead(section, offsets, known, arrived)
    q, inc = finish(SECTIONS - 1, offsets, q, part, arrived)
    return q.reshape(state.shape), inc.reshape(state.shape)


def solution(mesh):
    return jax.shard_map(
        body,
        mesh=mesh,
        in_specs=(P(None, "half", "circ", "rad"), P(), P("half")),
        out_specs=(P(None, "half", "circ", "rad"), P(None, "half", "circ", "rad")),
        check_vma=False,
    )
```

time: 80.9 us -> 80.5 us (level)
  the two profiles are of different devices: /device:TPU:1 before, /device:TPU:0 now
where the time goes in v2:
time: 80.5 us; the launch traced here: 79.4 us
  Pallas kernels  37.8 us (47%)
  starting transfers between devices  36.8 us (46%)
  between operations  2.58 us (3%)
  waiting for transfers between devices  2.03 us (3%)
    pallas_call x3, Pallas kernels, local_terms(): pl.pallas_call(functools.partial(local_kernel, section), out_shape=[FIELD...  17.1 us
    ppermute x3, starting transfers between devices, send_odd(): lax.ppermute(odd, 'circ', [(i, (i + (1 if i % 2 else -1)) % count) for i...  15.7 us
    ppermute x6, starting transfers between devices, swap_faces(): return lax.ppermute(face, ('circ', 'half'), pairs)  14.9 us
    pallas_call x3, Pallas kernels, finish(): pl.pallas_call(functools.partial(finish_kernel, section, last), out_shape...  12.9 us
    ppermute x3, starting transfers between devices, send_east(): lax.ppermute(east, 'circ', [(i, i ^ 1) for i in range(lax.axis_size('circ...  4.3 us
    pallas_call x2, Pallas kernels, lead(): pl.pallas_call(functools.partial(lead_kernel, section), out_shape=[RIM, R...  3.51 us
    pallas_call x1, Pallas kernels, body(): pl.pallas_call(enter_lead_kernel, out_shape=[RIM, RIM] + [flag] * SECTION...  2.72 us
    ppermute x6, waiting for transfers between devices, swap_faces(): return lax.ppermute(face, ('circ', 'half'), pairs)  2.01 us
  transfers between devices with their start and end apart: 15, of which 2 were waited for; matrix products, arithmetic and copies ran while one was open for 0% of the time, Pallas kernels for 34%

profile of v2, /device:TPU:0, one launch (start us, length us, event | category | flops | bytes accessed | tf_op | source)
XLA Modules:
  0.0 79.4 jit_solution(16063152469526764015)
XLA Ops:
  0.7 2.7 %enter_lead.1 = (f32[480,128]{1,0:T(8,128)S(1)}, f32[480,128]{1,0:T(8,128)S(1)}, s32[1]{0:T(128)}, s32[1]{0:T(128)}, s32[1]{0:T(128)}) custom-call(s32[3]{0:T(128)} %offsets_ref.7, f32[3840,128]{1,0:T(8,128)} %bitcast.6), custom_call_target="tpu_custom_call" | custom-call | tf_op jit(solution)/shard_map/enter_lead/pallas_call | solution.py:423
  3.4 9.0 %collective-permute-start.25 = (f32[480,128]{1,0:T(8,128)S(1)}, f32[480,128]{1,0:T(8,128)S(1)}, u32[]{:S(2)}, u32[]{:S(2)}) collective-permute-start(f32[480,128]{1,0:T(8,128)S(1)} %get-tuple-element.310), channel_id=1, source_target_pairs={{0,124},{4,8},{8,4},{12,16},{16,12},{20,24},{24,20},{28,32},{32,28... | collective-permute-start | bytes 737288 | tf_op jit(solution)/shard_map/ppermute | solution.py:324
  12.4 1.6 %enter.1 = (f32[96,128]{1,0:T(8,128)S(1)}, f32[400,128]{1,0:T(8,128)S(1)}) custom-call(f32[3840,128]{1,0:T(8,128)} %bitcast.7, f32[480,128]{1,0:T(8,128)S(1)} %get-tuple-element.307.sent_ref), custom_call_target="tpu_custom_call" | custom-call | flops 8000000 | bytes 7864320 | tf_op jit(solution)/shard_map/enter/pallas_call | solution.py:432
  14.0 0.8 collective-permute-start.26
  15.5 11.6 %conditional.3 = (f32[3840,128]{1,0:T(8,128)}, f32[960,128]{1,0:T(8,128)S(1)}, f32[400,128]{1,0:T(8,128)}, f32[400,128]{1,0:T(8,128)}, f32[400,128]{1,0:T(8,128)}) conditional(s32[]{:T(128)} %bitcast.3, (s32[48]{0:T(128)S(1)}, f32[128,128]{1,0:T(8,128)S(1)}, f32[3840,128]{1,0:T(8,128)S(1)}, f32[400,128]{1,0:T(8,128)S(1)}) %tuple.78, ...), branch_computations={%region_0.0_spmd, %region_1.0_spmd, %region_2.0_spmd} | conditional | flops 20000000 | bytes 7536760 | solution.py:447
  15.5 2.8 %collective-permute-start.3 = (f32[400,128]{1,0:T(8,128)S(1)}, f32[400,128]{1,0:T(8,128)}, u32[]{:S(2)}, u32[]{:S(2)}) collective-permute-start(f32[400,128]{1,0:T(8,128)S(1)} %get-tuple-element.169), channel_id=1, source_target_pairs={{0,5},{5,0},{4,9},{9,4},{8,13},{13,8},{12,17},{17,12},{16,21},{21,... | collective-permute-start | bytes 614408 | tf_op jit(solution)/shard_map/cond/branch_1_fun/ppermute | solution.py:315
  18.3 1.8 %collective-permute-start.2 = (f32[400,128]{1,0:T(8,128)S(1)}, f32[400,128]{1,0:T(8,128)}, u32[]{:S(2)}, u32[]{:S(2)}) collective-permute-start(f32[400,128]{1,0:T(8,128)S(1)} %get-tuple-element.169), channel_id=1, source_target_pairs={{0,1},{1,0},{4,5},{5,4},{8,9},{9,8},{12,13},{13,12},{16,17},{17,16... | collective-permute-start | bytes 614408 | tf_op jit(solution)/shard_map/cond/branch_1_fun/ppermute | solution.py:315
  20.1 5.9 %local0.4 = (f32[3840,128]{1,0:T(8,128)}, f32[960,128]{1,0:T(8,128)S(1)}, f32[400,128]{1,0:T(8,128)}) custom-call(s32[48]{0:T(128)S(1)} %get-tuple-element.163.pml_ref, f32[128,128]{1,0:T(8,128)S(1)} %get-tuple-element.164.band_ref, f32[3840,128]{1,0:T(8,128)S(1)} %get-tuple-element.165.q_ref), custom_call_target="tpu_custom_call" | custom-call | flops 20000000 | bytes 5898240 | tf_op jit(solution)/shard_map/cond/branch_1_fun/local0/pallas_call | solution.py:329
  26.0 1.0 %collective-permute-done.3 = f32[400,128]{1,0:T(8,128)} collective-permute-done((f32[400,128]{1,0:T(8,128)S(1)}, f32[400,128]{1,0:T(8,128)}, u32[]{:S(2)}, u32[]{:S(2)}) %collective-permute-start.3) | collective-permute-done | bytes 204832 | tf_op jit(solution)/shard_map/cond/branch_1_fun/ppermute | solution.py:315
  27.1 1.8 %lead0.1 = (f32[480,128]{1,0:T(8,128)S(1)}, f32[480,128]{1,0:T(8,128)S(1)}, f32[400,128]{1,0:T(8,128)S(1)}) custom-call(s32[3]{0:T(128)} %offsets_ref.7, f32[960,128]{1,0:T(8,128)S(1)} %get-tuple-element.314.rim_ref, f32[400,128]{1,0:T(8,128)} %get-tuple-element.315.face_ref, f32[480,128]{1,0:T(8,128)S(1)} %collective-permute-done.24.east_ref, ...), custom_call_target="tpu_custom_call" | custom-call | tf_op jit(solution)/shard_map/lead0/pallas_call | solution.py:359
  29.4 6.2 %collective-permute-start.28 = (f32[480,128]{1,0:T(8,128)S(1)}, f32[480,128]{1,0:T(8,128)S(1)}, u32[]{:S(2)}, u32[]{:S(2)}) collective-permute-start(f32[480,128]{1,0:T(8,128)S(1)} %get-tuple-element.320), channel_id=1, source_target_pairs={{0,124},{4,8},{8,4},{12,16},{16,12},{20,24},{24,20},{28,32},{32,28... | collective-permute-start | bytes 737288 | tf_op jit(solution)/shard_map/ppermute | solution.py:324
  36.2 15.0 %conditional.4 = (f32[3840,128]{1,0:T(8,128)}, f32[3840,128]{1,0:T(8,128)S(1)}, f32[960,128]{1,0:T(8,128)S(1)}, f32[400,128]{1,0:T(8,128)S(1)}, f32[96,128]{1,0:...) conditional(s32[]{:T(128)} %bitcast.2, (s32[3]{0:T(128)}, f32[3840,128]{1,0:T(8,128)S(1)}, ...), branch_computations={%region_3.0_spmd, %region_4.0_spmd, %region_5.0_spmd} | conditional | flops 28000000 | bytes 16581608 | solution.py:451
  36.9 2.2 %collective-permute-start.13 = (f32[400,128]{1,0:T(8,128)S(1)}, f32[400,128]{1,0:T(8,128)}, u32[]{:S(2)}, u32[]{:S(2)}) collective-permute-start(f32[400,128]{1,0:T(8,128)S(1)} %get-tuple-element.227), channel_id=1, source_target_pairs={{0,65},{65,0},{4,69},{69,4},{8,73},{73,8},{12,77},{77,12},{16,81},... | collective-permute-start | bytes 614408 | tf_op jit(solution)/shard_map/cond/branch_2_fun/ppermute | solution.py:315
  39.1 4.2 %finish0.5 = (f32[3840,128]{1,0:T(8,128)}, f32[3840,128]{1,0:T(8,128)S(1)}, f32[96,128]{1,0:T(8,128)S(1)}) custom-call(s32[3]{0:T(128)} %get-tuple-element.211.offsets_ref, f32[3840,128]{1,0:T(8,128)S(1)} %get-tuple-element.212.q_ref, f32[3840,128]{1,0:T(8,128)} %get-tuple-element.213.part_ref, f32[480,128]{1,0:T(8,128)} %copy-done.4, ...), custom_call_target="tpu_custom_call" | custom-call | flops 8000000 | bytes 7864320 | tf_op jit(solution)/shard_map/cond/branch_2_fun/finish0/pallas_call | solution.py:374
  43.2 1.2 %collective-permute-start.12 = (f32[96,128]{1,0:T(8,128)S(1)}, f32[96,128]{1,0:T(8,128)}, u32[]{:S(2)}, u32[]{:S(2)}) collective-permute-start(f32[96,128]{1,0:T(8,128)S(1)} %get-tuple-element.226), channel_id=1, source_target_pairs={{0,2},{2,0},{1,3},{3,1},{4,6},{6,4},{5,7},{7,5},{8,10},{10,8},{9,1... | collective-permute-start | bytes 147464 | tf_op jit(solution)/shard_map/cond/branch_2_fun/ppermute | solution.py:353
  44.4 5.8 %local1.5 = (f32[3840,128]{1,0:T(8,128)S(1)}, f32[960,128]{1,0:T(8,128)S(1)}, f32[400,128]{1,0:T(8,128)S(1)}) custom-call(s32[48]{0:T(128)S(1)} %copy-done.8, f32[128,128]{1,0:T(8,128)S(1)} %get-tuple-element.221.band_ref, f32[3840,128]{1,0:T(8,128)} %get-tuple-element.365.q_ref, f32[3840,128]{1,0:T(8,128)S(1)} %get-tuple-element.222.refs_0_), custom_call_target="tpu_custom_call" | custom-call | flops 20000000 | bytes 5898240 | tf_op jit(solution)/shard_map/cond/branch_2_fun/local1/pallas_call | solution.py:329
  50.2 1.0 %collective-permute-done.13 = f32[400,128]{1,0:T(8,128)} collective-permute-done((f32[400,128]{1,0:T(8,128)S(1)}, f32[400,128]{1,0:T(8,128)}, u32[]{:S(2)}, u32[]{:S(2)}) %collective-permute-start.13) | collective-permute-done | bytes 204832 | tf_op jit(solution)/shard_map/cond/branch_2_fun/ppermute | solution.py:315
  51.2 1.7 %lead1.1 = (f32[480,128]{1,0:T(8,128)S(1)}, f32[480,128]{1,0:T(8,128)S(1)}, f32[400,128]{1,0:T(8,128)S(1)}) custom-call(s32[3]{0:T(128)} %offsets_ref.7, f32[960,128]{1,0:T(8,128)S(1)} %get-tuple-element.324.rim_ref, f32[400,128]{1,0:T(8,128)S(1)} %get-tuple-element.325.face_ref, f32[480,128]{1,0:T(8,128)S(1)} %collective-permute-done.27.east_ref, ...), custom_call_target="tpu_custom_call" | custom-call | tf_op jit(solution)/shard_map/lead1/pallas_call | solution.py:359
  52.9 3.7 %collective-permute-start.29 = (f32[480,128]{1,0:T(8,128)S(1)}, f32[480,128]{1,0:T(8,128)S(1)}, u32[]{:S(2)}, u32[]{:S(2)}) collective-permute-start(f32[480,128]{1,0:T(8,128)S(1)} %get-tuple-element.329), channel_id=1, source_target_pairs={{0,4},{4,0},{8,12},{12,8},{16,20},{20,16},{24,28},{28,24},{32,36},... | collective-permute-start | bytes 737288 | tf_op jit(solution)/shard_map/ppermute | solution.py:319
  57.7 17.0 %conditional.5 = (f32[3840,128]{1,0:T(8,128)}, f32[3840,128]{1,0:T(8,128)S(1)}, f32[96,128]{1,0:T(8,128)}, f32[400,128]{1,0:T(8,128)}, f32[400,128]{1,0:T(8,128)}) conditional(s32[]{:T(128)} %bitcast.1, (s32[3]{0:T(128)}, f32[3840,128]{1,0:T(8,128)}, f32[3840,128]{1,0:T(8,128)S(1)}, f32[480,128]{1,0:T(8,128)S(1)}, ...), branch_computations={%region_6.0_spmd, %region_7.0_spmd, %region_8.0_spmd} | conditional | flops 28000000 | bytes 15598524 | solution.py:451
  57.8 7.4 %collective-permute-start.16 = (f32[400,128]{1,0:T(8,128)S(1)}, f32[400,128]{1,0:T(8,128)}, u32[]{:S(2)}, u32[]{:S(2)}) collective-permute-start(f32[400,128]{1,0:T(8,128)S(1)} %get-tuple-element.241), channel_id=1, source_target_pairs={{0,125},{125,0},{4,1},{1,4},{8,5},{5,8},{12,9},{9,12},{16,13},{13,... | collective-permute-start | bytes 614408 | tf_op jit(solution)/shard_map/cond/branch_0_fun/ppermute | solution.py:315
  65.2 4.1 %finish1.3 = (f32[3840,128]{1,0:T(8,128)}, f32[3840,128]{1,0:T(8,128)S(1)}, f32[96,128]{1,0:T(8,128)S(1)}) custom-call(s32[3]{0:T(128)} %get-tuple-element.228.offsets_ref, f32[3840,128]{1,0:T(8,128)} %get-tuple-element.229.q_ref, f32[3840,128]{1,0:T(8,128)S(1)} %get-tuple-element.230.part_ref, f32[480,128]{1,0:T(8,128)S(1)} %get-tuple-element.231.east_ref, ...), custom_call_target="tpu_custom_call" | custom-call | flops 8000000 | bytes 7864320 | tf_op jit(solution)/shard_map/cond/branch_0_fun/finish1/pallas_call | solution.py:374
  69.3 5.4 %local2.3 = f32[3840,128]{1,0:T(8,128)S(1)} custom-call(s32[48]{0:T(128)S(1)} %copy-done.9, f32[128,128]{1,0:T(8,128)S(1)} %get-tuple-element.238.band_ref, f32[3840,128]{1,0:T(8,128)} %get-tuple-element.372.q_ref, f32[3840,128]{1,0:T(8,128)S(1)} %get-tuple-element.239.refs_0_), custom_call_target="tpu_custom_call" | custom-call | flops 20000000 | bytes 5898240 | tf_op jit(solution)/shard_map/cond/branch_0_fun/local2/pallas_call | solution.py:329
  74.8 4.6 %finish2.1 = (f32[3840,128]{1,0:T(8,128)}, f32[3840,128]{1,0:T(8,128)}) custom-call(s32[3]{0:T(128)} %offsets_ref.7, f32[3840,128]{1,0:T(8,128)} %get-tuple-element.327.q_ref, f32[3840,128]{1,0:T(8,128)S(1)} %get-tuple-element.328.part_ref, f32[480,128]{1,0:T(8,128)S(1)} %collective-permute-done.29.east_ref, f32[480,128]{1,0:T(8,128)S(1)} %collective-permute-done.30.odd_ref, ...), custom_call_target="tpu_custom_call" | custom-call | flops 8000000 | bytes 7864320 | tf_op jit(solution)/shard_map/finish2/pallas_call | solution.py:374
  (31 shorter events, 1.9 us)
Async XLA Ops:
  0.6 14.8 %copy-start = (f32[5,48,16,128]{3,2,1,0:T(8,128)S(1)}, f32[5,48,16,128]{3,2,1,0:T(8,128)}, u32[]{:S(2)}) copy-start(f32[5,48,16,128]{3,2,1,0:T(8,128)} %param.21) | copy-start | bytes 5898244
  0.6 14.8 %copy-start.1 = (f32[128,128]{1,0:T(8,128)S(1)}, f32[128,128]{1,0:T(8,128)}, u32[]{:S(2)}) copy-start(f32[128,128]{1,0:T(8,128)} %constant.12.clone) | copy-start | bytes 196612
  0.7 14.8 %copy-start.5 = (s32[48]{0:T(128)S(1)}, s32[48]{0:T(128)}, u32[]{:S(2)}) copy-start(s32[48]{0:T(128)} %param.23) | copy-start | bytes 580
  3.4 23.6 %collective-permute-start.25 = (f32[480,128]{1,0:T(8,128)S(1)}, f32[480,128]{1,0:T(8,128)S(1)}, u32[]{:S(2)}, u32[]{:S(2)}) collective-permute-start(f32[480,128]{1,0:T(8,128)S(1)} %get-tuple-element.310), channel_id=1, source_target_pairs={{0,124},{4,8},{8,4},{12,16},{16,12},{20,24},{24,20},{28,32},{32,28... | collective-permute-start | bytes 737288 | tf_op jit(solution)/shard_map/ppermute | solution.py:324
  12.4 14.6 %collective-permute-start.24 = (f32[480,128]{1,0:T(8,128)S(1)}, f32[480,128]{1,0:T(8,128)S(1)}, u32[]{:S(2)}, u32[]{:S(2)}) collective-permute-start(f32[480,128]{1,0:T(8,128)S(1)} %get-tuple-element.307.sent_ref), channel_id=1, source_target_pairs={{0,4},{4,0},{8,12},{12,8},{16,20},{20,16},{24,28},{28,24},{32,36},... | collective-permute-start | bytes 737288 | tf_op jit(solution)/shard_map/ppermute | solution.py:319
  14.0 13.0 %collective-permute-start.26 = (f32[96,128]{1,0:T(8,128)S(1)}, f32[96,128]{1,0:T(8,128)S(1)}, u32[]{:S(2)}, u32[]{:S(2)}) collective-permute-start(f32[96,128]{1,0:T(8,128)S(1)} %get-tuple-element.311), channel_id=1, source_target_pairs={{0,2},{2,0},{1,3},{3,1},{4,6},{6,4},{5,7},{7,5},{8,10},{10,8},{9,1... | collective-permute-start | bytes 147464 | tf_op jit(solution)/shard_map/ppermute | solution.py:353
  15.5 11.5 %collective-permute-start.3 = (f32[400,128]{1,0:T(8,128)S(1)}, f32[400,128]{1,0:T(8,128)}, u32[]{:S(2)}, u32[]{:S(2)}) collective-permute-start(f32[400,128]{1,0:T(8,128)S(1)} %get-tuple-element.169), channel_id=1, source_target_pairs={{0,5},{5,0},{4,9},{9,4},{8,13},{13,8},{12,17},{17,12},{16,21},{21,... | collective-permute-start | bytes 614408 | tf_op jit(solution)/shard_map/cond/branch_1_fun/ppermute | solution.py:315
  18.3 8.7 %collective-permute-start.2 = (f32[400,128]{1,0:T(8,128)S(1)}, f32[400,128]{1,0:T(8,128)}, u32[]{:S(2)}, u32[]{:S(2)}) collective-permute-start(f32[400,128]{1,0:T(8,128)S(1)} %get-tuple-element.169), channel_id=1, source_target_pairs={{0,1},{1,0},{4,5},{5,4},{8,9},{9,8},{12,13},{13,12},{16,17},{17,16... | collective-permute-start | bytes 614408 | tf_op jit(solution)/shard_map/cond/branch_1_fun/ppermute | solution.py:315
  28.9 22.4 %collective-permute-start.27 = (f32[480,128]{1,0:T(8,128)S(1)}, f32[480,128]{1,0:T(8,128)S(1)}, u32[]{:S(2)}, u32[]{:S(2)}) collective-permute-start(f32[480,128]{1,0:T(8,128)S(1)} %get-tuple-element.319), channel_id=1, source_target_pairs={{0,4},{4,0},{8,12},{12,8},{16,20},{20,16},{24,28},{28,24},{32,36},... | collective-permute-start | bytes 737288 | tf_op jit(solution)/shard_map/ppermute | solution.py:319
  29.4 21.8 %collective-permute-start.28 = (f32[480,128]{1,0:T(8,128)S(1)}, f32[480,128]{1,0:T(8,128)S(1)}, u32[]{:S(2)}, u32[]{:S(2)}) collective-permute-start(f32[480,128]{1,0:T(8,128)S(1)} %get-tuple-element.320), channel_id=1, source_target_pairs={{0,124},{4,8},{8,4},{12,16},{16,12},{20,24},{24,20},{28,32},{32,28... | collective-permute-start | bytes 737288 | tf_op jit(solution)/shard_map/ppermute | solution.py:324
  36.2 2.9 %copy-start.4 = (f32[480,128]{1,0:T(8,128)}, f32[480,128]{1,0:T(8,128)S(1)}, u32[]{:S(2)}) copy-start(f32[480,128]{1,0:T(8,128)S(1)} %get-tuple-element.214.east_ref) | copy-start | bytes 737284 | tf_op jit(solution)/shard_map/cond
  36.2 14.0 %collective-permute-start.14 = (f32[400,128]{1,0:T(8,128)S(1)}, f32[400,128]{1,0:T(8,128)}, u32[]{:S(2)}, u32[]{:S(2)}) collective-permute-start(f32[400,128]{1,0:T(8,128)S(1)} %get-tuple-element.227), channel_id=1, source_target_pairs={{0,69},{69,0},{4,73},{73,4},{8,77},{77,8},{12,81},{81,12},{16,85},... | collective-permute-start | bytes 614408 | tf_op jit(solution)/shard_map/cond/branch_2_fun/ppermute | solution.py:315
  36.9 14.3 %collective-permute-start.13 = (f32[400,128]{1,0:T(8,128)S(1)}, f32[400,128]{1,0:T(8,128)}, u32[]{:S(2)}, u32[]{:S(2)}) collective-permute-start(f32[400,128]{1,0:T(8,128)S(1)} %get-tuple-element.227), channel_id=1, source_target_pairs={{0,65},{65,0},{4,69},{69,4},{8,73},{73,8},{12,77},{77,12},{16,81},... | collective-permute-start | bytes 614408 | tf_op jit(solution)/shard_map/cond/branch_2_fun/ppermute | solution.py:315
  39.1 5.4 %copy-start.8 = (s32[48]{0:T(128)S(1)}, s32[48]{0:T(128)}, u32[]{:S(2)}) copy-start(s32[48]{0:T(128)} %get-tuple-element.220.pml_ref) | copy-start | bytes 580 | tf_op jit(solution)/shard_map/cond
  43.2 7.0 %collective-permute-start.12 = (f32[96,128]{1,0:T(8,128)S(1)}, f32[96,128]{1,0:T(8,128)}, u32[]{:S(2)}, u32[]{:S(2)}) collective-permute-start(f32[96,128]{1,0:T(8,128)S(1)} %get-tuple-element.226), channel_id=1, source_target_pairs={{0,2},{2,0},{1,3},{3,1},{4,6},{6,4},{5,7},{7,5},{8,10},{10,8},{9,1... | collective-permute-start | bytes 147464 | tf_op jit(solution)/shard_map/cond/branch_2_fun/ppermute | solution.py:353
  52.9 21.8 %collective-permute-start.29 = (f32[480,128]{1,0:T(8,128)S(1)}, f32[480,128]{1,0:T(8,128)S(1)}, u32[]{:S(2)}, u32[]{:S(2)}) collective-permute-start(f32[480,128]{1,0:T(8,128)S(1)} %get-tuple-element.329), channel_id=1, source_target_pairs={{0,4},{4,0},{8,12},{12,8},{16,20},{20,16},{24,28},{28,24},{32,36},... | collective-permute-start | bytes 737288 | tf_op jit(solution)/shard_map/ppermute | solution.py:319
  56.7 18.1 %collective-permute-start.30 = (f32[480,128]{1,0:T(8,128)S(1)}, f32[480,128]{1,0:T(8,128)S(1)}, u32[]{:S(2)}, u32[]{:S(2)}) collective-permute-start(f32[480,128]{1,0:T(8,128)S(1)} %get-tuple-element.330), channel_id=1, source_target_pairs={{0,124},{4,8},{8,4},{12,16},{16,12},{20,24},{24,20},{28,32},{32,28... | collective-permute-start | bytes 737288 | tf_op jit(solution)/shard_map/ppermute | solution.py:324
  57.7 17.0 %collective-permute-start.17 = (f32[400,128]{1,0:T(8,128)S(1)}, f32[400,128]{1,0:T(8,128)}, u32[]{:S(2)}, u32[]{:S(2)}) collective-permute-start(f32[400,128]{1,0:T(8,128)S(1)} %get-tuple-element.241), channel_id=1, source_target_pairs={{0,1},{1,0},{4,5},{5,4},{8,9},{9,8},{12,13},{13,12},{16,17},{17,16... | collective-permute-start | bytes 614408 | tf_op jit(solution)/shard_map/cond/branch_0_fun/ppermute | solution.py:315
  57.8 16.9 %collective-permute-start.16 = (f32[400,128]{1,0:T(8,128)S(1)}, f32[400,128]{1,0:T(8,128)}, u32[]{:S(2)}, u32[]{:S(2)}) collective-permute-start(f32[400,128]{1,0:T(8,128)S(1)} %get-tuple-element.241), channel_id=1, source_target_pairs={{0,125},{125,0},{4,1},{1,4},{8,5},{5,8},{12,9},{9,12},{16,13},{13,... | collective-permute-start | bytes 614408 | tf_op jit(solution)/shard_map/cond/branch_0_fun/ppermute | solution.py:315
  65.2 4.1 %copy-start.9 = (s32[48]{0:T(128)S(1)}, s32[48]{0:T(128)}, u32[]{:S(2)}) copy-start(s32[48]{0:T(128)} %get-tuple-element.237.pml_ref) | copy-start | bytes 580 | tf_op jit(solution)/shard_map/cond
  69.3 5.4 %collective-permute-start.15 = (f32[96,128]{1,0:T(8,128)S(1)}, f32[96,128]{1,0:T(8,128)}, u32[]{:S(2)}, u32[]{:S(2)}) collective-permute-start(f32[96,128]{1,0:T(8,128)S(1)} %get-tuple-element.240), channel_id=1, source_target_pairs={{0,2},{2,0},{1,3},{3,1},{4,6},{6,4},{5,7},{7,5},{8,10},{10,8},{9,1... | collective-permute-start | bytes 147464 | tf_op jit(solution)/shard_map/cond/branch_0_fun/ppermute | solution.py:353

commit v3 on v2

--- a/solution.py
+++ b/solution.py
@@ -2,6 +2,7 @@
 
 import jax
 import jax.numpy as jnp
+import ml_dtypes
 import numpy as np
 from jax import lax
 from jax.experimental import pallas as pl
@@ -22,14 +23,26 @@
 damping = 0.8
 section_a = (0.0, -5.0 / 9.0, -153.0 / 128.0)
 section_b = (1.0 / 3.0, 15.0 / 16.0, 8.0 / 15.0)
-HI = lax.Precision.HIGHEST
-
-
-def band_matrix():
-    band = np.zeros((L, L), np.float32)
+
+
+def split_matrices():
+    band = np.zeros((L, L), np.float64)
     for k, c in enumerate(coeffs, start=1):
-        band += c * (np.eye(L, k=-k) - np.eye(L, k=k)).astype(np.float32)
-    return band
+        band += c * (np.eye(L, k=k) - np.eye(L, k=-k))
+    cells = np.kron(np.eye(L // C), band[:C, :C])
+
+    def halves(x):
+        high = x.astype(ml_dtypes.bfloat16)
+        return high, (x - high.astype(np.float64)).astype(ml_dtypes.bfloat16)
+
+    (rad_high, rad_low), (circ_high, circ_low) = halves(band.T), halves(cells)
+    none = np.zeros_like(rad_high)
+    return np.block([[rad_high, rad_low], [rad_high, none]]), np.block([[circ_high, circ_high], [circ_low, none]])
+
+
+def split(x):
+    high = x.astype(jnp.bfloat16)
+    return high, (x - high.astype(jnp.float32)).astype(jnp.bfloat16)
 
 
 def rows_of(f, a):
@@ -111,7 +124,7 @@
 ANY = pl.BlockSpec(memory_space=pl.ANY)
 
 
-def local_kernel(section, pml_ref, band_ref, q_ref, *refs):
+def local_kernel(section, pml_ref, rad_ref, circ_ref, q_ref, *refs):
     inc_ref = refs[0] if section else None
     *outs, pad = refs[1:] if section else refs
     out_ref = outs[0]
@@ -121,18 +134,7 @@
         pad[f * span : f * span + W * C, :] = zero
         pad[f * span + W * C : f * span + W * C + FIELD, :] = q_ref[f * FIELD : (f + 1) * FIELD, :]
         pad[(f + 1) * span - W * C : (f + 1) * span, :] = zero
-    cell = lax.broadcasted_iota(jnp.int32, (C, L), 0)
-    up = [jnp.where(cell < C - k, c, 0.0) for k, c in enumerate(coeffs, start=1)]
-    down = [jnp.where(cell >= k, c, 0.0) for k, c in enumerate(coeffs, start=1)]
-
-    def circ(x):
-        total = None
-        for k in range(1, W + 1):
-            term = up[k - 1] * pltpu.roll(x, C - k, 0) - down[k - 1] * pltpu.roll(x, k, 0)
-            total = term if total is None else total + term
-        return total
-
-    B = 4
+    B = L // C
 
     def step(n, carry):
         a0 = n * B
@@ -149,20 +151,23 @@
                     for p in range(B)
                 ]
             )
-        radial = jnp.dot(
-            jnp.concatenate(here[3] + here[4], axis=0),
-            band_ref[...],
-            precision=HI,
-            preferred_element_type=jnp.float32,
-        )
+        halves = {f: split(jnp.concatenate(here[f], axis=0)) for f in (2, 3, 4)}
+        lanes = [jnp.concatenate(halves[f], axis=1) for f in (3, 4)]
+        radial = jnp.dot(jnp.concatenate(lanes, axis=0), rad_ref[...], preferred_element_type=jnp.float32)
+        radial = radial[:, :L] + radial[:, L:]
+        cells = [jnp.concatenate([halves[2][h], halves[4][h]], axis=1) for h in range(2)]
+        circ = jnp.dot(circ_ref[...], jnp.concatenate(cells, axis=0), preferred_element_type=jnp.float32)
+        circ = circ[:L] + circ[L:]
         for p in range(B):
             rad3 = radial[p * C : (p + 1) * C]
             rad4 = radial[(B + p) * C : (B + p + 1) * C]
-            div = axial[1][p] + circ(here[2][p]) + rad3
+            circ2 = circ[p * C : (p + 1) * C, :L]
+            circ4 = circ[p * C : (p + 1) * C, L:]
+            div = axial[1][p] + circ2 + rad3
             rates = [
                 mach * axial[0][p] + div,
                 mach * axial[1][p] + axial[4][p],
-                mach * axial[2][p] + circ(here[4][p]),
+                mach * axial[2][p] + circ4,
                 mach * axial[3][p] + rad4,
                 mach * axial[4][p] + div,
             ]
@@ -329,13 +334,13 @@
     return pl.pallas_call(
         functools.partial(local_kernel, section),
         out_shape=[FIELDS] + known,
-        in_specs=[SM] + [VM] * (3 if section else 2),
+        in_specs=[SM] + [VM] * (4 if section else 3),
         out_specs=[VM] * (1 + len(known)),
         scratch_shapes=[pltpu.VMEM((F * (A + 2 * W) * C, L), jnp.float32)],
         compiler_params=PARAMS,
         cost_estimate=pl.CostEstimate(flops=20_000_000, bytes_accessed=3 * ROWS * L * 4, transcendentals=0),
         name=f"local{section}",
-    )(pml_zone, band_matrix(), q, *([inc] if section else []))
+    )(pml_zone, *split_matrices(), q, *([inc] if section else []))
 
 
 def first_branch(blocks, q, pml_zone, face):

time: 80.5 us -> 80.2 us (level)
  the two profiles are of different devices: /device:TPU:0 before, /device:TPU:1 now
where the time goes in v3:
time: 80.2 us; the launch traced here: 79.8 us
  Pallas kernels  33.8 us (42%)
  starting transfers between devices  33.7 us (42%)
  waiting for transfers between devices  7.84 us (10%)
  between operations  2.77 us (3%)
  local copies, waits for them, and re-layouts  1.42 us (2%)
    ppermute x3, starting transfers between devices, send_odd(): lax.ppermute(odd, 'circ', [(i, (i + (1 if i % 2 else -1)) % count) for i...  18 us
    pallas_call x3, Pallas kernels, finish(): pl.pallas_call(functools.partial(finish_kernel, section, last), out_shape...  13 us
    pallas_call x3, Pallas kernels, local_terms(): pl.pallas_call(functools.partial(local_kernel, section), out_shape=[FIELD...  12.8 us
    ppermute x6, starting transfers between devices, swap_faces(): return lax.ppermute(face, ('circ', 'half'), pairs)  10.8 us
    ppermute x6, waiting for transfers between devices, swap_faces(): return lax.ppermute(face, ('circ', 'half'), pairs)  7.82 us
    pallas_call x2, Pallas kernels, lead(): pl.pallas_call(functools.partial(lead_kernel, section), out_shape=[RIM, R...  3.63 us
    ppermute x3, starting transfers between devices, send_east(): lax.ppermute(east, 'circ', [(i, i ^ 1) for i in range(lax.axis_size('circ...  3.62 us
    pallas_call x1, Pallas kernels, body(): pl.pallas_call(enter_lead_kernel, out_shape=[RIM, RIM] + [flag] * SECTION...  2.72 us
  transfers between devices with their start and end apart: 15, of which 2 were waited for; matrix products, arithmetic and copies ran while one was open for 0% of the time, Pallas kernels for 29%

profile of v3, /device:TPU:1, one launch (start us, length us, event | category | flops | bytes accessed | tf_op | source)
XLA Modules:
  0.0 79.8 jit_solution(2046760852226746188)
XLA Ops:
  0.7 2.7 %enter_lead.1 = (f32[480,128]{1,0:T(8,128)S(1)}, f32[480,128]{1,0:T(8,128)S(1)}, s32[1]{0:T(128)}, s32[1]{0:T(128)}, s32[1]{0:T(128)}) custom-call(s32[3]{0:T(128)} %offsets_ref.7, f32[3840,128]{1,0:T(8,128)} %bitcast.6), custom_call_target="tpu_custom_call" | custom-call | tf_op jit(solution)/shard_map/enter_lead/pallas_call | solution.py:428
  3.4 9.5 %collective-permute-start.25 = (f32[480,128]{1,0:T(8,128)S(1)}, f32[480,128]{1,0:T(8,128)S(1)}, u32[]{:S(2)}, u32[]{:S(2)}) collective-permute-start(f32[480,128]{1,0:T(8,128)S(1)} %get-tuple-element.337), channel_id=1, source_target_pairs={{0,124},{4,8},{8,4},{12,16},{16,12},{20,24},{24,20},{28,32},{32,28... | collective-permute-start | bytes 737288 | tf_op jit(solution)/shard_map/ppermute | solution.py:329
  12.9 1.6 %enter.1 = (f32[96,128]{1,0:T(8,128)S(1)}, f32[400,128]{1,0:T(8,128)S(1)}) custom-call(f32[3840,128]{1,0:T(8,128)} %bitcast.7, f32[480,128]{1,0:T(8,128)S(1)} %get-tuple-element.334.sent_ref), custom_call_target="tpu_custom_call" | custom-call | flops 8000000 | bytes 7864320 | tf_op jit(solution)/shard_map/enter/pallas_call | solution.py:437
  15.7 12.1 %conditional.3 = (f32[3840,128]{1,0:T(8,128)}, f32[960,128]{1,0:T(8,128)S(1)}, f32[400,128]{1,0:T(8,128)S(1)}, f32[400,128]{1,0:T(8,128)}, f32[400,128]{1,0:T(8,128)}) conditional(s32[]{:T(128)} %bitcast.3, (s32[48]{0:T(128)S(1)}, bf16[256,256]{1,0:T(8,128)(2,1)S(1)}, bf16[256,256]{1,0:T(8,128)(2,1)S(1)}, f32[3840,128]{1,0:T(8,128)S(1)}, ...), branch_computations={%region_0.0_spmd, %region_1.0_spmd, %region_2.0_spmd} | conditional | flops 20000000 | bytes 7536760 | solution.py:452
  15.7 1.3 %collective-permute-start.1 = (f32[400,128]{1,0:T(8,128)S(1)}, f32[400,128]{1,0:T(8,128)}, u32[]{:S(2)}, u32[]{:S(2)}) collective-permute-start(f32[400,128]{1,0:T(8,128)S(1)} %get-tuple-element.181), channel_id=1, source_target_pairs={{0,1},{1,0},{4,5},{5,4},{8,9},{9,8},{12,13},{13,12},{16,17},{17,16... | collective-permute-start | bytes 614408 | tf_op jit(solution)/shard_map/cond/branch_0_fun/ppermute | solution.py:320
  17.0 3.8 %collective-permute-start = (f32[400,128]{1,0:T(8,128)S(1)}, f32[400,128]{1,0:T(8,128)}, u32[]{:S(2)}, u32[]{:S(2)}) collective-permute-start(f32[400,128]{1,0:T(8,128)S(1)} %get-tuple-element.181), channel_id=1, source_target_pairs={{0,125},{125,0},{4,1},{1,4},{8,5},{5,8},{12,9},{9,12},{16,13},{13,... | collective-permute-start | bytes 614408 | tf_op jit(solution)/shard_map/cond/branch_0_fun/ppermute | solution.py:320
  20.9 4.4 %local0.3 = (f32[3840,128]{1,0:T(8,128)}, f32[960,128]{1,0:T(8,128)S(1)}, f32[400,128]{1,0:T(8,128)S(1)}) custom-call(s32[48]{0:T(128)S(1)} %get-tuple-element.174.pml_ref, bf16[256,256]{1,0:T(8,128)(2,1)S(1)} %get-tuple-element.175.rad_ref, bf16[256,256]{1,0:T(8,128)(2,1)S(1)} %get-tuple-element.176.circ_ref, f32[3840,128]{1,0:T(8,128)S(1)} %get-tuple-element.177.q_ref), custom_call_target="tpu_custom_call" | custom-call | flops 20000000 | bytes 5898240 | tf_op jit(solution)/shard_map/cond/branch_0_fun/local0/pallas_call | solution.py:334
  25.3 2.5 %collective-permute-done = f32[400,128]{1,0:T(8,128)} collective-permute-done((f32[400,128]{1,0:T(8,128)S(1)}, f32[400,128]{1,0:T(8,128)}, u32[]{:S(2)}, u32[]{:S(2)}) %collective-permute-start) | collective-permute-done | bytes 204832 | tf_op jit(solution)/shard_map/cond/branch_0_fun/ppermute | solution.py:320
  28.5 1.8 %lead0.1 = (f32[480,128]{1,0:T(8,128)S(1)}, f32[480,128]{1,0:T(8,128)S(1)}, f32[400,128]{1,0:T(8,128)S(1)}) custom-call(s32[3]{0:T(128)S(1)} %copy-done.5, f32[960,128]{1,0:T(8,128)S(1)} %get-tuple-element.341.rim_ref, f32[400,128]{1,0:T(8,128)S(1)} %get-tuple-element.342.face_ref, f32[480,128]{1,0:T(8,128)} %copy-done.4, ...), custom_call_target="tpu_custom_call" | custom-call | tf_op jit(solution)/shard_map/lead0/pallas_call | solution.py:364
  30.3 1.0 %collective-permute-start.27 = (f32[480,128]{1,0:T(8,128)S(1)}, f32[480,128]{1,0:T(8,128)S(1)}, u32[]{:S(2)}, u32[]{:S(2)}) collective-permute-start(f32[480,128]{1,0:T(8,128)S(1)} %get-tuple-element.346), channel_id=1, source_target_pairs={{0,4},{4,0},{8,12},{12,8},{16,20},{20,16},{24,28},{28,24},{32,36},... | collective-permute-start | bytes 737288 | tf_op jit(solution)/shard_map/ppermute | solution.py:324
  31.3 5.2 %collective-permute-start.28 = (f32[480,128]{1,0:T(8,128)S(1)}, f32[480,128]{1,0:T(8,128)S(1)}, u32[]{:S(2)}, u32[]{:S(2)}) collective-permute-start(f32[480,128]{1,0:T(8,128)S(1)} %get-tuple-element.347), channel_id=1, source_target_pairs={{0,124},{4,8},{8,4},{12,16},{16,12},{20,24},{24,20},{28,32},{32,28... | collective-permute-start | bytes 737288 | tf_op jit(solution)/shard_map/ppermute | solution.py:329
  37.1 12.6 %conditional.4 = (f32[3840,128]{1,0:T(8,128)}, f32[3840,128]{1,0:T(8,128)S(1)}, f32[960,128]{1,0:T(8,128)S(1)}, f32[400,128]{1,0:T(8,128)S(1)}, f32[96,128]{1,0:...) conditional(s32[]{:T(128)} %bitcast.2, (s32[3]{0:T(128)S(1)}, f32[3840,128]{1,0:T(8,128)S(1)}, ...), branch_computations={%region_3.0_spmd, %region_4.0_spmd, %region_5.0_spmd} | conditional | flops 28000000 | bytes 15597744 | solution.py:456
  37.2 3.8 %collective-permute-start.11 = (f32[400,128]{1,0:T(8,128)S(1)}, f32[400,128]{1,0:T(8,128)}, u32[]{:S(2)}, u32[]{:S(2)}) collective-permute-start(f32[400,128]{1,0:T(8,128)S(1)} %get-tuple-element.233), channel_id=1, source_target_pairs={{0,5},{5,0},{4,9},{9,4},{8,13},{13,8},{12,17},{17,12},{16,21},{21,... | collective-permute-start | bytes 614408 | tf_op jit(solution)/shard_map/cond/branch_1_fun/ppermute | solution.py:320
  41.0 4.1 %finish0.4 = (f32[3840,128]{1,0:T(8,128)}, f32[3840,128]{1,0:T(8,128)S(1)}, f32[96,128]{1,0:T(8,128)S(1)}) custom-call(s32[3]{0:T(128)S(1)} %get-tuple-element.216.offsets_ref, f32[3840,128]{1,0:T(8,128)S(1)} %get-tuple-element.217.q_ref, f32[3840,128]{1,0:T(8,128)} %get-tuple-element.218.part_ref, f32[480,128]{1,0:T(8,128)} %get-tuple-element.219.east_ref, ...), custom_call_target="tpu_custom_call" | custom-call | flops 8000000 | bytes 7864320 | tf_op jit(solution)/shard_map/cond/branch_1_fun/finish0/pallas_call | solution.py:379
  45.1 4.4 %local1.4 = (f32[3840,128]{1,0:T(8,128)S(1)}, f32[960,128]{1,0:T(8,128)S(1)}, f32[400,128]{1,0:T(8,128)S(1)}) custom-call(s32[48]{0:T(128)S(1)} %get-tuple-element.225.pml_ref, bf16[256,256]{1,0:T(8,128)(2,1)S(1)} %get-tuple-element.226.rad_ref, bf16[256,256]{1,0:T(8,128)(2,1)S(1)} %get-tuple-element.227.circ_ref, f32[3840,128]{1,0:T(8,128)} %get-tuple-element.385.q_ref, ...), custom_call_target="tpu_custom_call" | custom-call | flops 20000000 | bytes 5898240 | tf_op jit(solution)/shard_map/cond/branch_1_fun/local1/pallas_call | solution.py:334
  50.4 1.8 %lead1.1 = (f32[480,128]{1,0:T(8,128)S(1)}, f32[480,128]{1,0:T(8,128)S(1)}, f32[400,128]{1,0:T(8,128)S(1)}) custom-call(s32[3]{0:T(128)S(1)} %copy-done.5, f32[960,128]{1,0:T(8,128)S(1)} %get-tuple-element.351.rim_ref, f32[400,128]{1,0:T(8,128)S(1)} %get-tuple-element.352.face_ref, f32[480,128]{1,0:T(8,128)S(1)} %collective-permute-done.27.east_ref, ...), custom_call_target="tpu_custom_call" | custom-call | tf_op jit(solution)/shard_map/lead1/pallas_call | solution.py:364
  52.3 2.6 %collective-permute-start.29 = (f32[480,128]{1,0:T(8,128)S(1)}, f32[480,128]{1,0:T(8,128)S(1)}, u32[]{:S(2)}, u32[]{:S(2)}) collective-permute-start(f32[480,128]{1,0:T(8,128)S(1)} %get-tuple-element.356), channel_id=1, source_target_pairs={{0,4},{4,0},{8,12},{12,8},{16,20},{20,16},{24,28},{28,24},{32,36},... | collective-permute-start | bytes 737288 | tf_op jit(solution)/shard_map/ppermute | solution.py:324
  54.9 3.3 %collective-permute-start.30 = (f32[480,128]{1,0:T(8,128)S(1)}, f32[480,128]{1,0:T(8,128)S(1)}, u32[]{:S(2)}, u32[]{:S(2)}) collective-permute-start(f32[480,128]{1,0:T(8,128)S(1)} %get-tuple-element.357), channel_id=1, source_target_pairs={{0,124},{4,8},{8,4},{12,16},{16,12},{20,24},{24,20},{28,32},{32,28... | collective-permute-start | bytes 737288 | tf_op jit(solution)/shard_map/ppermute | solution.py:329
  58.9 16.3 %conditional.5 = (f32[3840,128]{1,0:T(8,128)}, f32[3840,128]{1,0:T(8,128)S(1)}, f32[96,128]{1,0:T(8,128)}, f32[400,128]{1,0:T(8,128)}, f32[400,128]{1,0:T(8,128)}) conditional(s32[]{:T(128)} %bitcast.1, (s32[3]{0:T(128)S(1)}, f32[3840,128]{1,0:T(8,128)}, f32[3840,128]{1,0:T(8,128)S(1)}, f32[480,128]{1,0:T(8,128)S(1)}, ...), branch_computations={%region_6.0_spmd, %region_7.0_spmd, %region_8.0_spmd} | conditional | flops 28000000 | bytes 15597728 | solution.py:456
  58.9 1.8 %collective-permute-start.23 = (f32[400,128]{1,0:T(8,128)S(1)}, f32[400,128]{1,0:T(8,128)}, u32[]{:S(2)}, u32[]{:S(2)}) collective-permute-start(f32[400,128]{1,0:T(8,128)S(1)} %get-tuple-element.296), channel_id=1, source_target_pairs={{0,69},{69,0},{4,73},{73,4},{8,77},{77,8},{12,81},{81,12},{16,85},... | collective-permute-start | bytes 614408 | tf_op jit(solution)/shard_map/cond/branch_2_fun/ppermute | solution.py:320
  60.7 4.3 %finish1.5 = (f32[3840,128]{1,0:T(8,128)}, f32[3840,128]{1,0:T(8,128)S(1)}, f32[96,128]{1,0:T(8,128)S(1)}) custom-call(s32[3]{0:T(128)S(1)} %get-tuple-element.282.offsets_ref, f32[3840,128]{1,0:T(8,128)} %get-tuple-element.283.q_ref, f32[3840,128]{1,0:T(8,128)S(1)} %get-tuple-element.284.part_ref, f32[480,128]{1,0:T(8,128)S(1)} %get-tuple-element.285.east_ref, ...), custom_call_target="tpu_custom_call" | custom-call | flops 8000000 | bytes 7864320 | tf_op jit(solution)/shard_map/cond/branch_2_fun/finish1/pallas_call | solution.py:379
  65.8 4.0 %local2.5 = f32[3840,128]{1,0:T(8,128)S(1)} custom-call(s32[48]{0:T(128)S(1)} %get-tuple-element.291.pml_ref, bf16[256,256]{1,0:T(8,128)(2,1)S(1)} %get-tuple-element.292.rad_ref, bf16[256,256]{1,0:T(8,128)(2,1)S(1)} %get-tuple-element.293.circ_ref, f32[3840,128]{1,0:T(8,128)} %get-tuple-element.409.q_ref, f32[3840,128]{1,0:T(8,128)S(1)} %get-tuple-element.294.refs_0_), custom_call_target="tpu_custom_call" | custom-call | flops 20000000 | bytes 5898240 | tf_op jit(solution)/shard_map/cond/branch_2_fun/local2/pallas_call | solution.py:334
  69.9 5.3 %collective-permute-done.22 = f32[400,128]{1,0:T(8,128)} collective-permute-done((f32[400,128]{1,0:T(8,128)S(1)}, f32[400,128]{1,0:T(8,128)}, u32[]{:S(2)}, u32[]{:S(2)}) %collective-permute-start.22) | collective-permute-done | bytes 204832 | tf_op jit(solution)/shard_map/cond/branch_2_fun/ppermute | solution.py:320
  75.2 4.6 %finish2.1 = (f32[3840,128]{1,0:T(8,128)}, f32[3840,128]{1,0:T(8,128)}) custom-call(s32[3]{0:T(128)S(1)} %copy-done.5, f32[3840,128]{1,0:T(8,128)} %get-tuple-element.354.q_ref, f32[3840,128]{1,0:T(8,128)S(1)} %get-tuple-element.355.part_ref, f32[480,128]{1,0:T(8,128)S(1)} %collective-permute-done.29.east_ref, ...), custom_call_target="tpu_custom_call" | custom-call | flops 8000000 | bytes 7864320 | tf_op jit(solution)/shard_map/finish2/pallas_call | solution.py:379
  (33 shorter events, 2.8 us)
Async XLA Ops:
  0.6 15.0 %copy-start = (f32[5,48,16,128]{3,2,1,0:T(8,128)S(1)}, f32[5,48,16,128]{3,2,1,0:T(8,128)}, u32[]{:S(2)}) copy-start(f32[5,48,16,128]{3,2,1,0:T(8,128)} %param.30) | copy-start | bytes 5898244
  0.6 15.0 %copy-start.1 = (bf16[256,256]{1,0:T(8,128)(2,1)S(1)}, bf16[256,256]{1,0:T(8,128)(2,1)}, u32[]{:S(2)}) copy-start(bf16[256,256]{1,0:T(8,128)(2,1)} %constant.15.clone) | copy-start | bytes 393220
  0.7 15.0 %copy-start.2 = (bf16[256,256]{1,0:T(8,128)(2,1)S(1)}, bf16[256,256]{1,0:T(8,128)(2,1)}, u32[]{:S(2)}) copy-start(bf16[256,256]{1,0:T(8,128)(2,1)} %constant.14.clone) | copy-start | bytes 393220
  0.7 15.0 %copy-start.6 = (s32[48]{0:T(128)S(1)}, s32[48]{0:T(128)}, u32[]{:S(2)}) copy-start(s32[48]{0:T(128)} %param.32) | copy-start | bytes 580
  3.4 24.4 %collective-permute-start.25 = (f32[480,128]{1,0:T(8,128)S(1)}, f32[480,128]{1,0:T(8,128)S(1)}, u32[]{:S(2)}, u32[]{:S(2)}) collective-permute-start(f32[480,128]{1,0:T(8,128)S(1)} %get-tuple-element.337), channel_id=1, source_target_pairs={{0,124},{4,8},{8,4},{12,16},{16,12},{20,24},{24,20},{28,32},{32,28... | collective-permute-start | bytes 737288 | tf_op jit(solution)/shard_map/ppermute | solution.py:329
  12.9 14.9 %collective-permute-start.24 = (f32[480,128]{1,0:T(8,128)S(1)}, f32[480,128]{1,0:T(8,128)S(1)}, u32[]{:S(2)}, u32[]{:S(2)}) collective-permute-start(f32[480,128]{1,0:T(8,128)S(1)} %get-tuple-element.334.sent_ref), channel_id=1, source_target_pairs={{0,4},{4,0},{8,12},{12,8},{16,20},{20,16},{24,28},{28,24},{32,36},... | collective-permute-start | bytes 737288 | tf_op jit(solution)/shard_map/ppermute | solution.py:324
  14.5 13.3 %collective-permute-start.26 = (f32[96,128]{1,0:T(8,128)S(1)}, f32[96,128]{1,0:T(8,128)S(1)}, u32[]{:S(2)}, u32[]{:S(2)}) collective-permute-start(f32[96,128]{1,0:T(8,128)S(1)} %get-tuple-element.338), channel_id=1, source_target_pairs={{0,2},{2,0},{1,3},{3,1},{4,6},{6,4},{5,7},{7,5},{8,10},{10,8},{9,1... | collective-permute-start | bytes 147464 | tf_op jit(solution)/shard_map/ppermute | solution.py:358
  15.7 12.8 %copy-start.5 = (s32[3]{0:T(128)S(1)}, s32[3]{0:T(128)}, u32[]{:S(2)}) copy-start(s32[3]{0:T(128)} %offsets_ref.7) | copy-start | bytes 40
  15.7 9.6 %collective-permute-start.1 = (f32[400,128]{1,0:T(8,128)S(1)}, f32[400,128]{1,0:T(8,128)}, u32[]{:S(2)}, u32[]{:S(2)}) collective-permute-start(f32[400,128]{1,0:T(8,128)S(1)} %get-tuple-element.181), channel_id=1, source_target_pairs={{0,1},{1,0},{4,5},{5,4},{8,9},{9,8},{12,13},{13,12},{16,17},{17,16... | collective-permute-start | bytes 614408 | tf_op jit(solution)/shard_map/cond/branch_0_fun/ppermute | solution.py:320
  17.0 10.8 %collective-permute-start = (f32[400,128]{1,0:T(8,128)S(1)}, f32[400,128]{1,0:T(8,128)}, u32[]{:S(2)}, u32[]{:S(2)}) collective-permute-start(f32[400,128]{1,0:T(8,128)S(1)} %get-tuple-element.181), channel_id=1, source_target_pairs={{0,125},{125,0},{4,1},{1,4},{8,5},{5,8},{12,9},{9,12},{16,13},{13,... | collective-permute-start | bytes 614408 | tf_op jit(solution)/shard_map/cond/branch_0_fun/ppermute | solution.py:320
  27.8 0.7 copy-start.4
  30.3 19.4 %collective-permute-start.27 = (f32[480,128]{1,0:T(8,128)S(1)}, f32[480,128]{1,0:T(8,128)S(1)}, u32[]{:S(2)}, u32[]{:S(2)}) collective-permute-start(f32[480,128]{1,0:T(8,128)S(1)} %get-tuple-element.346), channel_id=1, source_target_pairs={{0,4},{4,0},{8,12},{12,8},{16,20},{20,16},{24,28},{28,24},{32,36},... | collective-permute-start | bytes 737288 | tf_op jit(solution)/shard_map/ppermute | solution.py:324
  31.3 18.5 %collective-permute-start.28 = (f32[480,128]{1,0:T(8,128)S(1)}, f32[480,128]{1,0:T(8,128)S(1)}, u32[]{:S(2)}, u32[]{:S(2)}) collective-permute-start(f32[480,128]{1,0:T(8,128)S(1)} %get-tuple-element.347), channel_id=1, source_target_pairs={{0,124},{4,8},{8,4},{12,16},{16,12},{20,24},{24,20},{28,32},{32,28... | collective-permute-start | bytes 737288 | tf_op jit(solution)/shard_map/ppermute | solution.py:329
  37.2 12.3 %collective-permute-start.11 = (f32[400,128]{1,0:T(8,128)S(1)}, f32[400,128]{1,0:T(8,128)}, u32[]{:S(2)}, u32[]{:S(2)}) collective-permute-start(f32[400,128]{1,0:T(8,128)S(1)} %get-tuple-element.233), channel_id=1, source_target_pairs={{0,5},{5,0},{4,9},{9,4},{8,13},{13,8},{12,17},{17,12},{16,21},{21,... | collective-permute-start | bytes 614408 | tf_op jit(solution)/shard_map/cond/branch_1_fun/ppermute | solution.py:320
  41.0 8.6 %collective-permute-start.10 = (f32[400,128]{1,0:T(8,128)S(1)}, f32[400,128]{1,0:T(8,128)}, u32[]{:S(2)}, u32[]{:S(2)}) collective-permute-start(f32[400,128]{1,0:T(8,128)S(1)} %get-tuple-element.233), channel_id=1, source_target_pairs={{0,1},{1,0},{4,5},{5,4},{8,9},{9,8},{12,13},{13,12},{16,17},{17,16... | collective-permute-start | bytes 614408 | tf_op jit(solution)/shard_map/cond/branch_1_fun/ppermute | solution.py:320
  45.1 4.4 %collective-permute-start.9 = (f32[96,128]{1,0:T(8,128)S(1)}, f32[96,128]{1,0:T(8,128)}, u32[]{:S(2)}, u32[]{:S(2)}) collective-permute-start(f32[96,128]{1,0:T(8,128)S(1)} %get-tuple-element.232), channel_id=1, source_target_pairs={{0,2},{2,0},{1,3},{3,1},{4,6},{6,4},{5,7},{7,5},{8,10},{10,8},{9,1... | collective-permute-start | bytes 147464 | tf_op jit(solution)/shard_map/cond/branch_1_fun/ppermute | solution.py:358
  49.7 0.7 copy-start.3
  52.3 22.9 %collective-permute-start.29 = (f32[480,128]{1,0:T(8,128)S(1)}, f32[480,128]{1,0:T(8,128)S(1)}, u32[]{:S(2)}, u32[]{:S(2)}) collective-permute-start(f32[480,128]{1,0:T(8,128)S(1)} %get-tuple-element.356), channel_id=1, source_target_pairs={{0,4},{4,0},{8,12},{12,8},{16,20},{20,16},{24,28},{28,24},{32,36},... | collective-permute-start | bytes 737288 | tf_op jit(solution)/shard_map/ppermute | solution.py:324
  54.9 20.3 %collective-permute-start.30 = (f32[480,128]{1,0:T(8,128)S(1)}, f32[480,128]{1,0:T(8,128)S(1)}, u32[]{:S(2)}, u32[]{:S(2)}) collective-permute-start(f32[480,128]{1,0:T(8,128)S(1)} %get-tuple-element.357), channel_id=1, source_target_pairs={{0,124},{4,8},{8,4},{12,16},{16,12},{20,24},{24,20},{28,32},{32,28... | collective-permute-start | bytes 737288 | tf_op jit(solution)/shard_map/ppermute | solution.py:329
  58.9 11.0 %collective-permute-start.23 = (f32[400,128]{1,0:T(8,128)S(1)}, f32[400,128]{1,0:T(8,128)}, u32[]{:S(2)}, u32[]{:S(2)}) collective-permute-start(f32[400,128]{1,0:T(8,128)S(1)} %get-tuple-element.296), channel_id=1, source_target_pairs={{0,69},{69,0},{4,73},{73,4},{8,77},{77,8},{12,81},{81,12},{16,85},... | collective-permute-start | bytes 614408 | tf_op jit(solution)/shard_map/cond/branch_2_fun/ppermute | solution.py:320
  60.7 14.5 %collective-permute-start.22 = (f32[400,128]{1,0:T(8,128)S(1)}, f32[400,128]{1,0:T(8,128)}, u32[]{:S(2)}, u32[]{:S(2)}) collective-permute-start(f32[400,128]{1,0:T(8,128)S(1)} %get-tuple-element.296), channel_id=1, source_target_pairs={{0,65},{65,0},{4,69},{69,4},{8,73},{73,8},{12,77},{77,12},{16,81},... | collective-permute-start | bytes 614408 | tf_op jit(solution)/shard_map/cond/branch_2_fun/ppermute | solution.py:320
  65.0 4.9 %collective-permute-start.21 = (f32[96,128]{1,0:T(8,128)S(1)}, f32[96,128]{1,0:T(8,128)}, u32[]{:S(2)}, u32[]{:S(2)}) collective-permute-start(f32[96,128]{1,0:T(8,128)S(1)} %get-tuple-element.295), channel_id=1, source_target_pairs={{0,2},{2,0},{1,3},{3,1},{4,6},{6,4},{5,7},{7,5},{8,10},{10,8},{9,1... | collective-permute-start | bytes 147464 | tf_op jit(solution)/shard_map/cond/branch_2_fun/ppermute | solution.py:358

commit v4 on v2

--- a/solution.py
+++ b/solution.py
@@ -132,7 +132,7 @@
             total = term if total is None else total + term
         return total
 
-    B = 4
+    B = 8
 
     def step(n, carry):
         a0 = n * B
@@ -338,9 +338,9 @@
     )(pml_zone, band_matrix(), q, *([inc] if section else []))
 
 
-def first_branch(blocks, q, pml_zone, face):
+def first_branch(blocks, q, pml_zone, rad, face):
     own, beyond = swap_faces(face, blocks), swap_faces(face, blocks + 1)
-    return local_terms(0, q, (), pml_zone), own, beyond
+    return local_terms(0, q, (), pml_zone), send_rad(rad), own, beyond
 
 
 def section_branch(section, blocks, offsets, q, part, arrived, pml_zone, face):
@@ -383,11 +383,16 @@
     )(offsets, q, part, *arrived)
 
 
-def enter_lead_kernel(offsets_ref, state_ref, east_ref, odd_ref, kind0, kind1, kind2, q_ref, sems):
+def enter_kernel(offsets_ref, state_ref, *refs):
+    east_ref, odd_ref, rad_ref, face_ref, kind0, kind1, kind2, q_ref, sems = refs
     copies = []
-    for n, f in enumerate((2, 4)):
+    for n, f in enumerate((2, 4, 3)):
         rows = pl.ds(f * FIELD, FIELD)
         copies.append(pltpu.make_async_copy(state_ref.at[rows], q_ref.at[rows], sems.at[n]))
+    edge = jnp.where(lax.axis_index("half") == 0, (A - W) * C, 0)
+    for f in (0, 1):
+        rows = pl.ds(pl.multiple_of(f * FIELD + edge, C), W * C)
+        copies.append(pltpu.make_async_copy(state_ref.at[rows], q_ref.at[rows], sems.at[3 + f]))
     for copy in copies:
         copy.start()
     for section, kind in enumerate((kind0, kind1, kind2)):
@@ -396,56 +401,28 @@
     for copy in copies:
         copy.wait()
     pack_rims(q_ref, east_ref, odd_ref)
-
-
-def enter_kernel(state_ref, sent_ref, *refs):
-    *messages, q_ref, sems = refs
-    copies = []
-    for n, f in enumerate((3, 4)):
-        rows = pl.ds(f * FIELD, FIELD)
-        copies.append(pltpu.make_async_copy(state_ref.at[rows], q_ref.at[rows], sems.at[n]))
-    edge = jnp.where(lax.axis_index("half") == 0, (A - W) * C, 0)
-    for f in (0, 1, 2):
-        rows = pl.ds(pl.multiple_of(f * FIELD + edge, C), W * C)
-        copies.append(pltpu.make_async_copy(state_ref.at[rows], q_ref.at[rows], sems.at[2 + f]))
-    for copy in copies:
-        copy.start()
-    for copy in copies:
-        copy.wait()
-    pack_rad(q_ref, messages[0])
-    pack_faces(q_ref, messages[1])
+    pack_rad(q_ref, rad_ref)
+    pack_faces(q_ref, face_ref)
 
 
 def body(state, offsets, pml_zone):
     q = state.reshape(ROWS, L)
-    held = pltpu.with_memory_space_constraint(q, pltpu.HBM)
     flag = jax.ShapeDtypeStruct((1,), jnp.int32)
-    east, odd, *kinds = pl.pallas_call(
-        enter_lead_kernel,
-        out_shape=[RIM, RIM] + [flag] * SECTIONS,
+    east, odd, rad, face, *kinds = pl.pallas_call(
+        enter_kernel,
+        out_shape=[RIM, RIM, RAD, FACE] + [flag] * SECTIONS,
         in_specs=[SM, pl.BlockSpec(memory_space=pltpu.HBM)],
-        out_specs=[VM, VM] + [SM] * SECTIONS,
-        scratch_shapes=[pltpu.VMEM((ROWS, L), jnp.float32), pltpu.SemaphoreType.DMA((2,))],
-        compiler_params=PARAMS,
-        name="enter_lead",
-    )(offsets, held)
-    rad, face = pl.pallas_call(
-        enter_kernel,
-        out_shape=[RAD, FACE],
-        in_specs=[pl.BlockSpec(memory_space=pltpu.HBM), ANY],
-        out_specs=[VM] * 2,
+        out_specs=[VM] * 4 + [SM] * SECTIONS,
         scratch_shapes=[pltpu.VMEM((ROWS, L), jnp.float32), pltpu.SemaphoreType.DMA((W,))],
         compiler_params=PARAMS,
-        cost_estimate=pl.CostEstimate(flops=8_000_000, bytes_accessed=4 * ROWS * L * 4, transcendentals=0),
         name="enter",
-    )(held, east)
+    )(offsets, pltpu.with_memory_space_constraint(q, pltpu.HBM))
     shifts = (-1, 0, C)
     for section in range(SECTIONS):
         from_east, from_odd = send_east(east), send_odd(odd)
         if section == 0:
-            from_rad = send_rad(rad)
-            (part, *known), own, beyond = lax.switch(
-                kinds[0][0], [functools.partial(first_branch, blocks) for blocks in shifts], q, pml_zone, face
+            (part, *known), from_rad, own, beyond = lax.switch(
+                kinds[0][0], [functools.partial(first_branch, blocks) for blocks in shifts], q, pml_zone, rad, face
             )
         else:
             q, (part, *known), from_rad, own, beyond = lax.switch(

time: 80.5 us -> 77.9 us (0.968)
  the two profiles are of different devices: /device:TPU:0 before, /device:TPU:1 now
where the time goes in v4:
time: 77.9 us; the launch traced here: 77.5 us
  Pallas kernels  35.1 us (45%)
  starting transfers between devices  31.5 us (40%)
  waiting for transfers between devices  7.61 us (10%)
  between operations  2.68 us (3%)
    ppermute x3, starting transfers between devices, send_odd(): lax.ppermute(odd, 'circ', [(i, (i + (1 if i % 2 else -1)) % count) for i...  18.5 us
    pallas_call x3, Pallas kernels, local_terms(): pl.pallas_call(functools.partial(local_kernel, section), out_shape=[FIELD...  16 us
    pallas_call x3, Pallas kernels, finish(): pl.pallas_call(functools.partial(finish_kernel, section, last), out_shape...  12.8 us
    ppermute x3, starting transfers between devices, send_east(): lax.ppermute(east, 'circ', [(i, i ^ 1) for i in range(lax.axis_size('circ...  6.62 us
    ppermute x6, waiting for transfers between devices, swap_faces(): return lax.ppermute(face, ('circ', 'half'), pairs)  4.65 us
    ppermute x6, starting transfers between devices, swap_faces(): return lax.ppermute(face, ('circ', 'half'), pairs)  3.67 us
    pallas_call x2, Pallas kernels, lead(): pl.pallas_call(functools.partial(lead_kernel, section), out_shape=[RIM, R...  3.41 us
    ppermute x3, waiting for transfers between devices, send_rad(): return lax.ppermute(rad, 'rad', [(0, 1), (1, 0)])  2.94 us
  transfers between devices with their start and end apart: 15, of which 4 were waited for; matrix products, arithmetic and copies ran while one was open for 0% of the time, Pallas kernels for 31%

profile of v4, /device:TPU:1, one launch (start us, length us, event | category | flops | bytes accessed | tf_op | source)
XLA Modules:
  0.0 77.5 jit_solution(2915959265938014040)
XLA Ops:
  0.6 2.9 %enter.1 = (f32[480,128]{1,0:T(8,128)S(1)}, f32[480,128]{1,0:T(8,128)S(1)}, f32[96,128]{1,0:T(8,128)S(1)}, f32[400,128]{1,0:T(8,128)S(1)}, s32[1]{0:T(128)}, /*index=5*/s32[1]{0:T(128)}, s32[1]{0:T(128)}) custom-call(s32[3]{0:T(128)} %offsets_ref.7, f32[3840,128]{1,0:T(8,128)} %bitcast.6), custom_call_target="tpu_custom_call" | custom-call | tf_op jit(solution)/shard_map/enter/pallas_call | solution.py:411
  3.6 3.8 %collective-permute-start.27 = (f32[480,128]{1,0:T(8,128)S(1)}, f32[480,128]{1,0:T(8,128)S(1)}, u32[]{:S(2)}, u32[]{:S(2)}) collective-permute-start(f32[480,128]{1,0:T(8,128)S(1)} %get-tuple-element.320), channel_id=1, source_target_pairs={{0,4},{4,0},{8,12},{12,8},{16,20},{20,16},{24,28},{28,24},{32,36},... | collective-permute-start | bytes 737288 | tf_op jit(solution)/shard_map/ppermute | solution.py:319
  7.4 5.8 %collective-permute-start.28 = (f32[480,128]{1,0:T(8,128)S(1)}, f32[480,128]{1,0:T(8,128)S(1)}, u32[]{:S(2)}, u32[]{:S(2)}) collective-permute-start(f32[480,128]{1,0:T(8,128)S(1)} %get-tuple-element.321), channel_id=1, source_target_pairs={{0,124},{4,8},{8,4},{12,16},{16,12},{20,24},{24,20},{28,32},{32,28... | collective-permute-start | bytes 737288 | tf_op jit(solution)/shard_map/ppermute | solution.py:324
  13.9 11.5 %conditional.3 = (f32[3840,128]{1,0:T(8,128)}, f32[960,128]{1,0:T(8,128)S(1)}, f32[400,128]{1,0:T(8,128)S(1)}, f32[96,128]{1,0:T(8,128)}, f32[400,128]{1,0:T(8,128)}, /*index=5*/f32[400,128]{1,0:T(8,128)}) conditional(s32[]{:T(128)} %bitcast.3, (s32[48]{0:T(128)S(1)}, f32[128,128]{1,0:T(8,128)}, f32[3840,128]{1,0:T(8,128)S(1)}, ...), branch_computations={%region_0.0_spmd, %region_1.0_spmd, %region_2.0_spmd} | conditional | flops 20000000 | bytes 7733416 | solution.py:424
  13.9 1.3 %collective-permute-start.2 = (f32[400,128]{1,0:T(8,128)S(1)}, f32[400,128]{1,0:T(8,128)}, u32[]{:S(2)}, u32[]{:S(2)}) collective-permute-start(f32[400,128]{1,0:T(8,128)S(1)} %get-tuple-element.169), channel_id=1, source_target_pairs={{0,1},{1,0},{4,5},{5,4},{8,9},{9,8},{12,13},{13,12},{16,17},{17,16... | collective-permute-start | bytes 614408 | tf_op jit(solution)/shard_map/cond/branch_0_fun/ppermute | solution.py:315
  15.2 1.3 %collective-permute-start = (f32[96,128]{1,0:T(8,128)S(1)}, f32[96,128]{1,0:T(8,128)}, u32[]{:S(2)}, u32[]{:S(2)}) collective-permute-start(f32[96,128]{1,0:T(8,128)S(1)} %get-tuple-element.168), channel_id=1, source_target_pairs={{0,2},{2,0},{1,3},{3,1},{4,6},{6,4},{5,7},{7,5},{8,10},{10,8},{9,1... | collective-permute-start | bytes 147464 | tf_op jit(solution)/shard_map/cond/branch_0_fun/ppermute | solution.py:353
  16.5 5.7 %local0.3 = (f32[3840,128]{1,0:T(8,128)}, f32[960,128]{1,0:T(8,128)S(1)}, f32[400,128]{1,0:T(8,128)S(1)}) custom-call(s32[48]{0:T(128)S(1)} %get-tuple-element.162.pml_ref, f32[128,128]{1,0:T(8,128)} %get-tuple-element.163.band_ref, f32[3840,128]{1,0:T(8,128)S(1)} %get-tuple-element.164.q_ref), custom_call_target="tpu_custom_call" | custom-call | flops 20000000 | bytes 5898240 | tf_op jit(solution)/shard_map/cond/branch_0_fun/local0/pallas_call | solution.py:329
  22.2 2.9 %collective-permute-done = f32[96,128]{1,0:T(8,128)} collective-permute-done((f32[96,128]{1,0:T(8,128)S(1)}, f32[96,128]{1,0:T(8,128)}, u32[]{:S(2)}, u32[]{:S(2)}) %collective-permute-start) | collective-permute-done | bytes 49184 | tf_op jit(solution)/shard_map/cond/branch_0_fun/ppermute | solution.py:353
  25.4 1.7 %lead0.1 = (f32[480,128]{1,0:T(8,128)S(1)}, f32[480,128]{1,0:T(8,128)S(1)}, f32[400,128]{1,0:T(8,128)S(1)}) custom-call(s32[3]{0:T(128)S(1)} %copy-done.7, f32[960,128]{1,0:T(8,128)S(1)} %get-tuple-element.325.rim_ref, f32[400,128]{1,0:T(8,128)S(1)} %get-tuple-element.326.face_ref, f32[480,128]{1,0:T(8,128)S(1)} %collective-permute-done.27.east_ref, ...), custom_call_target="tpu_custom_call" | custom-call | tf_op jit(solution)/shard_map/lead0/pallas_call | solution.py:359
  27.2 8.1 %collective-permute-start.30 = (f32[480,128]{1,0:T(8,128)S(1)}, f32[480,128]{1,0:T(8,128)S(1)}, u32[]{:S(2)}, u32[]{:S(2)}) collective-permute-start(f32[480,128]{1,0:T(8,128)S(1)} %get-tuple-element.331), channel_id=1, source_target_pairs={{0,124},{4,8},{8,4},{12,16},{16,12},{20,24},{24,20},{28,32},{32,28... | collective-permute-start | bytes 737288 | tf_op jit(solution)/shard_map/ppermute | solution.py:324
  36.0 12.0 %conditional.4 = (f32[3840,128]{1,0:T(8,128)}, f32[3840,128]{1,0:T(8,128)S(1)}, f32[960,128]{1,0:T(8,128)S(1)}, f32[400,128]{1,0:T(8,128)S(1)}, f32[96,128]{1,0:...) conditional(s32[]{:T(128)} %bitcast.2, (s32[3]{0:T(128)S(1)}, f32[3840,128]{1,0:T(8,128)S(1)}, ...), branch_computations={%region_3.0_spmd, %region_4.0_spmd, %region_5.0_spmd} | conditional | flops 28000000 | bytes 15859916 | solution.py:428
  36.0 1.8 %collective-permute-start.14 = (f32[400,128]{1,0:T(8,128)S(1)}, f32[400,128]{1,0:T(8,128)}, u32[]{:S(2)}, u32[]{:S(2)}) collective-permute-start(f32[400,128]{1,0:T(8,128)S(1)} %get-tuple-element.219), channel_id=1, source_target_pairs={{0,5},{5,0},{4,9},{9,4},{8,13},{13,8},{12,17},{17,12},{16,21},{21,... | collective-permute-start | bytes 614408 | tf_op jit(solution)/shard_map/cond/branch_1_fun/ppermute | solution.py:315
  37.8 4.1 %finish0.4 = (f32[3840,128]{1,0:T(8,128)}, f32[3840,128]{1,0:T(8,128)S(1)}, f32[96,128]{1,0:T(8,128)S(1)}) custom-call(s32[3]{0:T(128)S(1)} %get-tuple-element.203.offsets_ref, f32[3840,128]{1,0:T(8,128)S(1)} %get-tuple-element.204.q_ref, f32[3840,128]{1,0:T(8,128)} %get-tuple-element.205.part_ref, f32[480,128]{1,0:T(8,128)S(1)} %get-tuple-element.206.east_ref, ...), custom_call_target="tpu_custom_call" | custom-call | flops 8000000 | bytes 7864320 | tf_op jit(solution)/shard_map/cond/branch_1_fun/finish0/pallas_call | solution.py:374
  42.3 5.3 %local1.4 = (f32[3840,128]{1,0:T(8,128)S(1)}, f32[960,128]{1,0:T(8,128)S(1)}, f32[400,128]{1,0:T(8,128)S(1)}) custom-call(s32[48]{0:T(128)S(1)} %get-tuple-element.212.pml_ref, f32[128,128]{1,0:T(8,128)S(1)} %copy-done.2, f32[3840,128]{1,0:T(8,128)} %get-tuple-element.372.q_ref, f32[3840,128]{1,0:T(8,128)S(1)} %get-tuple-element.214.refs_0_), custom_call_target="tpu_custom_call" | custom-call | flops 20000000 | bytes 5898240 | tf_op jit(solution)/shard_map/cond/branch_1_fun/local1/pallas_call | solution.py:329
  48.0 1.7 %lead1.1 = (f32[480,128]{1,0:T(8,128)S(1)}, f32[480,128]{1,0:T(8,128)S(1)}, f32[400,128]{1,0:T(8,128)S(1)}) custom-call(s32[3]{0:T(128)S(1)} %copy-done.7, f32[960,128]{1,0:T(8,128)S(1)} %get-tuple-element.335.rim_ref, f32[400,128]{1,0:T(8,128)S(1)} %get-tuple-element.336.face_ref, f32[480,128]{1,0:T(8,128)S(1)} %collective-permute-done.29.east_ref, ...), custom_call_target="tpu_custom_call" | custom-call | tf_op jit(solution)/shard_map/lead1/pallas_call | solution.py:359
  49.7 2.7 %collective-permute-start.31 = (f32[480,128]{1,0:T(8,128)S(1)}, f32[480,128]{1,0:T(8,128)S(1)}, u32[]{:S(2)}, u32[]{:S(2)}) collective-permute-start(f32[480,128]{1,0:T(8,128)S(1)} %get-tuple-element.340), channel_id=1, source_target_pairs={{0,4},{4,0},{8,12},{12,8},{16,20},{20,16},{24,28},{28,24},{32,36},... | collective-permute-start | bytes 737288 | tf_op jit(solution)/shard_map/ppermute | solution.py:319
  52.5 4.6 %collective-permute-start.32 = (f32[480,128]{1,0:T(8,128)S(1)}, f32[480,128]{1,0:T(8,128)S(1)}, u32[]{:S(2)}, u32[]{:S(2)}) collective-permute-start(f32[480,128]{1,0:T(8,128)S(1)} %get-tuple-element.341), channel_id=1, source_target_pairs={{0,124},{4,8},{8,4},{12,16},{16,12},{20,24},{24,20},{28,32},{32,28... | collective-permute-start | bytes 737288 | tf_op jit(solution)/shard_map/ppermute | solution.py:324
  57.7 15.1 %conditional.5 = (f32[3840,128]{1,0:T(8,128)}, f32[3840,128]{1,0:T(8,128)S(1)}, f32[96,128]{1,0:T(8,128)}, f32[400,128]{1,0:T(8,128)}, f32[400,128]{1,0:T(8,128)}) conditional(s32[]{:T(128)} %bitcast.1, (s32[3]{0:T(128)S(1)}, f32[3840,128]{1,0:T(8,128)}, f32[3840,128]{1,0:T(8,128)S(1)}, f32[480,128]{1,0:T(8,128)S(1)}, ...), branch_computations={%region_6.0_spmd, %region_7.0_spmd, %region_8.0_spmd} | conditional | flops 28000000 | bytes 15859900 | solution.py:428
  57.7 0.6 collective-permute-start.26
  58.3 4.1 %finish1.5 = (f32[3840,128]{1,0:T(8,128)}, f32[3840,128]{1,0:T(8,128)S(1)}, f32[96,128]{1,0:T(8,128)S(1)}) custom-call(s32[3]{0:T(128)S(1)} %get-tuple-element.265.offsets_ref, f32[3840,128]{1,0:T(8,128)} %get-tuple-element.266.q_ref, f32[3840,128]{1,0:T(8,128)S(1)} %get-tuple-element.267.part_ref, f32[480,128]{1,0:T(8,128)S(1)} %get-tuple-element.268.east_ref, ...), custom_call_target="tpu_custom_call" | custom-call | flops 8000000 | bytes 7864320 | tf_op jit(solution)/shard_map/cond/branch_2_fun/finish1/pallas_call | solution.py:374
  62.5 1.0 %collective-permute-start.24 = (f32[96,128]{1,0:T(8,128)S(1)}, f32[96,128]{1,0:T(8,128)}, u32[]{:S(2)}, u32[]{:S(2)}) collective-permute-start(f32[96,128]{1,0:T(8,128)S(1)} %get-tuple-element.277), channel_id=1, source_target_pairs={{0,2},{2,0},{1,3},{3,1},{4,6},{6,4},{5,7},{7,5},{8,10},{10,8},{9,1... | collective-permute-start | bytes 147464 | tf_op jit(solution)/shard_map/cond/branch_2_fun/ppermute | solution.py:353
  63.5 4.9 %local2.5 = f32[3840,128]{1,0:T(8,128)S(1)} custom-call(s32[48]{0:T(128)S(1)} %get-tuple-element.274.pml_ref, f32[128,128]{1,0:T(8,128)S(1)} %copy-done.6, f32[3840,128]{1,0:T(8,128)} %get-tuple-element.396.q_ref, f32[3840,128]{1,0:T(8,128)S(1)} %get-tuple-element.276.refs_0_), custom_call_target="tpu_custom_call" | custom-call | flops 20000000 | bytes 5898240 | tf_op jit(solution)/shard_map/cond/branch_2_fun/local2/pallas_call | solution.py:329
  68.9 4.0 %collective-permute-done.25 = f32[400,128]{1,0:T(8,128)} collective-permute-done((f32[400,128]{1,0:T(8,128)S(1)}, f32[400,128]{1,0:T(8,128)}, u32[]{:S(2)}, u32[]{:S(2)}) %collective-permute-start.25) | collective-permute-done | bytes 204832 | tf_op jit(solution)/shard_map/cond/branch_2_fun/ppermute | solution.py:315
  72.8 4.6 %finish2.1 = (f32[3840,128]{1,0:T(8,128)}, f32[3840,128]{1,0:T(8,128)}) custom-call(s32[3]{0:T(128)S(1)} %copy-done.7, f32[3840,128]{1,0:T(8,128)} %get-tuple-element.338.q_ref, f32[3840,128]{1,0:T(8,128)S(1)} %get-tuple-element.339.part_ref, f32[480,128]{1,0:T(8,128)S(1)} %collective-permute-done.31.east_ref, ...), custom_call_target="tpu_custom_call" | custom-call | flops 8000000 | bytes 7864320 | tf_op jit(solution)/shard_map/finish2/pallas_call | solution.py:374
  (28 shorter events, 1.2 us)
Async XLA Ops:
  0.6 13.2 %copy-start = (f32[5,48,16,128]{3,2,1,0:T(8,128)S(1)}, f32[5,48,16,128]{3,2,1,0:T(8,128)}, u32[]{:S(2)}) copy-start(f32[5,48,16,128]{3,2,1,0:T(8,128)} %param.21) | copy-start | bytes 5898244
  0.6 13.2 %copy-start.8 = (s32[48]{0:T(128)S(1)}, s32[48]{0:T(128)}, u32[]{:S(2)}) copy-start(s32[48]{0:T(128)} %param.23) | copy-start | bytes 580
  3.6 21.8 %collective-permute-start.27 = (f32[480,128]{1,0:T(8,128)S(1)}, f32[480,128]{1,0:T(8,128)S(1)}, u32[]{:S(2)}, u32[]{:S(2)}) collective-permute-start(f32[480,128]{1,0:T(8,128)S(1)} %get-tuple-element.320), channel_id=1, source_target_pairs={{0,4},{4,0},{8,12},{12,8},{16,20},{20,16},{24,28},{28,24},{32,36},... | collective-permute-start | bytes 737288 | tf_op jit(solution)/shard_map/ppermute | solution.py:319
  7.4 18.0 %collective-permute-start.28 = (f32[480,128]{1,0:T(8,128)S(1)}, f32[480,128]{1,0:T(8,128)S(1)}, u32[]{:S(2)}, u32[]{:S(2)}) collective-permute-start(f32[480,128]{1,0:T(8,128)S(1)} %get-tuple-element.321), channel_id=1, source_target_pairs={{0,124},{4,8},{8,4},{12,16},{16,12},{20,24},{24,20},{28,32},{32,28... | collective-permute-start | bytes 737288 | tf_op jit(solution)/shard_map/ppermute | solution.py:324
  13.9 11.5 %copy-start.7 = (s32[3]{0:T(128)S(1)}, s32[3]{0:T(128)}, u32[]{:S(2)}) copy-start(s32[3]{0:T(128)} %offsets_ref.7) | copy-start | bytes 40
  13.9 11.3 %collective-permute-start.2 = (f32[400,128]{1,0:T(8,128)S(1)}, f32[400,128]{1,0:T(8,128)}, u32[]{:S(2)}, u32[]{:S(2)}) collective-permute-start(f32[400,128]{1,0:T(8,128)S(1)} %get-tuple-element.169), channel_id=1, source_target_pairs={{0,1},{1,0},{4,5},{5,4},{8,9},{9,8},{12,13},{13,12},{16,17},{17,16... | collective-permute-start | bytes 614408 | tf_op jit(solution)/shard_map/cond/branch_0_fun/ppermute | solution.py:315
  15.2 10.2 %collective-permute-start.1 = (f32[400,128]{1,0:T(8,128)S(1)}, f32[400,128]{1,0:T(8,128)}, u32[]{:S(2)}, u32[]{:S(2)}) collective-permute-start(f32[400,128]{1,0:T(8,128)S(1)} %get-tuple-element.169), channel_id=1, source_target_pairs={{0,125},{125,0},{4,1},{1,4},{8,5},{5,8},{12,9},{9,12},{16,13},{13,... | collective-permute-start | bytes 614408 | tf_op jit(solution)/shard_map/cond/branch_0_fun/ppermute | solution.py:315
  15.2 10.0 %collective-permute-start = (f32[96,128]{1,0:T(8,128)S(1)}, f32[96,128]{1,0:T(8,128)}, u32[]{:S(2)}, u32[]{:S(2)}) collective-permute-start(f32[96,128]{1,0:T(8,128)S(1)} %get-tuple-element.168), channel_id=1, source_target_pairs={{0,2},{2,0},{1,3},{3,1},{4,6},{6,4},{5,7},{7,5},{8,10},{10,8},{9,1... | collective-permute-start | bytes 147464 | tf_op jit(solution)/shard_map/cond/branch_0_fun/ppermute | solution.py:353
  27.1 20.9 %collective-permute-start.29 = (f32[480,128]{1,0:T(8,128)S(1)}, f32[480,128]{1,0:T(8,128)S(1)}, u32[]{:S(2)}, u32[]{:S(2)}) collective-permute-start(f32[480,128]{1,0:T(8,128)S(1)} %get-tuple-element.330), channel_id=1, source_target_pairs={{0,4},{4,0},{8,12},{12,8},{16,20},{20,16},{24,28},{28,24},{32,36},... | collective-permute-start | bytes 737288 | tf_op jit(solution)/shard_map/ppermute | solution.py:319
  27.2 20.8 %collective-permute-start.30 = (f32[480,128]{1,0:T(8,128)S(1)}, f32[480,128]{1,0:T(8,128)S(1)}, u32[]{:S(2)}, u32[]{:S(2)}) collective-permute-start(f32[480,128]{1,0:T(8,128)S(1)} %get-tuple-element.331), channel_id=1, source_target_pairs={{0,124},{4,8},{8,4},{12,16},{16,12},{20,24},{24,20},{28,32},{32,28... | collective-permute-start | bytes 737288 | tf_op jit(solution)/shard_map/ppermute | solution.py:324
  36.0 11.6 %collective-permute-start.14 = (f32[400,128]{1,0:T(8,128)S(1)}, f32[400,128]{1,0:T(8,128)}, u32[]{:S(2)}, u32[]{:S(2)}) collective-permute-start(f32[400,128]{1,0:T(8,128)S(1)} %get-tuple-element.219), channel_id=1, source_target_pairs={{0,5},{5,0},{4,9},{9,4},{8,13},{13,8},{12,17},{17,12},{16,21},{21,... | collective-permute-start | bytes 614408 | tf_op jit(solution)/shard_map/cond/branch_1_fun/ppermute | solution.py:315
  37.8 9.8 %collective-permute-start.13 = (f32[400,128]{1,0:T(8,128)S(1)}, f32[400,128]{1,0:T(8,128)}, u32[]{:S(2)}, u32[]{:S(2)}) collective-permute-start(f32[400,128]{1,0:T(8,128)S(1)} %get-tuple-element.219), channel_id=1, source_target_pairs={{0,1},{1,0},{4,5},{5,4},{8,9},{9,8},{12,13},{13,12},{16,17},{17,16... | collective-permute-start | bytes 614408 | tf_op jit(solution)/shard_map/cond/branch_1_fun/ppermute | solution.py:315
  37.8 4.5 %copy-start.2 = (f32[128,128]{1,0:T(8,128)S(1)}, f32[128,128]{1,0:T(8,128)}, u32[]{:S(2)}) copy-start(f32[128,128]{1,0:T(8,128)} %get-tuple-element.213.band_ref) | copy-start | bytes 196612 | tf_op jit(solution)/shard_map/cond
  41.9 5.7 %collective-permute-start.12 = (f32[96,128]{1,0:T(8,128)S(1)}, f32[96,128]{1,0:T(8,128)}, u32[]{:S(2)}, u32[]{:S(2)}) collective-permute-start(f32[96,128]{1,0:T(8,128)S(1)} %get-tuple-element.218), channel_id=1, source_target_pairs={{0,2},{2,0},{1,3},{3,1},{4,6},{6,4},{5,7},{7,5},{8,10},{10,8},{9,1... | collective-permute-start | bytes 147464 | tf_op jit(solution)/shard_map/cond/branch_1_fun/ppermute | solution.py:353
  49.7 23.1 %collective-permute-start.31 = (f32[480,128]{1,0:T(8,128)S(1)}, f32[480,128]{1,0:T(8,128)S(1)}, u32[]{:S(2)}, u32[]{:S(2)}) collective-permute-start(f32[480,128]{1,0:T(8,128)S(1)} %get-tuple-element.340), channel_id=1, source_target_pairs={{0,4},{4,0},{8,12},{12,8},{16,20},{20,16},{24,28},{28,24},{32,36},... | collective-permute-start | bytes 737288 | tf_op jit(solution)/shard_map/ppermute | solution.py:319
  52.5 20.4 %collective-permute-start.32 = (f32[480,128]{1,0:T(8,128)S(1)}, f32[480,128]{1,0:T(8,128)S(1)}, u32[]{:S(2)}, u32[]{:S(2)}) collective-permute-start(f32[480,128]{1,0:T(8,128)S(1)} %get-tuple-element.341), channel_id=1, source_target_pairs={{0,124},{4,8},{8,4},{12,16},{16,12},{20,24},{24,20},{28,32},{32,28... | collective-permute-start | bytes 737288 | tf_op jit(solution)/shard_map/ppermute | solution.py:324
  57.7 11.1 %collective-permute-start.26 = (f32[400,128]{1,0:T(8,128)S(1)}, f32[400,128]{1,0:T(8,128)}, u32[]{:S(2)}, u32[]{:S(2)}) collective-permute-start(f32[400,128]{1,0:T(8,128)S(1)} %get-tuple-element.278), channel_id=1, source_target_pairs={{0,69},{69,0},{4,73},{73,4},{8,77},{77,8},{12,81},{81,12},{16,85},... | collective-permute-start | bytes 614408 | tf_op jit(solution)/shard_map/cond/branch_2_fun/ppermute | solution.py:315
  58.3 14.5 %collective-permute-start.25 = (f32[400,128]{1,0:T(8,128)S(1)}, f32[400,128]{1,0:T(8,128)}, u32[]{:S(2)}, u32[]{:S(2)}) collective-permute-start(f32[400,128]{1,0:T(8,128)S(1)} %get-tuple-element.278), channel_id=1, source_target_pairs={{0,65},{65,0},{4,69},{69,4},{8,73},{73,8},{12,77},{77,12},{16,81},... | collective-permute-start | bytes 614408 | tf_op jit(solution)/shard_map/cond/branch_2_fun/ppermute | solution.py:315
  58.3 5.1 %copy-start.6 = (f32[128,128]{1,0:T(8,128)S(1)}, f32[128,128]{1,0:T(8,128)}, u32[]{:S(2)}) copy-start(f32[128,128]{1,0:T(8,128)} %get-tuple-element.275.band_ref) | copy-start | bytes 196612 | tf_op jit(solution)/shard_map/cond
  62.5 6.0 %collective-permute-start.24 = (f32[96,128]{1,0:T(8,128)S(1)}, f32[96,128]{1,0:T(8,128)}, u32[]{:S(2)}, u32[]{:S(2)}) collective-permute-start(f32[96,128]{1,0:T(8,128)S(1)} %get-tuple-element.277), channel_id=1, source_target_pairs={{0,2},{2,0},{1,3},{3,1},{4,6},{6,4},{5,7},{7,5},{8,10},{10,8},{9,1... | collective-permute-start | bytes 147464 | tf_op jit(solution)/shard_map/cond/branch_2_fun/ppermute | solution.py:353

commit v5 on v4

--- a/solution.py
+++ b/solution.py
@@ -132,7 +132,7 @@
             total = term if total is None else total + term
         return total
 
-    B = 8
+    B = 12
 
     def step(n, carry):
         a0 = n * B
@@ -294,7 +294,7 @@
                 new_ref[rows, :] = q_ref[rows, :] + b * value
         return carry
 
-    lax.fori_loop(0, FIELD // GROUP, step, 0)
+    lax.fori_loop(0, FIELD // GROUP, step, 0, unroll=2)
 
     for a, extra in interface_terms(section, offsets_ref, own_ref, next_ref, faces, range(F)):
         for f in range(F):

time: 77.9 us -> 76.9 us (0.987)
  starting transfers between devices: 31.5 us -> 33.1 us
  Pallas kernels: 35.1 us -> 33.9 us
  waiting for transfers between devices: 7.61 us -> 6.47 us
    ppermute x3, waiting for transfers between devices: 2.94 us -> 0.01 us  [send_rad(): return lax.ppermute(rad, 'rad', [(0, 1), (1, 0)])]
    ppermute x6, starting transfers between devices: 3.67 us -> 5.84 us  [swap_faces(): return lax.ppermute(face, ('circ', 'half'), pairs)]
    ppermute x6, waiting for transfers between devices: 4.65 us -> 6.45 us  [swap_faces(): return lax.ppermute(face, ('circ', 'half'), pairs)]
    ppermute x3, starting transfers between devices: 18.5 us -> 19.4 us  [send_odd(): lax.ppermute(odd, 'circ', [(i, (i + (1 if i % 2 else -1)) % count) for i...]
    pallas_call x3, Pallas kernels: 12.8 us -> 12 us  [finish(): pl.pallas_call(functools.partial(finish_kernel, section, last), out_shape...]
    ppermute x3, starting transfers between devices: 6.62 us -> 5.79 us  [send_east(): lax.ppermute(east, 'circ', [(i, i ^ 1) for i in range(lax.axis_size('circ...]
  transfers between devices with their start and end apart: 15 -> 15, of which waited for: 4 -> 3; matrix products, arithmetic and copies ran while one was open for 0% -> 0% of each run, Pallas kernels for 31% -> 30%
where the time goes in v5:
time: 76.9 us; the launch traced here: 76.5 us
  Pallas kernels  33.9 us (44%)
  starting transfers between devices  33.1 us (43%)
  waiting for transfers between devices  6.47 us (8%)
  between operations  2.69 us (3%)
    ppermute x3, starting transfers between devices, send_odd(): lax.ppermute(odd, 'circ', [(i, (i + (1 if i % 2 else -1)) % count) for i...  19.4 us
    pallas_call x3, Pallas kernels, local_terms(): pl.pallas_call(functools.partial(local_kernel, section), out_shape=[FIELD...  15.5 us
    pallas_call x3, Pallas kernels, finish(): pl.pallas_call(functools.partial(finish_kernel, section, last), out_shape...  12 us
    ppermute x6, waiting for transfers between devices, swap_faces(): return lax.ppermute(face, ('circ', 'half'), pairs)  6.45 us
    ppermute x6, starting transfers between devices, swap_faces(): return lax.ppermute(face, ('circ', 'half'), pairs)  5.84 us
    ppermute x3, starting transfers between devices, send_east(): lax.ppermute(east, 'circ', [(i, i ^ 1) for i in range(lax.axis_size('circ...  5.79 us
    pallas_call x2, Pallas kernels, lead(): pl.pallas_call(functools.partial(lead_kernel, section), out_shape=[RIM, R...  3.41 us
    pallas_call x1, Pallas kernels, body(): pl.pallas_call(enter_kernel, out_shape=[RIM, RIM, RAD, FACE] + [flag] * S...  2.94 us
  transfers between devices with their start and end apart: 15, of which 3 were waited for; matrix products, arithmetic and copies ran while one was open for 0% of the time, Pallas kernels for 30%

profile of v5, /device:TPU:1, one launch (start us, length us, event | category | flops | bytes accessed | tf_op | source)
XLA Modules:
  0.0 76.5 jit_solution(18397972355012837278)
XLA Ops:
  0.6 2.9 %enter.1 = (f32[480,128]{1,0:T(8,128)S(1)}, f32[480,128]{1,0:T(8,128)S(1)}, f32[96,128]{1,0:T(8,128)S(1)}, f32[400,128]{1,0:T(8,128)S(1)}, s32[1]{0:T(128)}, /*index=5*/s32[1]{0:T(128)}, s32[1]{0:T(128)}) custom-call(s32[3]{0:T(128)} %offsets_ref.7, f32[3840,128]{1,0:T(8,128)} %bitcast.6), custom_call_target="tpu_custom_call" | custom-call | tf_op jit(solution)/shard_map/enter/pallas_call | solution.py:411
  3.6 3.8 %collective-permute-start.27 = (f32[480,128]{1,0:T(8,128)S(1)}, f32[480,128]{1,0:T(8,128)S(1)}, u32[]{:S(2)}, u32[]{:S(2)}) collective-permute-start(f32[480,128]{1,0:T(8,128)S(1)} %get-tuple-element.320), channel_id=1, source_target_pairs={{0,4},{4,0},{8,12},{12,8},{16,20},{20,16},{24,28},{28,24},{32,36},... | collective-permute-start | bytes 737288 | tf_op jit(solution)/shard_map/ppermute | solution.py:319
  7.4 5.8 %collective-permute-start.28 = (f32[480,128]{1,0:T(8,128)S(1)}, f32[480,128]{1,0:T(8,128)S(1)}, u32[]{:S(2)}, u32[]{:S(2)}) collective-permute-start(f32[480,128]{1,0:T(8,128)S(1)} %get-tuple-element.321), channel_id=1, source_target_pairs={{0,124},{4,8},{8,4},{12,16},{16,12},{20,24},{24,20},{28,32},{32,28... | collective-permute-start | bytes 737288 | tf_op jit(solution)/shard_map/ppermute | solution.py:324
  13.9 11.2 %conditional.3 = (f32[3840,128]{1,0:T(8,128)}, f32[960,128]{1,0:T(8,128)S(1)}, f32[400,128]{1,0:T(8,128)S(1)}, f32[96,128]{1,0:T(8,128)}, f32[400,128]{1,0:T(8,128)}, /*index=5*/f32[400,128]{1,0:T(8,128)}) conditional(s32[]{:T(128)} %bitcast.3, (s32[48]{0:T(128)S(1)}, f32[128,128]{1,0:T(8,128)}, f32[3840,128]{1,0:T(8,128)S(1)}, ...), branch_computations={%region_0.0_spmd, %region_1.0_spmd, %region_2.0_spmd} | conditional | flops 20000000 | bytes 7733416 | solution.py:424
  13.9 2.6 %collective-permute-start.5 = (f32[400,128]{1,0:T(8,128)S(1)}, f32[400,128]{1,0:T(8,128)}, u32[]{:S(2)}, u32[]{:S(2)}) collective-permute-start(f32[400,128]{1,0:T(8,128)S(1)} %get-tuple-element.177), channel_id=1, source_target_pairs={{0,5},{5,0},{4,9},{9,4},{8,13},{13,8},{12,17},{17,12},{16,21},{21,... | collective-permute-start | bytes 614408 | tf_op jit(solution)/shard_map/cond/branch_1_fun/ppermute | solution.py:315
  16.9 5.6 %local0.4 = (f32[3840,128]{1,0:T(8,128)}, f32[960,128]{1,0:T(8,128)S(1)}, f32[400,128]{1,0:T(8,128)S(1)}) custom-call(s32[48]{0:T(128)S(1)} %get-tuple-element.170.pml_ref, f32[128,128]{1,0:T(8,128)} %get-tuple-element.171.band_ref, f32[3840,128]{1,0:T(8,128)S(1)} %get-tuple-element.172.q_ref), custom_call_target="tpu_custom_call" | custom-call | flops 20000000 | bytes 5898240 | tf_op jit(solution)/shard_map/cond/branch_1_fun/local0/pallas_call | solution.py:329
  22.5 2.6 %collective-permute-done.5 = f32[400,128]{1,0:T(8,128)} collective-permute-done((f32[400,128]{1,0:T(8,128)S(1)}, f32[400,128]{1,0:T(8,128)}, u32[]{:S(2)}, u32[]{:S(2)}) %collective-permute-start.5) | collective-permute-done | bytes 204832 | tf_op jit(solution)/shard_map/cond/branch_1_fun/ppermute | solution.py:315
  25.1 1.7 %lead0.1 = (f32[480,128]{1,0:T(8,128)S(1)}, f32[480,128]{1,0:T(8,128)S(1)}, f32[400,128]{1,0:T(8,128)S(1)}) custom-call(s32[3]{0:T(128)S(1)} %copy-done.7, f32[960,128]{1,0:T(8,128)S(1)} %get-tuple-element.325.rim_ref, f32[400,128]{1,0:T(8,128)S(1)} %get-tuple-element.326.face_ref, f32[480,128]{1,0:T(8,128)S(1)} %collective-permute-done.27.east_ref, ...), custom_call_target="tpu_custom_call" | custom-call | tf_op jit(solution)/shard_map/lead0/pallas_call | solution.py:359
  26.8 1.9 %collective-permute-start.29 = (f32[480,128]{1,0:T(8,128)S(1)}, f32[480,128]{1,0:T(8,128)S(1)}, u32[]{:S(2)}, u32[]{:S(2)}) collective-permute-start(f32[480,128]{1,0:T(8,128)S(1)} %get-tuple-element.330), channel_id=1, source_target_pairs={{0,4},{4,0},{8,12},{12,8},{16,20},{20,16},{24,28},{28,24},{32,36},... | collective-permute-start | bytes 737288 | tf_op jit(solution)/shard_map/ppermute | solution.py:319
  28.7 5.8 %collective-permute-start.30 = (f32[480,128]{1,0:T(8,128)S(1)}, f32[480,128]{1,0:T(8,128)S(1)}, u32[]{:S(2)}, u32[]{:S(2)}) collective-permute-start(f32[480,128]{1,0:T(8,128)S(1)} %get-tuple-element.331), channel_id=1, source_target_pairs={{0,124},{4,8},{8,4},{12,16},{16,12},{20,24},{24,20},{28,32},{32,28... | collective-permute-start | bytes 737288 | tf_op jit(solution)/shard_map/ppermute | solution.py:324
  35.1 12.5 %conditional.4 = (f32[3840,128]{1,0:T(8,128)}, f32[3840,128]{1,0:T(8,128)S(1)}, f32[960,128]{1,0:T(8,128)S(1)}, f32[400,128]{1,0:T(8,128)S(1)}, f32[96,128]{1,0:...) conditional(s32[]{:T(128)} %bitcast.2, (s32[3]{0:T(128)S(1)}, f32[3840,128]{1,0:T(8,128)S(1)}, ...), branch_computations={%region_3.0_spmd, %region_4.0_spmd, %region_5.0_spmd} | conditional | flops 28000000 | bytes 15859916 | solution.py:428
  35.1 2.2 %collective-permute-start.11 = (f32[400,128]{1,0:T(8,128)S(1)}, f32[400,128]{1,0:T(8,128)}, u32[]{:S(2)}, u32[]{:S(2)}) collective-permute-start(f32[400,128]{1,0:T(8,128)S(1)} %get-tuple-element.202), channel_id=1, source_target_pairs={{0,1},{1,0},{4,5},{5,4},{8,9},{9,8},{12,13},{13,12},{16,17},{17,16... | collective-permute-start | bytes 614408 | tf_op jit(solution)/shard_map/cond/branch_0_fun/ppermute | solution.py:315
  37.3 3.8 %finish0.3 = (f32[3840,128]{1,0:T(8,128)}, f32[3840,128]{1,0:T(8,128)S(1)}, f32[96,128]{1,0:T(8,128)S(1)}) custom-call(s32[3]{0:T(128)S(1)} %get-tuple-element.186.offsets_ref, f32[3840,128]{1,0:T(8,128)S(1)} %get-tuple-element.187.q_ref, f32[3840,128]{1,0:T(8,128)} %get-tuple-element.188.part_ref, f32[480,128]{1,0:T(8,128)S(1)} %get-tuple-element.189.east_ref, ...), custom_call_target="tpu_custom_call" | custom-call | flops 8000000 | bytes 7864320 | tf_op jit(solution)/shard_map/cond/branch_0_fun/finish0/pallas_call | solution.py:374
  41.1 1.1 %collective-permute-start.9 = (f32[96,128]{1,0:T(8,128)S(1)}, f32[96,128]{1,0:T(8,128)}, u32[]{:S(2)}, u32[]{:S(2)}) collective-permute-start(f32[96,128]{1,0:T(8,128)S(1)} %get-tuple-element.201), channel_id=1, source_target_pairs={{0,2},{2,0},{1,3},{3,1},{4,6},{6,4},{5,7},{7,5},{8,10},{10,8},{9,1... | collective-permute-start | bytes 147464 | tf_op jit(solution)/shard_map/cond/branch_0_fun/ppermute | solution.py:353
  42.2 5.2 %local1.3 = (f32[3840,128]{1,0:T(8,128)S(1)}, f32[960,128]{1,0:T(8,128)S(1)}, f32[400,128]{1,0:T(8,128)S(1)}) custom-call(s32[48]{0:T(128)S(1)} %get-tuple-element.195.pml_ref, f32[128,128]{1,0:T(8,128)S(1)} %copy-done.1, f32[3840,128]{1,0:T(8,128)} %get-tuple-element.365.q_ref, f32[3840,128]{1,0:T(8,128)S(1)} %get-tuple-element.197.refs_0_), custom_call_target="tpu_custom_call" | custom-call | flops 20000000 | bytes 5898240 | tf_op jit(solution)/shard_map/cond/branch_0_fun/local1/pallas_call | solution.py:329
  47.6 1.7 %lead1.1 = (f32[480,128]{1,0:T(8,128)S(1)}, f32[480,128]{1,0:T(8,128)S(1)}, f32[400,128]{1,0:T(8,128)S(1)}) custom-call(s32[3]{0:T(128)S(1)} %copy-done.7, f32[960,128]{1,0:T(8,128)S(1)} %get-tuple-element.335.rim_ref, f32[400,128]{1,0:T(8,128)S(1)} %get-tuple-element.336.face_ref, f32[480,128]{1,0:T(8,128)S(1)} %collective-permute-done.29.east_ref, ...), custom_call_target="tpu_custom_call" | custom-call | tf_op jit(solution)/shard_map/lead1/pallas_call | solution.py:359
  49.5 7.9 %collective-permute-start.32 = (f32[480,128]{1,0:T(8,128)S(1)}, f32[480,128]{1,0:T(8,128)S(1)}, u32[]{:S(2)}, u32[]{:S(2)}) collective-permute-start(f32[480,128]{1,0:T(8,128)S(1)} %get-tuple-element.341), channel_id=1, source_target_pairs={{0,124},{4,8},{8,4},{12,16},{16,12},{20,24},{24,20},{28,32},{32,28... | collective-permute-start | bytes 737288 | tf_op jit(solution)/shard_map/ppermute | solution.py:324
  57.9 14.2 %conditional.5 = (f32[3840,128]{1,0:T(8,128)}, f32[3840,128]{1,0:T(8,128)S(1)}, f32[96,128]{1,0:T(8,128)}, f32[400,128]{1,0:T(8,128)}, f32[400,128]{1,0:T(8,128)}) conditional(s32[]{:T(128)} %bitcast.1, (s32[3]{0:T(128)S(1)}, f32[3840,128]{1,0:T(8,128)}, f32[3840,128]{1,0:T(8,128)S(1)}, f32[480,128]{1,0:T(8,128)S(1)}, ...), branch_computations={%region_6.0_spmd, %region_7.0_spmd, %region_8.0_spmd} | conditional | flops 28000000 | bytes 15859900 | solution.py:428
  58.0 1.0 %collective-permute-start.26 = (f32[400,128]{1,0:T(8,128)S(1)}, f32[400,128]{1,0:T(8,128)}, u32[]{:S(2)}, u32[]{:S(2)}) collective-permute-start(f32[400,128]{1,0:T(8,128)S(1)} %get-tuple-element.278), channel_id=1, source_target_pairs={{0,69},{69,0},{4,73},{73,4},{8,77},{77,8},{12,81},{81,12},{16,85},... | collective-permute-start | bytes 614408 | tf_op jit(solution)/shard_map/cond/branch_2_fun/ppermute | solution.py:315
  59.0 3.8 %finish1.5 = (f32[3840,128]{1,0:T(8,128)}, f32[3840,128]{1,0:T(8,128)S(1)}, f32[96,128]{1,0:T(8,128)S(1)}) custom-call(s32[3]{0:T(128)S(1)} %get-tuple-element.265.offsets_ref, f32[3840,128]{1,0:T(8,128)} %get-tuple-element.266.q_ref, f32[3840,128]{1,0:T(8,128)S(1)} %get-tuple-element.267.part_ref, f32[480,128]{1,0:T(8,128)S(1)} %get-tuple-element.268.east_ref, ...), custom_call_target="tpu_custom_call" | custom-call | flops 8000000 | bytes 7864320 | tf_op jit(solution)/shard_map/cond/branch_2_fun/finish1/pallas_call | solution.py:374
  63.4 4.8 %local2.5 = f32[3840,128]{1,0:T(8,128)S(1)} custom-call(s32[48]{0:T(128)S(1)} %get-tuple-element.274.pml_ref, f32[128,128]{1,0:T(8,128)S(1)} %copy-done.6, f32[3840,128]{1,0:T(8,128)} %get-tuple-element.396.q_ref, f32[3840,128]{1,0:T(8,128)S(1)} %get-tuple-element.276.refs_0_), custom_call_target="tpu_custom_call" | custom-call | flops 20000000 | bytes 5898240 | tf_op jit(solution)/shard_map/cond/branch_2_fun/local2/pallas_call | solution.py:329
  68.3 0.9 %collective-permute-done.26 = f32[400,128]{1,0:T(8,128)} collective-permute-done((f32[400,128]{1,0:T(8,128)S(1)}, f32[400,128]{1,0:T(8,128)}, u32[]{:S(2)}, u32[]{:S(2)}) %collective-permute-start.26) | collective-permute-done | bytes 204832 | tf_op jit(solution)/shard_map/cond/branch_2_fun/ppermute | solution.py:315
  69.2 2.9 %collective-permute-done.25 = f32[400,128]{1,0:T(8,128)} collective-permute-done((f32[400,128]{1,0:T(8,128)S(1)}, f32[400,128]{1,0:T(8,128)}, u32[]{:S(2)}, u32[]{:S(2)}) %collective-permute-start.25) | collective-permute-done | bytes 204832 | tf_op jit(solution)/shard_map/cond/branch_2_fun/ppermute | solution.py:315
  72.1 4.3 %finish2.1 = (f32[3840,128]{1,0:T(8,128)}, f32[3840,128]{1,0:T(8,128)}) custom-call(s32[3]{0:T(128)S(1)} %copy-done.7, f32[3840,128]{1,0:T(8,128)} %get-tuple-element.338.q_ref, f32[3840,128]{1,0:T(8,128)S(1)} %get-tuple-element.339.part_ref, f32[480,128]{1,0:T(8,128)S(1)} %collective-permute-done.31.east_ref, ...), custom_call_target="tpu_custom_call" | custom-call | flops 8000000 | bytes 7864320 | tf_op jit(solution)/shard_map/finish2/pallas_call | solution.py:374
  (28 shorter events, 1.1 us)
Async XLA Ops:
  0.6 13.2 %copy-start = (f32[5,48,16,128]{3,2,1,0:T(8,128)S(1)}, f32[5,48,16,128]{3,2,1,0:T(8,128)}, u32[]{:S(2)}) copy-start(f32[5,48,16,128]{3,2,1,0:T(8,128)} %param.21) | copy-start | bytes 5898244
  0.6 13.2 %copy-start.8 = (s32[48]{0:T(128)S(1)}, s32[48]{0:T(128)}, u32[]{:S(2)}) copy-start(s32[48]{0:T(128)} %param.23) | copy-start | bytes 580
  3.6 21.5 %collective-permute-start.27 = (f32[480,128]{1,0:T(8,128)S(1)}, f32[480,128]{1,0:T(8,128)S(1)}, u32[]{:S(2)}, u32[]{:S(2)}) collective-permute-start(f32[480,128]{1,0:T(8,128)S(1)} %get-tuple-element.320), channel_id=1, source_target_pairs={{0,4},{4,0},{8,12},{12,8},{16,20},{20,16},{24,28},{28,24},{32,36},... | collective-permute-start | bytes 737288 | tf_op jit(solution)/shard_map/ppermute | solution.py:319
  7.4 17.7 %collective-permute-start.28 = (f32[480,128]{1,0:T(8,128)S(1)}, f32[480,128]{1,0:T(8,128)S(1)}, u32[]{:S(2)}, u32[]{:S(2)}) collective-permute-start(f32[480,128]{1,0:T(8,128)S(1)} %get-tuple-element.321), channel_id=1, source_target_pairs={{0,124},{4,8},{8,4},{12,16},{16,12},{20,24},{24,20},{28,32},{32,28... | collective-permute-start | bytes 737288 | tf_op jit(solution)/shard_map/ppermute | solution.py:324
  13.9 11.2 %copy-start.7 = (s32[3]{0:T(128)S(1)}, s32[3]{0:T(128)}, u32[]{:S(2)}) copy-start(s32[3]{0:T(128)} %offsets_ref.7) | copy-start | bytes 40
  13.9 11.2 %collective-permute-start.5 = (f32[400,128]{1,0:T(8,128)S(1)}, f32[400,128]{1,0:T(8,128)}, u32[]{:S(2)}, u32[]{:S(2)}) collective-permute-start(f32[400,128]{1,0:T(8,128)S(1)} %get-tuple-element.177), channel_id=1, source_target_pairs={{0,5},{5,0},{4,9},{9,4},{8,13},{13,8},{12,17},{17,12},{16,21},{21,... | collective-permute-start | bytes 614408 | tf_op jit(solution)/shard_map/cond/branch_1_fun/ppermute | solution.py:315
  16.5 8.6 %collective-permute-start.4 = (f32[400,128]{1,0:T(8,128)S(1)}, f32[400,128]{1,0:T(8,128)}, u32[]{:S(2)}, u32[]{:S(2)}) collective-permute-start(f32[400,128]{1,0:T(8,128)S(1)} %get-tuple-element.177), channel_id=1, source_target_pairs={{0,1},{1,0},{4,5},{5,4},{8,9},{9,8},{12,13},{13,12},{16,17},{17,16... | collective-permute-start | bytes 614408 | tf_op jit(solution)/shard_map/cond/branch_1_fun/ppermute | solution.py:315
  16.5 6.0 %collective-permute-start.3 = (f32[96,128]{1,0:T(8,128)S(1)}, f32[96,128]{1,0:T(8,128)}, u32[]{:S(2)}, u32[]{:S(2)}) collective-permute-start(f32[96,128]{1,0:T(8,128)S(1)} %get-tuple-element.176), channel_id=1, source_target_pairs={{0,2},{2,0},{1,3},{3,1},{4,6},{6,4},{5,7},{7,5},{8,10},{10,8},{9,1... | collective-permute-start | bytes 147464 | tf_op jit(solution)/shard_map/cond/branch_1_fun/ppermute | solution.py:353
  26.8 20.8 %collective-permute-start.29 = (f32[480,128]{1,0:T(8,128)S(1)}, f32[480,128]{1,0:T(8,128)S(1)}, u32[]{:S(2)}, u32[]{:S(2)}) collective-permute-start(f32[480,128]{1,0:T(8,128)S(1)} %get-tuple-element.330), channel_id=1, source_target_pairs={{0,4},{4,0},{8,12},{12,8},{16,20},{20,16},{24,28},{28,24},{32,36},... | collective-permute-start | bytes 737288 | tf_op jit(solution)/shard_map/ppermute | solution.py:319
  28.7 18.9 %collective-permute-start.30 = (f32[480,128]{1,0:T(8,128)S(1)}, f32[480,128]{1,0:T(8,128)S(1)}, u32[]{:S(2)}, u32[]{:S(2)}) collective-permute-start(f32[480,128]{1,0:T(8,128)S(1)} %get-tuple-element.331), channel_id=1, source_target_pairs={{0,124},{4,8},{8,4},{12,16},{16,12},{20,24},{24,20},{28,32},{32,28... | collective-permute-start | bytes 737288 | tf_op jit(solution)/shard_map/ppermute | solution.py:324
  35.1 12.2 %collective-permute-start.11 = (f32[400,128]{1,0:T(8,128)S(1)}, f32[400,128]{1,0:T(8,128)}, u32[]{:S(2)}, u32[]{:S(2)}) collective-permute-start(f32[400,128]{1,0:T(8,128)S(1)} %get-tuple-element.202), channel_id=1, source_target_pairs={{0,1},{1,0},{4,5},{5,4},{8,9},{9,8},{12,13},{13,12},{16,17},{17,16... | collective-permute-start | bytes 614408 | tf_op jit(solution)/shard_map/cond/branch_0_fun/ppermute | solution.py:315
  37.3 10.1 %collective-permute-start.10 = (f32[400,128]{1,0:T(8,128)S(1)}, f32[400,128]{1,0:T(8,128)}, u32[]{:S(2)}, u32[]{:S(2)}) collective-permute-start(f32[400,128]{1,0:T(8,128)S(1)} %get-tuple-element.202), channel_id=1, source_target_pairs={{0,125},{125,0},{4,1},{1,4},{8,5},{5,8},{12,9},{9,12},{16,13},{13,... | collective-permute-start | bytes 614408 | tf_op jit(solution)/shard_map/cond/branch_0_fun/ppermute | solution.py:315
  37.3 4.9 %copy-start.1 = (f32[128,128]{1,0:T(8,128)S(1)}, f32[128,128]{1,0:T(8,128)}, u32[]{:S(2)}) copy-start(f32[128,128]{1,0:T(8,128)} %get-tuple-element.196.band_ref) | copy-start | bytes 196612 | tf_op jit(solution)/shard_map/cond
  41.1 6.2 %collective-permute-start.9 = (f32[96,128]{1,0:T(8,128)S(1)}, f32[96,128]{1,0:T(8,128)}, u32[]{:S(2)}, u32[]{:S(2)}) collective-permute-start(f32[96,128]{1,0:T(8,128)S(1)} %get-tuple-element.201), channel_id=1, source_target_pairs={{0,2},{2,0},{1,3},{3,1},{4,6},{6,4},{5,7},{7,5},{8,10},{10,8},{9,1... | collective-permute-start | bytes 147464 | tf_op jit(solution)/shard_map/cond/branch_0_fun/ppermute | solution.py:353
  49.4 22.8 %collective-permute-start.31 = (f32[480,128]{1,0:T(8,128)S(1)}, f32[480,128]{1,0:T(8,128)S(1)}, u32[]{:S(2)}, u32[]{:S(2)}) collective-permute-start(f32[480,128]{1,0:T(8,128)S(1)} %get-tuple-element.340), channel_id=1, source_target_pairs={{0,4},{4,0},{8,12},{12,8},{16,20},{20,16},{24,28},{28,24},{32,36},... | collective-permute-start | bytes 737288 | tf_op jit(solution)/shard_map/ppermute | solution.py:319
  49.5 22.7 %collective-permute-start.32 = (f32[480,128]{1,0:T(8,128)S(1)}, f32[480,128]{1,0:T(8,128)S(1)}, u32[]{:S(2)}, u32[]{:S(2)}) collective-permute-start(f32[480,128]{1,0:T(8,128)S(1)} %get-tuple-element.341), channel_id=1, source_target_pairs={{0,124},{4,8},{8,4},{12,16},{16,12},{20,24},{24,20},{28,32},{32,28... | collective-permute-start | bytes 737288 | tf_op jit(solution)/shard_map/ppermute | solution.py:324
  58.0 11.2 %collective-permute-start.26 = (f32[400,128]{1,0:T(8,128)S(1)}, f32[400,128]{1,0:T(8,128)}, u32[]{:S(2)}, u32[]{:S(2)}) collective-permute-start(f32[400,128]{1,0:T(8,128)S(1)} %get-tuple-element.278), channel_id=1, source_target_pairs={{0,69},{69,0},{4,73},{73,4},{8,77},{77,8},{12,81},{81,12},{16,85},... | collective-permute-start | bytes 614408 | tf_op jit(solution)/shard_map/cond/branch_2_fun/ppermute | solution.py:315
  59.0 13.1 %collective-permute-start.25 = (f32[400,128]{1,0:T(8,128)S(1)}, f32[400,128]{1,0:T(8,128)}, u32[]{:S(2)}, u32[]{:S(2)}) collective-permute-start(f32[400,128]{1,0:T(8,128)S(1)} %get-tuple-element.278), channel_id=1, source_target_pairs={{0,65},{65,0},{4,69},{69,4},{8,73},{73,8},{12,77},{77,12},{16,81},... | collective-permute-start | bytes 614408 | tf_op jit(solution)/shard_map/cond/branch_2_fun/ppermute | solution.py:315
  59.0 4.4 %copy-start.6 = (f32[128,128]{1,0:T(8,128)S(1)}, f32[128,128]{1,0:T(8,128)}, u32[]{:S(2)}) copy-start(f32[128,128]{1,0:T(8,128)} %get-tuple-element.275.band_ref) | copy-start | bytes 196612 | tf_op jit(solution)/shard_map/cond
  62.8 5.4 %collective-permute-start.24 = (f32[96,128]{1,0:T(8,128)S(1)}, f32[96,128]{1,0:T(8,128)}, u32[]{:S(2)}, u32[]{:S(2)}) collective-permute-start(f32[96,128]{1,0:T(8,128)S(1)} %get-tuple-element.277), channel_id=1, source_target_pairs={{0,2},{2,0},{1,3},{3,1},{4,6},{6,4},{5,7},{7,5},{8,10},{10,8},{9,1... | collective-permute-start | bytes 147464 | tf_op jit(solution)/shard_map/cond/branch_2_fun/ppermute | solution.py:353

commit v6 on v5

--- a/solution.py
+++ b/solution.py
@@ -398,10 +398,13 @@
     for section, kind in enumerate((kind0, kind1, kind2)):
         place = lax.div(offsets_ref[section], C)
         kind[0] = jnp.where(place == 0, 1, jnp.where(place == C, 2, 0))
-    for copy in copies:
-        copy.wait()
+    copies[0].wait()
+    copies[1].wait()
     pack_rims(q_ref, east_ref, odd_ref)
+    copies[2].wait()
     pack_rad(q_ref, rad_ref)
+    copies[3].wait()
+    copies[4].wait()
     pack_faces(q_ref, face_ref)
 
 

time: 76.9 us -> 77.8 us (1.012)
  waiting for transfers between devices: 6.47 us -> 11.1 us
  starting transfers between devices: 33.1 us -> 28.9 us
    ppermute x3, starting transfers between devices: 19.4 us -> 15.3 us  [send_odd(): lax.ppermute(odd, 'circ', [(i, (i + (1 if i % 2 else -1)) % count) for i...]
    ppermute x3, waiting for transfers between devices: 0.01 us -> 2.45 us  [send_rad(): return lax.ppermute(rad, 'rad', [(0, 1), (1, 0)])]
    ppermute x6, waiting for transfers between devices: 6.45 us -> 8.66 us  [swap_faces(): return lax.ppermute(face, ('circ', 'half'), pairs)]
  transfers between devices with their start and end apart: 15 -> 15, of which waited for: 3 -> 4; matrix products, arithmetic and copies ran while one was open for 0% -> 0% of each run, Pallas kernels for 30% -> 30%
where the time goes in v6:
time: 77.8 us; the launch traced here: 77.1 us
  Pallas kernels  34.2 us (44%)
  starting transfers between devices  28.9 us (37%)
  waiting for transfers between devices  11.1 us (14%)
  between operations  2.66 us (3%)
    pallas_call x3, Pallas kernels, local_terms(): pl.pallas_call(functools.partial(local_kernel, section), out_shape=[FIELD...  15.5 us
    ppermute x3, starting transfers between devices, send_odd(): lax.ppermute(odd, 'circ', [(i, (i + (1 if i % 2 else -1)) % count) for i...  15.3 us
    pallas_call x3, Pallas kernels, finish(): pl.pallas_call(functools.partial(finish_kernel, section, last), out_shape...  12 us
    ppermute x6, waiting for transfers between devices, swap_faces(): return lax.ppermute(face, ('circ', 'half'), pairs)  8.66 us
    ppermute x6, starting transfers between devices, swap_faces(): return lax.ppermute(face, ('circ', 'half'), pairs)  5.88 us
    ppermute x3, starting transfers between devices, send_east(): lax.ppermute(east, 'circ', [(i, i ^ 1) for i in range(lax.axis_size('circ...  5.82 us
    pallas_call x2, Pallas kernels, lead(): pl.pallas_call(functools.partial(lead_kernel, section), out_shape=[RIM, R...  3.41 us
    pallas_call x1, Pallas kernels, body(): pl.pallas_call(enter_kernel, out_shape=[RIM, RIM, RAD, FACE] + [flag] * S...  3.24 us
  transfers between devices with their start and end apart: 15, of which 4 were waited for; matrix products, arithmetic and copies ran while one was open for 0% of the time, Pallas kernels for 30%

profile of v6, /device:TPU:1, one launch (start us, length us, event | category | flops | bytes accessed | tf_op | source)
XLA Modules:
  0.0 77.1 jit_solution(13665478841323391126)
XLA Ops:
  0.6 3.2 %enter.1 = (f32[480,128]{1,0:T(8,128)S(1)}, f32[480,128]{1,0:T(8,128)S(1)}, f32[96,128]{1,0:T(8,128)S(1)}, f32[400,128]{1,0:T(8,128)S(1)}, s32[1]{0:T(128)}, /*index=5*/s32[1]{0:T(128)}, s32[1]{0:T(128)}) custom-call(s32[3]{0:T(128)} %offsets_ref.7, f32[3840,128]{1,0:T(8,128)} %bitcast.6), custom_call_target="tpu_custom_call" | custom-call | tf_op jit(solution)/shard_map/enter/pallas_call | solution.py:414
  3.9 3.8 %collective-permute-start.27 = (f32[480,128]{1,0:T(8,128)S(1)}, f32[480,128]{1,0:T(8,128)S(1)}, u32[]{:S(2)}, u32[]{:S(2)}) collective-permute-start(f32[480,128]{1,0:T(8,128)S(1)} %get-tuple-element.320), channel_id=1, source_target_pairs={{0,4},{4,0},{8,12},{12,8},{16,20},{20,16},{24,28},{28,24},{32,36},... | collective-permute-start | bytes 737288 | tf_op jit(solution)/shard_map/ppermute | solution.py:319
  7.7 5.8 %collective-permute-start.28 = (f32[480,128]{1,0:T(8,128)S(1)}, f32[480,128]{1,0:T(8,128)S(1)}, u32[]{:S(2)}, u32[]{:S(2)}) collective-permute-start(f32[480,128]{1,0:T(8,128)S(1)} %get-tuple-element.321), channel_id=1, source_target_pairs={{0,124},{4,8},{8,4},{12,16},{16,12},{20,24},{24,20},{28,32},{32,28... | collective-permute-start | bytes 737288 | tf_op jit(solution)/shard_map/ppermute | solution.py:324
  14.2 11.2 %conditional.3 = (f32[3840,128]{1,0:T(8,128)}, f32[960,128]{1,0:T(8,128)S(1)}, f32[400,128]{1,0:T(8,128)S(1)}, f32[96,128]{1,0:T(8,128)}, f32[400,128]{1,0:T(8,128)}, /*index=5*/f32[400,128]{1,0:T(8,128)}) conditional(s32[]{:T(128)} %bitcast.3, (s32[48]{0:T(128)S(1)}, f32[128,128]{1,0:T(8,128)}, f32[3840,128]{1,0:T(8,128)S(1)}, ...), branch_computations={%region_0.0_spmd, %region_1.0_spmd, %region_2.0_spmd} | conditional | flops 20000000 | bytes 7733416 | solution.py:427
  14.2 2.6 %collective-permute-start.5 = (f32[400,128]{1,0:T(8,128)S(1)}, f32[400,128]{1,0:T(8,128)}, u32[]{:S(2)}, u32[]{:S(2)}) collective-permute-start(f32[400,128]{1,0:T(8,128)S(1)} %get-tuple-element.177), channel_id=1, source_target_pairs={{0,5},{5,0},{4,9},{9,4},{8,13},{13,8},{12,17},{17,12},{16,21},{21,... | collective-permute-start | bytes 614408 | tf_op jit(solution)/shard_map/cond/branch_1_fun/ppermute | solution.py:315
  17.2 5.6 %local0.4 = (f32[3840,128]{1,0:T(8,128)}, f32[960,128]{1,0:T(8,128)S(1)}, f32[400,128]{1,0:T(8,128)S(1)}) custom-call(s32[48]{0:T(128)S(1)} %get-tuple-element.170.pml_ref, f32[128,128]{1,0:T(8,128)} %get-tuple-element.171.band_ref, f32[3840,128]{1,0:T(8,128)S(1)} %get-tuple-element.172.q_ref), custom_call_target="tpu_custom_call" | custom-call | flops 20000000 | bytes 5898240 | tf_op jit(solution)/shard_map/cond/branch_1_fun/local0/pallas_call | solution.py:329
  22.8 2.6 %collective-permute-done.5 = f32[400,128]{1,0:T(8,128)} collective-permute-done((f32[400,128]{1,0:T(8,128)S(1)}, f32[400,128]{1,0:T(8,128)}, u32[]{:S(2)}, u32[]{:S(2)}) %collective-permute-start.5) | collective-permute-done | bytes 204832 | tf_op jit(solution)/shard_map/cond/branch_1_fun/ppermute | solution.py:315
  25.4 1.7 %lead0.1 = (f32[480,128]{1,0:T(8,128)S(1)}, f32[480,128]{1,0:T(8,128)S(1)}, f32[400,128]{1,0:T(8,128)S(1)}) custom-call(s32[3]{0:T(128)S(1)} %copy-done.7, f32[960,128]{1,0:T(8,128)S(1)} %get-tuple-element.325.rim_ref, f32[400,128]{1,0:T(8,128)S(1)} %get-tuple-element.326.face_ref, f32[480,128]{1,0:T(8,128)S(1)} %collective-permute-done.27.east_ref, ...), custom_call_target="tpu_custom_call" | custom-call | tf_op jit(solution)/shard_map/lead0/pallas_call | solution.py:359
  27.1 1.9 %collective-permute-start.29 = (f32[480,128]{1,0:T(8,128)S(1)}, f32[480,128]{1,0:T(8,128)S(1)}, u32[]{:S(2)}, u32[]{:S(2)}) collective-permute-start(f32[480,128]{1,0:T(8,128)S(1)} %get-tuple-element.330), channel_id=1, source_target_pairs={{0,4},{4,0},{8,12},{12,8},{16,20},{20,16},{24,28},{28,24},{32,36},... | collective-permute-start | bytes 737288 | tf_op jit(solution)/shard_map/ppermute | solution.py:319
  29.0 5.8 %collective-permute-start.30 = (f32[480,128]{1,0:T(8,128)S(1)}, f32[480,128]{1,0:T(8,128)S(1)}, u32[]{:S(2)}, u32[]{:S(2)}) collective-permute-start(f32[480,128]{1,0:T(8,128)S(1)} %get-tuple-element.331), channel_id=1, source_target_pairs={{0,124},{4,8},{8,4},{12,16},{16,12},{20,24},{24,20},{28,32},{32,28... | collective-permute-start | bytes 737288 | tf_op jit(solution)/shard_map/ppermute | solution.py:324
  35.4 16.1 %conditional.4 = (f32[3840,128]{1,0:T(8,128)}, f32[3840,128]{1,0:T(8,128)S(1)}, f32[960,128]{1,0:T(8,128)S(1)}, f32[400,128]{1,0:T(8,128)S(1)}, f32[96,128]{1,0:...) conditional(s32[]{:T(128)} %bitcast.2, (s32[3]{0:T(128)S(1)}, f32[3840,128]{1,0:T(8,128)S(1)}, ...), branch_computations={%region_3.0_spmd, %region_4.0_spmd, %region_5.0_spmd} | conditional | flops 28000000 | bytes 15859916 | solution.py:431
  37.5 3.8 %finish0.5 = (f32[3840,128]{1,0:T(8,128)}, f32[3840,128]{1,0:T(8,128)S(1)}, f32[96,128]{1,0:T(8,128)S(1)}) custom-call(s32[3]{0:T(128)S(1)} %get-tuple-element.220.offsets_ref, f32[3840,128]{1,0:T(8,128)S(1)} %get-tuple-element.221.q_ref, f32[3840,128]{1,0:T(8,128)} %get-tuple-element.222.part_ref, f32[480,128]{1,0:T(8,128)S(1)} %get-tuple-element.223.east_ref, ...), custom_call_target="tpu_custom_call" | custom-call | flops 8000000 | bytes 7864320 | tf_op jit(solution)/shard_map/cond/branch_2_fun/finish0/pallas_call | solution.py:374
  41.3 1.1 %collective-permute-start.15 = (f32[96,128]{1,0:T(8,128)S(1)}, f32[96,128]{1,0:T(8,128)}, u32[]{:S(2)}, u32[]{:S(2)}) collective-permute-start(f32[96,128]{1,0:T(8,128)S(1)} %get-tuple-element.235), channel_id=1, source_target_pairs={{0,2},{2,0},{1,3},{3,1},{4,6},{6,4},{5,7},{7,5},{8,10},{10,8},{9,1... | collective-permute-start | bytes 147464 | tf_op jit(solution)/shard_map/cond/branch_2_fun/ppermute | solution.py:353
  42.3 5.2 %local1.5 = (f32[3840,128]{1,0:T(8,128)S(1)}, f32[960,128]{1,0:T(8,128)S(1)}, f32[400,128]{1,0:T(8,128)S(1)}) custom-call(s32[48]{0:T(128)S(1)} %get-tuple-element.229.pml_ref, f32[128,128]{1,0:T(8,128)S(1)} %copy-done.3, f32[3840,128]{1,0:T(8,128)} %get-tuple-element.379.q_ref, f32[3840,128]{1,0:T(8,128)S(1)} %get-tuple-element.231.refs_0_), custom_call_target="tpu_custom_call" | custom-call | flops 20000000 | bytes 5898240 | tf_op jit(solution)/shard_map/cond/branch_2_fun/local1/pallas_call | solution.py:329
  47.5 4.0 %collective-permute-done.16 = f32[400,128]{1,0:T(8,128)} collective-permute-done((f32[400,128]{1,0:T(8,128)S(1)}, f32[400,128]{1,0:T(8,128)}, u32[]{:S(2)}, u32[]{:S(2)}) %collective-permute-start.16) | collective-permute-done | bytes 204832 | tf_op jit(solution)/shard_map/cond/branch_2_fun/ppermute | solution.py:315
  51.5 1.7 %lead1.1 = (f32[480,128]{1,0:T(8,128)S(1)}, f32[480,128]{1,0:T(8,128)S(1)}, f32[400,128]{1,0:T(8,128)S(1)}) custom-call(s32[3]{0:T(128)S(1)} %copy-done.7, f32[960,128]{1,0:T(8,128)S(1)} %get-tuple-element.335.rim_ref, f32[400,128]{1,0:T(8,128)S(1)} %get-tuple-element.336.face_ref, f32[480,128]{1,0:T(8,128)S(1)} %collective-permute-done.29.east_ref, ...), custom_call_target="tpu_custom_call" | custom-call | tf_op jit(solution)/shard_map/lead1/pallas_call | solution.py:359
  53.4 3.8 %collective-permute-start.32 = (f32[480,128]{1,0:T(8,128)S(1)}, f32[480,128]{1,0:T(8,128)S(1)}, u32[]{:S(2)}, u32[]{:S(2)}) collective-permute-start(f32[480,128]{1,0:T(8,128)S(1)} %get-tuple-element.341), channel_id=1, source_target_pairs={{0,124},{4,8},{8,4},{12,16},{16,12},{20,24},{24,20},{28,32},{32,28... | collective-permute-start | bytes 737288 | tf_op jit(solution)/shard_map/ppermute | solution.py:324
  57.8 15.0 %conditional.5 = (f32[3840,128]{1,0:T(8,128)}, f32[3840,128]{1,0:T(8,128)S(1)}, f32[96,128]{1,0:T(8,128)}, f32[400,128]{1,0:T(8,128)}, f32[400,128]{1,0:T(8,128)}) conditional(s32[]{:T(128)} %bitcast.1, (s32[3]{0:T(128)S(1)}, f32[3840,128]{1,0:T(8,128)}, f32[3840,128]{1,0:T(8,128)S(1)}, f32[480,128]{1,0:T(8,128)S(1)}, ...), branch_computations={%region_6.0_spmd, %region_7.0_spmd, %region_8.0_spmd} | conditional | flops 28000000 | bytes 15859900 | solution.py:431
  57.8 1.4 %collective-permute-start.20 = (f32[400,128]{1,0:T(8,128)S(1)}, f32[400,128]{1,0:T(8,128)}, u32[]{:S(2)}, u32[]{:S(2)}) collective-permute-start(f32[400,128]{1,0:T(8,128)S(1)} %get-tuple-element.250), channel_id=1, source_target_pairs={{0,1},{1,0},{4,5},{5,4},{8,9},{9,8},{12,13},{13,12},{16,17},{17,16... | collective-permute-start | bytes 614408 | tf_op jit(solution)/shard_map/cond/branch_0_fun/ppermute | solution.py:315
  59.2 3.8 %finish1.3 = (f32[3840,128]{1,0:T(8,128)}, f32[3840,128]{1,0:T(8,128)S(1)}, f32[96,128]{1,0:T(8,128)S(1)}) custom-call(s32[3]{0:T(128)S(1)} %get-tuple-element.237.offsets_ref, f32[3840,128]{1,0:T(8,128)} %get-tuple-element.238.q_ref, f32[3840,128]{1,0:T(8,128)S(1)} %get-tuple-element.239.part_ref, f32[480,128]{1,0:T(8,128)S(1)} %get-tuple-element.240.east_ref, ...), custom_call_target="tpu_custom_call" | custom-call | flops 8000000 | bytes 7864320 | tf_op jit(solution)/shard_map/cond/branch_0_fun/finish1/pallas_call | solution.py:374
  63.5 4.8 %local2.3 = f32[3840,128]{1,0:T(8,128)S(1)} custom-call(s32[48]{0:T(128)S(1)} %get-tuple-element.246.pml_ref, f32[128,128]{1,0:T(8,128)S(1)} %copy-done.4, f32[3840,128]{1,0:T(8,128)} %get-tuple-element.386.q_ref, f32[3840,128]{1,0:T(8,128)S(1)} %get-tuple-element.248.refs_0_), custom_call_target="tpu_custom_call" | custom-call | flops 20000000 | bytes 5898240 | tf_op jit(solution)/shard_map/cond/branch_0_fun/local2/pallas_call | solution.py:329
  68.3 2.4 %collective-permute-done.18 = f32[96,128]{1,0:T(8,128)} collective-permute-done((f32[96,128]{1,0:T(8,128)S(1)}, f32[96,128]{1,0:T(8,128)}, u32[]{:S(2)}, u32[]{:S(2)}) %collective-permute-start.18) | collective-permute-done | bytes 49184 | tf_op jit(solution)/shard_map/cond/branch_0_fun/ppermute | solution.py:353
  70.7 2.1 %collective-permute-done.19 = f32[400,128]{1,0:T(8,128)} collective-permute-done((f32[400,128]{1,0:T(8,128)S(1)}, f32[400,128]{1,0:T(8,128)}, u32[]{:S(2)}, u32[]{:S(2)}) %collective-permute-start.19) | collective-permute-done | bytes 204832 | tf_op jit(solution)/shard_map/cond/branch_0_fun/ppermute | solution.py:315
  72.8 4.3 %finish2.1 = (f32[3840,128]{1,0:T(8,128)}, f32[3840,128]{1,0:T(8,128)}) custom-call(s32[3]{0:T(128)S(1)} %copy-done.7, f32[3840,128]{1,0:T(8,128)} %get-tuple-element.338.q_ref, f32[3840,128]{1,0:T(8,128)S(1)} %get-tuple-element.339.part_ref, f32[480,128]{1,0:T(8,128)S(1)} %collective-permute-done.31.east_ref, ...), custom_call_target="tpu_custom_call" | custom-call | flops 8000000 | bytes 7864320 | tf_op jit(solution)/shard_map/finish2/pallas_call | solution.py:374
  (28 shorter events, 2.8 us)
Async XLA Ops:
  0.6 13.5 %copy-start = (f32[5,48,16,128]{3,2,1,0:T(8,128)S(1)}, f32[5,48,16,128]{3,2,1,0:T(8,128)}, u32[]{:S(2)}) copy-start(f32[5,48,16,128]{3,2,1,0:T(8,128)} %param.21) | copy-start | bytes 5898244
  0.6 13.5 %copy-start.8 = (s32[48]{0:T(128)S(1)}, s32[48]{0:T(128)}, u32[]{:S(2)}) copy-start(s32[48]{0:T(128)} %param.23) | copy-start | bytes 580
  3.9 21.5 %collective-permute-start.27 = (f32[480,128]{1,0:T(8,128)S(1)}, f32[480,128]{1,0:T(8,128)S(1)}, u32[]{:S(2)}, u32[]{:S(2)}) collective-permute-start(f32[480,128]{1,0:T(8,128)S(1)} %get-tuple-element.320), channel_id=1, source_target_pairs={{0,4},{4,0},{8,12},{12,8},{16,20},{20,16},{24,28},{28,24},{32,36},... | collective-permute-start | bytes 737288 | tf_op jit(solution)/shard_map/ppermute | solution.py:319
  7.7 17.7 %collective-permute-start.28 = (f32[480,128]{1,0:T(8,128)S(1)}, f32[480,128]{1,0:T(8,128)S(1)}, u32[]{:S(2)}, u32[]{:S(2)}) collective-permute-start(f32[480,128]{1,0:T(8,128)S(1)} %get-tuple-element.321), channel_id=1, source_target_pairs={{0,124},{4,8},{8,4},{12,16},{16,12},{20,24},{24,20},{28,32},{32,28... | collective-permute-start | bytes 737288 | tf_op jit(solution)/shard_map/ppermute | solution.py:324
  14.2 11.2 %copy-start.7 = (s32[3]{0:T(128)S(1)}, s32[3]{0:T(128)}, u32[]{:S(2)}) copy-start(s32[3]{0:T(128)} %offsets_ref.7) | copy-start | bytes 40
  14.2 11.2 %collective-permute-start.5 = (f32[400,128]{1,0:T(8,128)S(1)}, f32[400,128]{1,0:T(8,128)}, u32[]{:S(2)}, u32[]{:S(2)}) collective-permute-start(f32[400,128]{1,0:T(8,128)S(1)} %get-tuple-element.177), channel_id=1, source_target_pairs={{0,5},{5,0},{4,9},{9,4},{8,13},{13,8},{12,17},{17,12},{16,21},{21,... | collective-permute-start | bytes 614408 | tf_op jit(solution)/shard_map/cond/branch_1_fun/ppermute | solution.py:315
  16.8 8.6 %collective-permute-start.4 = (f32[400,128]{1,0:T(8,128)S(1)}, f32[400,128]{1,0:T(8,128)}, u32[]{:S(2)}, u32[]{:S(2)}) collective-permute-start(f32[400,128]{1,0:T(8,128)S(1)} %get-tuple-element.177), channel_id=1, source_target_pairs={{0,1},{1,0},{4,5},{5,4},{8,9},{9,8},{12,13},{13,12},{16,17},{17,16... | collective-permute-start | bytes 614408 | tf_op jit(solution)/shard_map/cond/branch_1_fun/ppermute | solution.py:315
  16.8 6.0 %collective-permute-start.3 = (f32[96,128]{1,0:T(8,128)S(1)}, f32[96,128]{1,0:T(8,128)}, u32[]{:S(2)}, u32[]{:S(2)}) collective-permute-start(f32[96,128]{1,0:T(8,128)S(1)} %get-tuple-element.176), channel_id=1, source_target_pairs={{0,2},{2,0},{1,3},{3,1},{4,6},{6,4},{5,7},{7,5},{8,10},{10,8},{9,1... | collective-permute-start | bytes 147464 | tf_op jit(solution)/shard_map/cond/branch_1_fun/ppermute | solution.py:353
  27.1 24.4 %collective-permute-start.29 = (f32[480,128]{1,0:T(8,128)S(1)}, f32[480,128]{1,0:T(8,128)S(1)}, u32[]{:S(2)}, u32[]{:S(2)}) collective-permute-start(f32[480,128]{1,0:T(8,128)S(1)} %get-tuple-element.330), channel_id=1, source_target_pairs={{0,4},{4,0},{8,12},{12,8},{16,20},{20,16},{24,28},{28,24},{32,36},... | collective-permute-start | bytes 737288 | tf_op jit(solution)/shard_map/ppermute | solution.py:319
  29.0 22.5 %collective-permute-start.30 = (f32[480,128]{1,0:T(8,128)S(1)}, f32[480,128]{1,0:T(8,128)S(1)}, u32[]{:S(2)}, u32[]{:S(2)}) collective-permute-start(f32[480,128]{1,0:T(8,128)S(1)} %get-tuple-element.331), channel_id=1, source_target_pairs={{0,124},{4,8},{8,4},{12,16},{16,12},{20,24},{24,20},{28,32},{32,28... | collective-permute-start | bytes 737288 | tf_op jit(solution)/shard_map/ppermute | solution.py:324
  35.6 11.9 %collective-permute-start.17 = (f32[400,128]{1,0:T(8,128)S(1)}, f32[400,128]{1,0:T(8,128)}, u32[]{:S(2)}, u32[]{:S(2)}) collective-permute-start(f32[400,128]{1,0:T(8,128)S(1)} %get-tuple-element.236), channel_id=1, source_target_pairs={{0,69},{69,0},{4,73},{73,4},{8,77},{77,8},{12,81},{81,12},{16,85},... | collective-permute-start | bytes 614408 | tf_op jit(solution)/shard_map/cond/branch_2_fun/ppermute | solution.py:315
  36.7 14.9 %collective-permute-start.16 = (f32[400,128]{1,0:T(8,128)S(1)}, f32[400,128]{1,0:T(8,128)}, u32[]{:S(2)}, u32[]{:S(2)}) collective-permute-start(f32[400,128]{1,0:T(8,128)S(1)} %get-tuple-element.236), channel_id=1, source_target_pairs={{0,65},{65,0},{4,69},{69,4},{8,73},{73,8},{12,77},{77,12},{16,81},... | collective-permute-start | bytes 614408 | tf_op jit(solution)/shard_map/cond/branch_2_fun/ppermute | solution.py:315
  37.5 4.9 %copy-start.3 = (f32[128,128]{1,0:T(8,128)S(1)}, f32[128,128]{1,0:T(8,128)}, u32[]{:S(2)}) copy-start(f32[128,128]{1,0:T(8,128)} %get-tuple-element.230.band_ref) | copy-start | bytes 196612 | tf_op jit(solution)/shard_map/cond
  41.3 6.2 %collective-permute-start.15 = (f32[96,128]{1,0:T(8,128)S(1)}, f32[96,128]{1,0:T(8,128)}, u32[]{:S(2)}, u32[]{:S(2)}) collective-permute-start(f32[96,128]{1,0:T(8,128)S(1)} %get-tuple-element.235), channel_id=1, source_target_pairs={{0,2},{2,0},{1,3},{3,1},{4,6},{6,4},{5,7},{7,5},{8,10},{10,8},{9,1... | collective-permute-start | bytes 147464 | tf_op jit(solution)/shard_map/cond/branch_2_fun/ppermute | solution.py:353
  53.2 19.6 %collective-permute-start.31 = (f32[480,128]{1,0:T(8,128)S(1)}, f32[480,128]{1,0:T(8,128)S(1)}, u32[]{:S(2)}, u32[]{:S(2)}) collective-permute-start(f32[480,128]{1,0:T(8,128)S(1)} %get-tuple-element.340), channel_id=1, source_target_pairs={{0,4},{4,0},{8,12},{12,8},{16,20},{20,16},{24,28},{28,24},{32,36},... | collective-permute-start | bytes 737288 | tf_op jit(solution)/shard_map/ppermute | solution.py:319
  53.4 19.4 %collective-permute-start.32 = (f32[480,128]{1,0:T(8,128)S(1)}, f32[480,128]{1,0:T(8,128)S(1)}, u32[]{:S(2)}, u32[]{:S(2)}) collective-permute-start(f32[480,128]{1,0:T(8,128)S(1)} %get-tuple-element.341), channel_id=1, source_target_pairs={{0,124},{4,8},{8,4},{12,16},{16,12},{20,24},{24,20},{28,32},{32,28... | collective-permute-start | bytes 737288 | tf_op jit(solution)/shard_map/ppermute | solution.py:324
  57.8 12.9 %collective-permute-start.20 = (f32[400,128]{1,0:T(8,128)S(1)}, f32[400,128]{1,0:T(8,128)}, u32[]{:S(2)}, u32[]{:S(2)}) collective-permute-start(f32[400,128]{1,0:T(8,128)S(1)} %get-tuple-element.250), channel_id=1, source_target_pairs={{0,1},{1,0},{4,5},{5,4},{8,9},{9,8},{12,13},{13,12},{16,17},{17,16... | collective-permute-start | bytes 614408 | tf_op jit(solution)/shard_map/cond/branch_0_fun/ppermute | solution.py:315
  59.2 13.6 %collective-permute-start.19 = (f32[400,128]{1,0:T(8,128)S(1)}, f32[400,128]{1,0:T(8,128)}, u32[]{:S(2)}, u32[]{:S(2)}) collective-permute-start(f32[400,128]{1,0:T(8,128)S(1)} %get-tuple-element.250), channel_id=1, source_target_pairs={{0,125},{125,0},{4,1},{1,4},{8,5},{5,8},{12,9},{9,12},{16,13},{13,... | collective-permute-start | bytes 614408 | tf_op jit(solution)/shard_map/cond/branch_0_fun/ppermute | solution.py:315
  59.2 4.2 %copy-start.4 = (f32[128,128]{1,0:T(8,128)S(1)}, f32[128,128]{1,0:T(8,128)}, u32[]{:S(2)}) copy-start(f32[128,128]{1,0:T(8,128)} %get-tuple-element.247.band_ref) | copy-start | bytes 196612 | tf_op jit(solution)/shard_map/cond
  63.1 7.6 %collective-permute-start.18 = (f32[96,128]{1,0:T(8,128)S(1)}, f32[96,128]{1,0:T(8,128)}, u32[]{:S(2)}, u32[]{:S(2)}) collective-permute-start(f32[96,128]{1,0:T(8,128)S(1)} %get-tuple-element.249), channel_id=1, source_target_pairs={{0,2},{2,0},{1,3},{3,1},{4,6},{6,4},{5,7},{7,5},{8,10},{10,8},{9,1... | collective-permute-start | bytes 147464 | tf_op jit(solution)/shard_map/cond/branch_0_fun/ppermute | solution.py:353
